TPU v7x, 256 devices: a whole 4x4x8 slice. The times are simulated.
256 devices in a mesh: dp: 16 (over z, x_hi), fsdp: 16 (over y, x_lo, core).
Axes of the slice: x: 4 (x_hi: 2, x_lo: 2; x = x_hi * 2 + x_lo), y: 4, z: 8, core: 2. Of those that a mesh axis runs over, the one named last changes fastest.
Arguments:
- inputs: bfloat16 [1024, 14, 14, 256], P(('dp', 'fsdp')), may hold values from -6 to 6
- out_grads: bfloat16 [1024, 14, 14, 256], P(('dp', 'fsdp')), may hold values from -6 to 6
- patch_basis: bfloat16 [1152, 2304], P(None, 'fsdp'), may hold values from -0.1875 to 0.1875
- output_basis: bfloat16 [256, 256], P(None, 'fsdp'), may hold values from -0.375 to 0.375
Outputs:
- second_moment: float32 [256, 2304], P('dp', 'fsdp')
- scaled_sum: float32 [256, 2304], P('dp', 'fsdp')
All inputs are finite; a program needn't handle non-finite values.
Results may differ from a plain program's by a relative error of at most 0.0041.
Values may be sent and summed in bfloat16 or wider, within the bound.
No kernel may reach another device: no remote copies, remote signals or barrier semaphores. Data moves between devices by JAX's collectives and lax.ppermute only.
A program may use at most 64 MiB of HBM per device.

v0:
```python
import math

import jax
import jax.numpy as jnp
from jax import lax
from jax.sharding import PartitionSpec as P


def patch_rows(feature_maps):
    count = feature_maps.shape[0]
    grid_side = feature_maps.shape[1]
    padded = jnp.pad(feature_maps, ((0, 0), (1, 1), (1, 1), (0, 0)))
    shifted = [
        padded[:, row_tap : row_tap + grid_side, col_tap : col_tap + grid_side, :]
        for row_tap in range(3)
        for col_tap in range(3)
    ]
    return jnp.concatenate(shifted, axis=3).reshape(count, grid_side * grid_side, -1)


def on_device(inputs, out_grads, patch_basis, output_basis):
    examples_dev = inputs.shape[0]
    grid_side = inputs.shape[1]
    block_width = patch_basis.shape[0]
    out_width = output_basis.shape[0]
    total_examples = examples_dev * lax.axis_size("dp") * lax.axis_size("fsdp")
    inv_side = 1.0 / grid_side
    full_patch, full_out = (
        lax.all_gather(patch_basis, "fsdp", axis=1, tiled=True),
        lax.all_gather(output_basis, "fsdp", axis=1, tiled=True),
    )
    columns = full_patch.shape[1]

    def accumulate(position, running):
        example_input = lax.dynamic_index_in_dim(inputs, position, 0, keepdims=True)
        example_grad = lax.dynamic_index_in_dim(out_grads, position, 0, keepdims=False)
        patches = patch_rows(example_input)[0]
        low_part = jnp.dot(
            patches[:, :block_width],
            full_patch[:, :block_width],
            preferred_element_type=jnp.float32,
        )
        high_part = jnp.dot(
            patches[:, block_width:],
            full_patch[:, block_width:],
            preferred_element_type=jnp.float32,
        )
        rotated = jnp.concatenate([low_part, high_part], axis=1).astype(jnp.bfloat16)
        grad_rot = jnp.dot(
            example_grad.reshape(-1, out_width), full_out, preferred_element_type=jnp.float32
        ).astype(jnp.bfloat16)
        projected = jnp.dot(grad_rot.T, rotated, preferred_element_type=jnp.float32) * inv_side
        return (running[0] + projected * projected, running[1] + projected)

    empty_sums = jnp.zeros((out_width, columns), jnp.float32)
    squares, linear = lax.fori_loop(0, examples_dev, accumulate, (empty_sums, empty_sums))
    squares, linear = (
        lax.psum_scatter(squares, "fsdp", scatter_dimension=1, tiled=True),
        lax.psum_scatter(linear, "fsdp", scatter_dimension=1, tiled=True),
    )
    squares, linear = (
        lax.psum_scatter(squares, "dp", scatter_dimension=0, tiled=True),
        lax.psum_scatter(linear, "dp", scatter_dimension=0, tiled=True),
    )
    return (squares / total_examples, linear * (1.0 / math.sqrt(total_examples)))


def solution(mesh):
    in_specs = (
        P(("dp", "fsdp"), None, None, None),
        P(("dp", "fsdp"), None, None, None),
        P(None, "fsdp"),
        P(None, "fsdp"),
    )
    out_specs = (P("dp", "fsdp"), P("dp", "fsdp"))
    return jax.shard_map(
        on_device, mesh=mesh, in_specs=in_specs, out_specs=out_specs, check_vma=False
    )
```

profile of v0, /device:TPU:2, one launch (start us, length us, event | category | flops | bytes accessed | tf_op | source)
XLA Modules:
  0.0 665.7 jit_solution(16799020347901168019)
XLA Ops:
  7.2 0.0 all-gather.2.cloned.1.call-start
  7.2 0.7 all-gather.2.cloned.1.call-update
  7.9 0.0 reduce-scatter.15.cloned.1.call-start
  8.0 18.8 %all_gather.6 = bf16[256,256]{0,1:T(8,128)(2,1)S(1)} all-gather(bf16[256,16]{0,1:T(8,128)(2,1)} %param.9), channel_id=1, replica_groups=mesh['dp'=16,'fsdp'=16] {'fsdp'}, dimensions={1}, use_global_device_ids=true | all-gather | bytes 139264 | tf_op jit(solution)/shard_map/all_gather | solution.py:30
  26.8 0.8 copy.13
  27.6 1.8 copy.14
  29.4 1.9 copy.12
  31.3 23.1 %all-gather.2.cloned.1.call-done = bf16[1152,2304]{0,1:T(8,128)(2,1)} async-done(((bf16[1152,144]{0,1:T(8,128)(2,1)}), bf16[1152,2304]{0,1:T(8,128)(2,1)}) %all-gather.2.cloned.1.call-update) | async-done | bytes 5308432 | tf_op jit(solution)/shard_map/all_gather | solution.py:29
  54.4 8.6 %copy.15 = bf16[1152,2304]{1,0:T(8,128)(2,1)} copy(bf16[1152,2304]{0,1:T(8,128)(2,1)} %all-gather.2.cloned.1.call-done) | data formatting | bytes 10616832
  63.0 52.0 %while.18 = (s32[]{:T(128)}, f32[256,2304]{1,0:T(8,128)}, f32[256,2304]{1,0:T(8,128)S(1)}, bf16[4,14,14,256]{3,2,1,0:T(8,128)(2,1)}, bf16[256,256]{1,0:T(8,128)(...) while((s32[]{:T(128)}, f32[256,2304]{1,0:T(8,128)}, ...), condition=%wide.region_1.2_spmd.clone, body=%wide.region_0.1_spmd.clone.sunk | while | flops 1303197696 | bytes 26702024 | solution.py:56
  63.0 1.0 constant_dynamic-slice_fusion.3
  63.9 0.7 reshape.34
  64.9 1.2 reshape.33
  66.1 2.8 fusion.33
  68.9 0.0 copy-done.1
  69.0 0.0 copy-start.2
  69.0 0.0 copy-start.3
  69.0 2.6 fusion.32
  71.6 0.0 copy-done.2
  71.6 0.0 copy-done.3
  71.6 3.1 select_add_fusion.3
  74.7 1.0 constant_dynamic-slice_fusion.3
  75.7 0.7 reshape.34
  76.7 1.2 reshape.33
  77.9 2.8 fusion.33
  80.7 0.0 copy-done.1
  80.7 0.0 copy-start.2
  80.7 0.0 copy-start.3
  80.7 2.6 fusion.32
  83.4 0.0 copy-done.2
  83.4 0.0 copy-done.3
  83.4 4.7 select_add_fusion.3
  88.1 1.0 constant_dynamic-slice_fusion.3
  89.1 0.7 reshape.34
  90.1 1.2 reshape.33
  91.3 2.8 fusion.33
  94.1 0.0 copy-done.1
  94.1 0.0 copy-start.2
  94.1 2.6 fusion.32
  96.8 4.7 select_add_fusion.3
  101.5 1.0 constant_dynamic-slice_fusion.3
  102.5 0.7 reshape.34
  103.5 1.2 reshape.33
  104.7 2.8 fusion.33
  107.5 2.6 fusion.32
  110.2 4.7 select_add_fusion.3
  114.9 2.0 copy.18
  116.9 0.0 reduce-scatter.15.cloned.1.call-update
  116.9 0.0 reduce-scatter.13.cloned.1.call-start
  117.0 1.6 copy-done
  118.6 2.0 copy.16
  120.5 0.0 reduce-scatter.13.cloned.1.call-update
  120.6 0.0 reduce-scatter.11.cloned.1.call-start
  120.6 60.6 %reduce-scatter.15.cloned.1.call-done = f32[144,256]{1,0:T(8,128)} async-done(((f32[2304,256]{1,0:T(8,128)}), f32[144,256]{1,0:T(8,128)}) %reduce-scatter.15.cloned.1.call-update) | async-done | bytes 147472
  181.2 1.7 copy.19
  182.9 0.0 reduce-scatter.11.cloned.1.call-update
  182.9 0.0 reduce-scatter.9.cloned.1.call-start
  183.0 67.3 %reduce-scatter.13.cloned.1.call-done = f32[144,256]{1,0:T(8,128)} async-done(((f32[2304,256]{1,0:T(8,128)}), f32[144,256]{1,0:T(8,128)}) %reduce-scatter.13.cloned.1.call-update) | async-done | bytes 147472
  250.3 1.8 copy.17
  252.0 0.0 reduce-scatter.9.cloned.1.call-update
  252.0 203.9 %reduce-scatter.11.cloned.1.call-done = f32[16,144]{1,0:T(8,128)} async-done(((f32[256,144]{1,0:T(8,128)}), f32[16,144]{1,0:T(8,128)}) %reduce-scatter.11.cloned.1.call-update) | async-done | bytes 9232 | tf_op jit(solution)/shard_map/reduce_scatter | solution.py:63
  455.9 1.3 broadcast_multiply_fusion
  457.3 200.6 %reduce-scatter.9.cloned.1.call-done = f32[16,144]{1,0:T(8,128)} async-done(((f32[256,144]{1,0:T(8,128)}), f32[16,144]{1,0:T(8,128)}) %reduce-scatter.9.cloned.1.call-update) | async-done | bytes 9232 | tf_op jit(solution)/shard_map/reduce_scatter | solution.py:62
  657.8 1.3 broadcast_multiply_fusion.1
  (51 shorter events, 1.0 us)
Async XLA Ops:
  7.2 47.2 %all-gather.2.cloned.1.call-start = ((), (), s32[]{:S(2)}) async-start(), calls=%async_computation.4 | async-start | bytes 5640192 | tf_op jit(solution)/shard_map/all_gather | solution.py:29
  7.9 173.3 %reduce-scatter.15.cloned.1.call-start = ((), (), s32[]{:S(2)}) async-start(), calls=%async_computation.8 | async-start | bytes 2506752
  66.1 2.8 copy-start.1
  69.0 2.7 copy-start.2
  69.0 2.7 copy-start.3
  77.9 2.8 copy-start.1
  80.7 2.7 copy-start.2
  80.7 2.7 copy-start.3
  91.3 2.8 copy-start.1
  94.1 2.7 copy-start.2
  94.1 2.7 copy-start.3
  104.7 2.8 copy-start.1
  107.5 2.7 copy-start.2
  107.5 2.7 copy-start.3
  116.9 1.7 copy-start
  116.9 133.3 %reduce-scatter.13.cloned.1.call-start = ((), (), s32[]{:S(2)}) async-start(), calls=%async_computation.7 | async-start | bytes 2506752
  120.6 335.4 %reduce-scatter.11.cloned.1.call-start = ((), (), s32[]{:S(2)}) async-start(), calls=%async_computation.6 | async-start | bytes 278528 | tf_op jit(solution)/shard_map/reduce_scatter | solution.py:63
  182.9 474.9 %reduce-scatter.9.cloned.1.call-start = ((), (), s32[]{:S(2)}) async-start(), calls=%async_computation.5 | async-start | bytes 278528 | tf_op jit(solution)/shard_map/reduce_scatter | solution.py:62
Sparse Core Ops, SparseCore 0:
  9.8 44.5 all-gather.1
  117.1 64.0 reduce-scatter.14
  183.7 66.5 reduce-scatter.12
  253.9 201.9 reduce-scatter.10
  460.1 197.7 reduce-scatter.8
where the time goes:
time: 667 us; the launch traced here: 666 us
  waiting for transfers between devices  556 us (83%)
  matrix products  39.1 us (6%)
  local copies, waits for them, and re-layouts  34.5 us (5%)
  blocking collectives  18.8 us (3%)
  between operations  13.8 us (2%)
    reduce_scatter x1, waiting for transfers between devices, on_device(): lax.psum_scatter(linear, 'dp', scatter_dimension=0, tiled=True)  204 us
    reduce_scatter x1, waiting for transfers between devices, on_device(): lax.psum_scatter(squares, 'dp', scatter_dimension=0, tiled=True)  201 us
    unnamed x7, waiting for transfers between devices  129 us
    all_gather x1, waiting for transfers between devices, on_device(): lax.all_gather(patch_basis, 'fsdp', axis=1, tiled=True)  23.1 us
    unnamed x10, local copies, waits for them, and re-layouts  22 us
    all_gather x1, blocking collectives, on_device(): lax.all_gather(output_basis, 'fsdp', axis=1, tiled=True)  18.8 us
    dot_general x4, matrix products, accumulate(): jnp.dot(grad_rot.T, rotated, preferred_element_type=jnp.float32) * inv_side  17.3 us
  transfers between devices with their start and end apart: 5, of which 5 were waited for; matrix products, arithmetic and copies ran while one was open for 2% of the time, Pallas kernels for 0%

commit v1 on v0

v1 whole, which is shorter than its diff:
```python
import functools
import math

import jax
import jax.numpy as jnp
from jax import lax
from jax.experimental import pallas as pl
from jax.experimental.pallas import tpu as pltpu
from jax.sharding import Mesh, PartitionSpec as P

AXES = ("z", "xh", "y", "xl", "c")
SIZES = (8, 2, 4, 2, 2)
BF16 = jnp.bfloat16
F32 = jnp.float32
CONTRACT_LAST = (((1,), (1,)), ((), ()))


def ring(value, axis, size, step):
    return lax.ppermute(value, axis, [(i, (i + step) % size) for i in range(size)])


def swap_cores(value):
    return lax.ppermute(value, "c", [(0, 1), (1, 0)])


def swap_x(value):
    def partner(x, core):
        return (x + 1 if (x + core) % 2 == 0 else x - 1) % 4

    pairs = [(x * 2 + core, partner(x, core) * 2 + core) for x in range(4) for core in range(2)]
    return lax.ppermute(value, ("xh", "xl", "c"), pairs)


def prepare(inputs, out_grads):
    both = jnp.stack([inputs, out_grads])
    padded = jnp.pad(both, ((0, 0), (0, 0), (0, 0), (0, 2), (0, 0)))
    return padded.reshape(2, inputs.shape[0], 224, 256)


def moments_kernel(
    at_ref, own, other, far, far_other, s0, sp, sm, s2a, s2b, u_ref,
    squares_ref, linear_ref, basis, rows, patches, out_basis,
):
    y = at_ref[0]
    half = s0.shape[0] // 2

    def place(step, value):
        owner = lax.rem(y + step, 4)
        basis[owner // 2, pl.ds(pl.multiple_of((owner % 2) * 144, 16), 144), :] = value

    place(0, s0[...])
    place(1, sp[...])
    place(3, sm[...])
    place(2, jnp.concatenate([s2a[...], s2b[...]], axis=0))
    for piece in range(16):
        at = pl.multiple_of(at_ref[1 + piece], 16)
        out_basis[pl.ds(at, 16), :] = u_ref[16 * piece : 16 * piece + 16, :]
    rows[...] = jnp.zeros_like(rows)
    squares_ref[...] = jnp.zeros_like(squares_ref)
    linear_ref[...] = jnp.zeros_like(linear_ref)

    for group in (own, other, far, far_other):

        @pl.loop(0, 4)
        def _(n, group=group):
            feature = group[0, n].astype(F32)
            rows[0, 16:240, :] = pltpu.roll(feature, 1, 0).astype(BF16)
            rows[1, 16:240, :] = group[0, n]
            rows[2, 16:240, :] = pltpu.roll(feature, 223, 0).astype(BF16)
            for tap in range(9):
                ky, kx = tap // 3, tap % 3
                shifted = rows[kx, 16 * ky : 16 * ky + 224, :]
                if tap < 4:
                    patches[0, :, 256 * tap : 256 * tap + 256] = shifted
                elif tap == 4:
                    patches[0, :, 1024:1152] = shifted[:, :128]
                    patches[1, :, 0:128] = shifted[:, 128:]
                else:
                    patches[1, :, 256 * tap - 1152 : 256 * tap - 896] = shifted
            grad_rot = lax.dot_general(
                group[1, n], out_basis[...], CONTRACT_LAST, preferred_element_type=F32
            ).astype(BF16)
            for block in range(2):
                rotated = lax.dot_general(
                    basis[block], patches[block], CONTRACT_LAST, preferred_element_type=F32
                ).astype(BF16)
                projected = jnp.dot(rotated, grad_rot, preferred_element_type=F32)
                squares_ref[block] += projected * projected
                linear_ref[block] += projected


def moments(at, *operands):
    shape = jax.ShapeDtypeStruct((2, 288, 256), F32)
    vmem = pl.BlockSpec(memory_space=pltpu.VMEM)
    return pl.pallas_call(
        moments_kernel,
        out_shape=(shape, shape),
        in_specs=[pl.BlockSpec(memory_space=pltpu.SMEM)] + [vmem] * len(operands),
        out_specs=(vmem, vmem),
        scratch_shapes=[
            pltpu.VMEM((2, 288, 1152), BF16),
            pltpu.VMEM((3, 256, 256), BF16),
            pltpu.VMEM((2, 224, 1152), BF16),
            pltpu.VMEM((256, 256), BF16),
        ],
        compiler_params=pltpu.CompilerParams(vmem_limit_bytes=40 * 2**20),
        name="moments",
    )(at, *operands)


def on_device(inputs, out_grads, patch_basis, output_basis):
    examples = inputs.shape[0] * math.prod(SIZES)
    y, xl, core = lax.axis_index("y"), lax.axis_index("xl"), lax.axis_index("c")

    own = prepare(inputs, out_grads)
    other = swap_cores(own)
    u0 = output_basis.T
    u1 = jnp.concatenate([u0, swap_cores(u0)])
    far = swap_x(own)
    s0 = patch_basis.T
    sp, sm = ring(s0, "y", 4, 3), ring(s0, "y", 4, 1)
    u2 = jnp.concatenate([u1, ring(u1, "xl", 2, 1)])
    up, um = ring(u2, "y", 4, 3), ring(u2, "y", 4, 1)
    s2a, s2b = ring(sp[:72], "y", 4, 3), ring(sm[72:], "y", 4, 1)
    ut = ring(up, "y", 4, 3)
    far_other = swap_cores(far)
    u = jnp.concatenate([u2, up, ut, um])
    offsets = [
        (((y + dy) % 4 * 2 + (xl + dx) % 2) * 2 + (core + dc) % 2) * 16
        for dy in range(4)
        for dx in range(2)
        for dc in range(2)
    ]
    at = jnp.stack([y] + offsets).astype(jnp.int32)
    squares, linear = moments(at, own, other, far, far_other, s0, sp, sm, s2a, s2b, u)

    sums = jnp.stack([squares, linear]).astype(BF16).reshape(2, 4, 144, 256)
    sums = lax.all_to_all(sums.transpose(1, 0, 2, 3), "y", 0, 0, tiled=True)
    sums = jnp.sum(sums.astype(F32), axis=0).reshape(288, 256).T
    sums = lax.all_to_all(sums, ("z", "xh"), 0, 0, tiled=True)
    sums = jnp.sum(sums.reshape(16, 16, 288), axis=0)
    side = inputs.shape[1]
    return (
        sums[:, :144] * (1.0 / (side * side * examples)),
        sums[:, 144:] * (1.0 / (side * math.sqrt(examples))),
    )


def solution(mesh):
    fine = Mesh(mesh.devices.reshape(SIZES), AXES)
    every, columns = ("z", "xh", "y", "xl", "c"), ("y", "xl", "c")
    return jax.shard_map(
        on_device,
        mesh=fine,
        in_specs=(P(every), P(every), P(None, columns), P(None, columns)),
        out_specs=(P(("z", "xh"), columns), P(("z", "xh"), columns)),
        check_vma=False,
    )
```

time: 667 us -> 97 us (0.15)
  waiting for transfers between devices: 556 us -> 14.5 us
  matrix products: 39.1 us -> 0 us
  local copies, waits for them, and re-layouts: 34.5 us -> 1.94 us
  Pallas kernels: 0 us -> 20.5 us
  starting transfers between devices: 0.2 us -> 18 us
  blocking collectives: 18.8 us -> 36.5 us
  between operations: 13.8 us -> 0.76 us
    reduce_scatter x2 -> x0, waiting for transfers between devices: 404 us -> none  [the longest x1 204 us: on_device(): lax.psum_scatter(linear, 'dp', scatter_dimension=0, tiled=True)]
    unnamed x7 -> x0, waiting for transfers between devices: 129 us -> none
    dot_general x12 -> x0, matrix products: 39.1 us -> none  [the longest x4 17.3 us: accumulate(): jnp.dot(grad_rot.T, rotated, preferred_element_type=jnp.float32) * inv_side]
    all_to_all x0 -> x2, blocking collectives: none -> 36.5 us  [the longest x1 23.3 us: on_device(): sums = lax.all_to_all(sums, ('z', 'xh'), 0, 0, tiled=True)]
    all_gather x1 -> x0, waiting for transfers between devices: 23.1 us -> none  [on_device(): lax.all_gather(patch_basis, 'fsdp', axis=1, tiled=True)]
    pallas_call x0 -> x1, Pallas kernels: none -> 20.5 us  [moments(): pl.pallas_call(moments_kernel, out_shape=(shape, shape), in_specs=[pl.Blo...]
    unnamed x10 -> x6, local copies, waits for them, and re-layouts: 22 us -> 1.55 us
    all_gather x1 -> x0, blocking collectives: 18.8 us -> none  [on_device(): lax.all_gather(output_basis, 'fsdp', axis=1, tiled=True)]
  transfers between devices with their start and end apart: 5 -> 12, of which waited for: 5 -> 6; matrix products, arithmetic and copies ran while one was open for 2% -> 3% of each run, Pallas kernels for 0% -> 0%
where the time goes in v1:
time: 97 us; the launch traced here: 96.4 us
  blocking collectives  36.5 us (38%)
  Pallas kernels  20.5 us (21%)
  starting transfers between devices  18 us (19%)
  waiting for transfers between devices  14.5 us (15%)
  other arithmetic  4.08 us (4%)
  local copies, waits for them, and re-layouts  1.94 us (2%)
    all_to_all x1, blocking collectives, on_device(): sums = lax.all_to_all(sums, ('z', 'xh'), 0, 0, tiled=True)  23.3 us
    pallas_call x1, Pallas kernels, moments(): pl.pallas_call(moments_kernel, out_shape=(shape, shape), in_specs=[pl.Blo...  20.5 us
    ppermute x8, starting transfers between devices, ring(): lax.ppermute(value, axis, [(i, (i + step) % size) for i in range(size)])  15.2 us
    all_to_all x1, blocking collectives, on_device(): sums = lax.all_to_all(sums.transpose(1, 0, 2, 3), 'y', 0, 0, tiled=True)  13.2 us
    ppermute x1, waiting for transfers between devices, swap_x(): return lax.ppermute(value, ('xh', 'xl', 'c'), pairs)  7.63 us
    ppermute x8, waiting for transfers between devices, ring(): lax.ppermute(value, axis, [(i, (i + step) % size) for i in range(size)])  6.9 us
    ppermute x1, starting transfers between devices, swap_x(): return lax.ppermute(value, ('xh', 'xl', 'c'), pairs)  2.36 us
  transfers between devices with their start and end apart: 12, of which 6 were waited for; matrix products, arithmetic and copies ran while one was open for 3% of the time, Pallas kernels for 0%

profile of v1, /device:TPU:2, one launch (start us, length us, event | category | flops | bytes accessed | tf_op | source)
XLA Modules:
  0.0 96.4 jit_solution(5245239896387671744)
XLA Ops:
  0.6 1.7 %pad_maximum_fusion = bf16[2,4,14,14,256]{4,1,3,2,0:T(4,128)(2,1)S(1)} fusion(bf16[1,4,14,14,256]{4,1,3,2,0:T(4,128)(2,1)} %bitcast.42, bf16[1,4,14,14,256]{4,1,3,2,0:T(4,128)(2,1)} %bitcast.43), kind=kLoop, calls=%fused_computation.1 | loop fusion | flops 401408 | bytes 1605632 | tf_op jit(solution)/shard_map/stack | solution.py:35
  2.4 0.1 copy.14
  2.5 0.1 pad.4.clone
  2.6 2.4 %collective-permute-start.1 = (bf16[2,4,224,256]{3,2,1,0:T(8,128)(2,1)S(1)}, bf16[2,4,224,256]{3,2,1,0:T(8,128)(2,1)S(1)}, u32[]{:S(2)}, u32[]{:S(2)}) collective-permute-start(bf16[2,4,224,256]{3,2,1,0:T(8,128)(2,1)S(1)} %bitcast.35), channel_id=1, source_target_pairs={{0,2},{1,19},{2,0},{3,17},{16,18},{17,3},{18,16},{19,1},{4,6},{5,2... | collective-permute-start | bytes 2752520 | tf_op jit(solution)/shard_map/ppermute | solution.py:31
  5.0 0.0 collective-permute-start.4
  5.0 3.2 %collective-permute-start.3 = (bf16[144,1152]{1,0:T(8,128)(2,1)}, bf16[144,1152]{1,0:T(8,128)(2,1)S(1)}, u32[]{:S(2)}, u32[]{:S(2)}) collective-permute-start(bf16[144,1152]{1,0:T(8,128)(2,1)} %bitcast.20.s0), channel_id=1, source_target_pairs={{0,12},{4,0},{8,4},{12,8},{1,13},{5,1},{9,5},{13,9},{2,14},{6,2},{... | collective-permute-start | bytes 995336 | tf_op jit(solution)/shard_map/ppermute | solution.py:19
  8.2 0.0 collective-permute-start
  8.2 0.5 collective-permute-start.7
  8.7 7.6 %collective-permute-done.1.far = bf16[2,4,224,256]{3,2,1,0:T(8,128)(2,1)S(1)} collective-permute-done((bf16[2,4,224,256]{3,2,1,0:T(8,128)(2,1)S(1)}, bf16[2,4,224,256]{3,2,1,0:T(8,128)(2,1)S(1)}, u32[]{:S(2)}, u32[]{:S(2)}) %collective-permute-start.1) | collective-permute-done | bytes 917536 | tf_op jit(solution)/shard_map/ppermute | solution.py:31
  16.4 0.0 collective-permute-start.2
  16.4 0.7 constant_dynamic-update-slice_fusion.5
  17.1 0.1 stack.89.at_ref
  17.1 0.0 collective-permute-done.7
  17.2 0.7 pad_maximum_fusion.2
  17.9 2.0 %collective-permute-start.8 = (bf16[32,256]{1,0:T(8,128)(2,1)S(1)}, bf16[32,256]{1,0:T(8,128)(2,1)S(1)}, u32[]{:S(2)}, u32[]{:S(2)}) collective-permute-start(bf16[32,256]{1,0:T(8,128)(2,1)S(1)} %pad_maximum_fusion.2), channel_id=1, source_target_pairs={{0,2},{2,0},{1,3},{3,1},{4,6},{6,4},{5,7},{7,5},{8,10},{10,8},{9,1... | collective-permute-start | bytes 49160 | tf_op jit(solution)/shard_map/ppermute | solution.py:19
  19.9 0.7 constant_dynamic-update-slice_fusion.4
  20.6 1.0 %collective-permute-done.8 = bf16[32,256]{1,0:T(8,128)(2,1)S(1)} collective-permute-done((bf16[32,256]{1,0:T(8,128)(2,1)S(1)}, bf16[32,256]{1,0:T(8,128)(2,1)S(1)}, u32[]{:S(2)}, u32[]{:S(2)}) %collective-permute-start.8) | collective-permute-done | bytes 16416 | tf_op jit(solution)/shard_map/ppermute | solution.py:19
  21.6 0.7 pad_maximum_fusion.1
  22.3 2.8 %collective-permute-start.9 = (bf16[64,256]{1,0:T(8,128)(2,1)S(1)}, bf16[64,256]{1,0:T(8,128)(2,1)S(1)}, u32[]{:S(2)}, u32[]{:S(2)}) collective-permute-start(bf16[64,256]{1,0:T(8,128)(2,1)S(1)} %pad_maximum_fusion.1), channel_id=1, source_target_pairs={{0,12},{4,0},{8,4},{12,8},{1,13},{5,1},{9,5},{13,9},{2,14},{6,2},{... | collective-permute-start | bytes 98312 | tf_op jit(solution)/shard_map/ppermute | solution.py:19
  25.1 1.6 %collective-permute-done.9 = bf16[64,256]{1,0:T(8,128)(2,1)S(1)} collective-permute-done((bf16[64,256]{1,0:T(8,128)(2,1)S(1)}, bf16[64,256]{1,0:T(8,128)(2,1)S(1)}, u32[]{:S(2)}, u32[]{:S(2)}) %collective-permute-start.9) | collective-permute-done | bytes 32800 | tf_op jit(solution)/shard_map/ppermute | solution.py:19
  26.7 3.5 %collective-permute-start.10 = (bf16[64,256]{1,0:T(8,128)(2,1)S(1)}, bf16[64,256]{1,0:T(8,128)(2,1)S(1)}, u32[]{:S(2)}, u32[]{:S(2)}) collective-permute-start(bf16[64,256]{1,0:T(8,128)(2,1)S(1)} %collective-permute-done.9), channel_id=1, source_target_pairs={{0,12},{4,0},{8,4},{12,8},{1,13},{5,1},{9,5},{13,9},{2,14},{6,2},{... | collective-permute-start | bytes 98312 | tf_op jit(solution)/shard_map/ppermute | solution.py:19
  30.2 0.0 collective-permute-done.4.sm
  30.2 0.0 collective-permute-start.11
  30.3 0.0 collective-permute-done.3.sp
  30.3 0.1 collective-permute-start.6
  30.4 1.4 %collective-permute-done.10 = bf16[64,256]{1,0:T(8,128)(2,1)S(1)} collective-permute-done((bf16[64,256]{1,0:T(8,128)(2,1)S(1)}, bf16[64,256]{1,0:T(8,128)(2,1)S(1)}, u32[]{:S(2)}, u32[]{:S(2)}) %collective-permute-start.10) | collective-permute-done | bytes 32800 | tf_op jit(solution)/shard_map/ppermute | solution.py:19
  31.8 3.5 %collective-permute-start.5 = (bf16[72,1152]{1,0:T(8,128)(2,1)S(1)}, bf16[72,1152]{1,0:T(8,128)(2,1)S(1)}, u32[]{:S(2)}, u32[]{:S(2)}) collective-permute-start(bf16[72,1152]{1,0:T(8,128)(2,1)S(1)} %slice.16), channel_id=1, source_target_pairs={{0,12},{4,0},{8,4},{12,8},{1,13},{5,1},{9,5},{13,9},{2,14},{6,2},{... | collective-permute-start | bytes 497672 | tf_op jit(solution)/shard_map/ppermute | solution.py:19
  35.4 0.0 collective-permute-done.11
  35.4 1.8 %collective-permute-done.6.s2b = bf16[72,1152]{1,0:T(8,128)(2,1)S(1)} collective-permute-done((bf16[72,1152]{1,0:T(8,128)(2,1)S(1)}, bf16[72,1152]{1,0:T(8,128)(2,1)S(1)}, u32[]{:S(2)}, u32[]{:S(2)}) %collective-permute-start.6) | collective-permute-done | bytes 165920 | tf_op jit(solution)/shard_map/ppermute | solution.py:19
  37.1 1.1 %collective-permute-done.5.s2a = bf16[72,1152]{1,0:T(8,128)(2,1)S(1)} collective-permute-done((bf16[72,1152]{1,0:T(8,128)(2,1)S(1)}, bf16[72,1152]{1,0:T(8,128)(2,1)S(1)}, u32[]{:S(2)}, u32[]{:S(2)}) %collective-permute-start.5) | collective-permute-done | bytes 165920 | tf_op jit(solution)/shard_map/ppermute | solution.py:19
  38.2 0.0 collective-permute-done.other
  38.2 0.0 collective-permute-done.2.far_other
  38.2 20.5 %moments.1 = (f32[2,288,256]{2,1,0:T(8,128)S(1)}, f32[2,288,256]{2,1,0:T(8,128)S(1)}) custom-call(s32[17]{0:T(128)S(1)} %stack.89.at_ref, bf16[2,4,224,256]{3,2,1,0:T(8,128)(2,1)S(1)} %bitcast.37, bf16[2,4,224,256]{3,2,1,0:T(8,128)(2,1)S(1)} %collective-permute-done.other, bf16[2,4,224,256]{3,2,1,0:T(8,128)(2,1)S(1)} %collective-permute-done.1.far, ...), custom_call_target="tpu_custom_call" | custom-call | tf_op jit(solution)/shard_map/moments/pallas_call | solution.py:95
  58.8 0.1 maximum_bitcast_fusion
  58.9 13.2 %all_to_all.14 = bf16[4,2,144,256]{3,2,1,0:T(8,128)(2,1)S(1)} all-to-all(bf16[4,2,144,256]{3,2,1,0:T(8,128)(2,1)S(1)} %maximum_bitcast_fusion), channel_id=1, replica_groups=mesh['z'=8,'xh'=2,'y'=4,'xl'=2,'c'=2] {'y'}, dimensions={0} | all-to-all | bytes 1179648 | tf_op jit(solution)/shard_map/all_to_all | solution.py:138
  72.1 0.1 convert_reduce_fusion
  72.2 0.2 copy.13
  72.4 23.3 %all_to_all.15 = f32[16,16,288]{2,1,0:T(8,128)S(1)} all-to-all(f32[16,16,288]{2,1,0:T(8,128)S(1)} %bitcast.38), channel_id=1, replica_groups=mesh['z'=8,'xh'=2,'y'=4,'xl'=2,'c'=2] {'z','xh'}, dimensions={0} | all-to-all | bytes 589824 | tf_op jit(solution)/shard_map/all_to_all | solution.py:140
  95.7 0.7 slice_multiply_fusion
  (9 shorter events, 0.1 us)
Async XLA Ops:
  2.6 13.7 %collective-permute-start.1 = (bf16[2,4,224,256]{3,2,1,0:T(8,128)(2,1)S(1)}, bf16[2,4,224,256]{3,2,1,0:T(8,128)(2,1)S(1)}, u32[]{:S(2)}, u32[]{:S(2)}) collective-permute-start(bf16[2,4,224,256]{3,2,1,0:T(8,128)(2,1)S(1)} %bitcast.35), channel_id=1, source_target_pairs={{0,2},{1,19},{2,0},{3,17},{16,18},{17,3},{18,16},{19,1},{4,6},{5,2... | collective-permute-start | bytes 2752520 | tf_op jit(solution)/shard_map/ppermute | solution.py:31
  5.0 25.3 %collective-permute-start.4 = (bf16[144,1152]{1,0:T(8,128)(2,1)}, bf16[144,1152]{1,0:T(8,128)(2,1)S(1)}, u32[]{:S(2)}, u32[]{:S(2)}) collective-permute-start(bf16[144,1152]{1,0:T(8,128)(2,1)} %bitcast.20.s0), channel_id=1, source_target_pairs={{0,4},{4,8},{8,12},{12,0},{1,5},{5,9},{9,13},{13,1},{2,6},{6,10},{... | collective-permute-start | bytes 995336 | tf_op jit(solution)/shard_map/ppermute | solution.py:19
  5.0 25.3 %collective-permute-start.3 = (bf16[144,1152]{1,0:T(8,128)(2,1)}, bf16[144,1152]{1,0:T(8,128)(2,1)S(1)}, u32[]{:S(2)}, u32[]{:S(2)}) collective-permute-start(bf16[144,1152]{1,0:T(8,128)(2,1)} %bitcast.20.s0), channel_id=1, source_target_pairs={{0,12},{4,0},{8,4},{12,8},{1,13},{5,1},{9,5},{13,9},{2,14},{6,2},{... | collective-permute-start | bytes 995336 | tf_op jit(solution)/shard_map/ppermute | solution.py:19
  8.2 30.0 %collective-permute-start = (bf16[2,4,224,256]{3,2,1,0:T(8,128)(2,1)S(1)}, bf16[2,4,224,256]{3,2,1,0:T(8,128)(2,1)S(1)}, u32[]{:S(2)}, u32[]{:S(2)}) collective-permute-start(bf16[2,4,224,256]{3,2,1,0:T(8,128)(2,1)S(1)} %bitcast.36), channel_id=1, source_target_pairs={{0,1},{1,0},{2,3},{3,2},{4,5},{5,4},{6,7},{7,6},{8,9},{9,8},{10,11... | collective-permute-start | bytes 2752520 | tf_op jit(solution)/shard_map/ppermute | solution.py:23
  8.2 8.9 %collective-permute-start.7 = (bf16[16,256]{1,0:T(8,128)(2,1)}, bf16[16,256]{1,0:T(8,128)(2,1)}, u32[]{:S(2)}, u32[]{:S(2)}) collective-permute-start(bf16[16,256]{1,0:T(8,128)(2,1)} %bitcast.21), channel_id=1, source_target_pairs={{0,1},{1,0},{2,3},{3,2},{4,5},{5,4},{6,7},{7,6},{8,9},{9,8},{10,11... | collective-permute-start | bytes 24584 | tf_op jit(solution)/shard_map/ppermute | solution.py:23
  16.4 21.9 %collective-permute-start.2 = (bf16[2,4,224,256]{3,2,1,0:T(8,128)(2,1)S(1)}, bf16[2,4,224,256]{3,2,1,0:T(8,128)(2,1)}, u32[]{:S(2)}, u32[]{:S(2)}) collective-permute-start(bf16[2,4,224,256]{3,2,1,0:T(8,128)(2,1)S(1)} %collective-permute-done.1.far), channel_id=1, source_target_pairs={{0,1},{1,0},{2,3},{3,2},{4,5},{5,4},{6,7},{7,6},{8,9},{9,8},{10,11... | collective-permute-start | bytes 2752520 | tf_op jit(solution)/shard_map/ppermute | solution.py:23
  17.9 3.7 %collective-permute-start.8 = (bf16[32,256]{1,0:T(8,128)(2,1)S(1)}, bf16[32,256]{1,0:T(8,128)(2,1)S(1)}, u32[]{:S(2)}, u32[]{:S(2)}) collective-permute-start(bf16[32,256]{1,0:T(8,128)(2,1)S(1)} %pad_maximum_fusion.2), channel_id=1, source_target_pairs={{0,2},{2,0},{1,3},{3,1},{4,6},{6,4},{5,7},{7,5},{8,10},{10,8},{9,1... | collective-permute-start | bytes 49160 | tf_op jit(solution)/shard_map/ppermute | solution.py:19
  22.3 4.4 %collective-permute-start.9 = (bf16[64,256]{1,0:T(8,128)(2,1)S(1)}, bf16[64,256]{1,0:T(8,128)(2,1)S(1)}, u32[]{:S(2)}, u32[]{:S(2)}) collective-permute-start(bf16[64,256]{1,0:T(8,128)(2,1)S(1)} %pad_maximum_fusion.1), channel_id=1, source_target_pairs={{0,12},{4,0},{8,4},{12,8},{1,13},{5,1},{9,5},{13,9},{2,14},{6,2},{... | collective-permute-start | bytes 98312 | tf_op jit(solution)/shard_map/ppermute | solution.py:19
  26.7 5.1 %collective-permute-start.10 = (bf16[64,256]{1,0:T(8,128)(2,1)S(1)}, bf16[64,256]{1,0:T(8,128)(2,1)S(1)}, u32[]{:S(2)}, u32[]{:S(2)}) collective-permute-start(bf16[64,256]{1,0:T(8,128)(2,1)S(1)} %collective-permute-done.9), channel_id=1, source_target_pairs={{0,12},{4,0},{8,4},{12,8},{1,13},{5,1},{9,5},{13,9},{2,14},{6,2},{... | collective-permute-start | bytes 98312 | tf_op jit(solution)/shard_map/ppermute | solution.py:19
  30.2 5.1 %collective-permute-start.11 = (bf16[64,256]{1,0:T(8,128)(2,1)S(1)}, bf16[64,256]{1,0:T(8,128)(2,1)S(1)}, u32[]{:S(2)}, u32[]{:S(2)}) collective-permute-start(bf16[64,256]{1,0:T(8,128)(2,1)S(1)} %pad_maximum_fusion.1), channel_id=1, source_target_pairs={{0,4},{4,8},{8,12},{12,0},{1,5},{5,9},{9,13},{13,1},{2,6},{6,10},{... | collective-permute-start | bytes 98312 | tf_op jit(solution)/shard_map/ppermute | solution.py:19
  30.3 6.9 %collective-permute-start.6 = (bf16[72,1152]{1,0:T(8,128)(2,1)S(1)}, bf16[72,1152]{1,0:T(8,128)(2,1)S(1)}, u32[]{:S(2)}, u32[]{:S(2)}) collective-permute-start(bf16[72,1152]{1,0:T(8,128)(2,1)S(1)} %slice.17), channel_id=1, source_target_pairs={{0,4},{4,8},{8,12},{12,0},{1,5},{5,9},{9,13},{13,1},{2,6},{6,10},{... | collective-permute-start | bytes 497672 | tf_op jit(solution)/shard_map/ppermute | solution.py:19
  31.8 6.4 %collective-permute-start.5 = (bf16[72,1152]{1,0:T(8,128)(2,1)S(1)}, bf16[72,1152]{1,0:T(8,128)(2,1)S(1)}, u32[]{:S(2)}, u32[]{:S(2)}) collective-permute-start(bf16[72,1152]{1,0:T(8,128)(2,1)S(1)} %slice.16), channel_id=1, source_target_pairs={{0,12},{4,0},{8,4},{12,8},{1,13},{5,1},{9,5},{13,9},{2,14},{6,2},{... | collective-permute-start | bytes 497672 | tf_op jit(solution)/shard_map/ppermute | solution.py:19

commit v2 on v1

v2 whole, which is shorter than its diff:
```python
import functools
import math

import jax
import jax.numpy as jnp
from jax import lax
from jax.experimental import pallas as pl
from jax.experimental.pallas import tpu as pltpu
from jax.sharding import Mesh, PartitionSpec as P

AXES = ("z", "xh", "y", "xl", "c")
SIZES = (8, 2, 4, 2, 2)
BF16 = jnp.bfloat16
F32 = jnp.float32
CONTRACT_LAST = (((1,), (1,)), ((), ()))


def ring(value, axis, size, step):
    return lax.ppermute(value, axis, [(i, (i + step) % size) for i in range(size)])


def swap_cores(value):
    return lax.ppermute(value, "c", [(0, 1), (1, 0)])


def swap_x(value):
    def partner(x, core):
        return (x + 1 if (x + core) % 2 == 0 else x - 1) % 4

    pairs = [(x * 2 + core, partner(x, core) * 2 + core) for x in range(4) for core in range(2)]
    return lax.ppermute(value, ("xh", "xl", "c"), pairs)


def prepare(inputs, out_grads):
    both = jnp.stack([inputs, out_grads])
    padded = jnp.pad(both, ((0, 0), (0, 0), (0, 0), (0, 2), (0, 0)))
    return padded.reshape(2, inputs.shape[0], 224, 256)


def moments_kernel(
    at_ref, own, other, far, far_other, a0, b0, ap, bp, am, bm, a2, b2, u_near, u_core,
    squares_ref, linear_ref, basis, rows, patches, grads, out_basis,
):
    y = at_ref[0]

    for step, top, bottom in ((0, a0, b0), (1, ap, bp), (3, am, bm), (2, a2, b2)):
        owner = lax.rem(y + step, 4)
        at = pl.multiple_of((owner % 2) * 144, 16)
        basis[owner // 2, pl.ds(at, 80), :] = top[...]
        basis[owner // 2, pl.ds(pl.multiple_of(at + 80, 16), 64), :] = bottom[0:64, :]
    for piece in range(16):
        source = u_near if piece < 8 else u_core
        row = pl.multiple_of(at_ref[1 + piece], 16)
        out_basis[pl.ds(row, 16), :] = source[16 * (piece % 8) : 16 * (piece % 8) + 16, :]
    rows[...] = jnp.zeros_like(rows)
    grads[...] = jnp.zeros_like(grads)
    squares_ref[...] = jnp.zeros_like(squares_ref)
    linear_ref[...] = jnp.zeros_like(linear_ref)

    for group in (own, other, far, far_other):
        for n in range(4):
            feature = group[0, n].astype(F32)
            rows[n, 0, 16:240, :] = pltpu.roll(feature, 1, 0).astype(BF16)
            rows[n, 1, 16:240, :] = group[0, n]
            rows[n, 2, 16:240, :] = pltpu.roll(feature, 223, 0).astype(BF16)
            at = slice(256 * n, 256 * n + 256)
            for tap in range(9):
                ky, kx = tap // 3, tap % 3
                shifted = rows[n, kx, 16 * ky : 16 * ky + 256, :]
                if tap < 4:
                    patches[0, at, 256 * tap : 256 * tap + 256] = shifted
                elif tap == 4:
                    patches[0, at, 1024:1152] = shifted[:, :128]
                    patches[1, at, 0:128] = shifted[:, 128:]
                else:
                    patches[1, at, 256 * tap - 1152 : 256 * tap - 896] = shifted
            grads[n, 0:224, :] = lax.dot_general(
                group[1, n], out_basis[...], CONTRACT_LAST, preferred_element_type=F32
            ).astype(BF16)
        for block in range(2):
            rotated = lax.dot_general(
                basis[block], patches[block], CONTRACT_LAST, preferred_element_type=F32
            ).astype(BF16)
            squares, linear = squares_ref[block], linear_ref[block]
            for n in range(4):
                projected = jnp.dot(
                    rotated[:, 256 * n : 256 * n + 256], grads[n], preferred_element_type=F32
                )
                squares = squares + projected * projected
                linear = linear + projected
            squares_ref[block] = squares
            linear_ref[block] = linear


def moments(at, *operands):
    shape = jax.ShapeDtypeStruct((2, 288, 256), F32)
    vmem = pl.BlockSpec(memory_space=pltpu.VMEM)
    return pl.pallas_call(
        moments_kernel,
        out_shape=(shape, shape),
        in_specs=[pl.BlockSpec(memory_space=pltpu.SMEM)] + [vmem] * len(operands),
        out_specs=(vmem, vmem),
        scratch_shapes=[
            pltpu.VMEM((2, 288, 1152), BF16),
            pltpu.VMEM((4, 3, 288, 256), BF16),
            pltpu.VMEM((2, 1024, 1152), BF16),
            pltpu.VMEM((4, 256, 256), BF16),
            pltpu.VMEM((256, 256), BF16),
        ],
        compiler_params=pltpu.CompilerParams(vmem_limit_bytes=40 * 2**20),
        name="moments",
    )(at, *operands)


def on_device(inputs, out_grads, patch_basis, output_basis):
    examples = inputs.shape[0] * math.prod(SIZES)
    y, xl, core = lax.axis_index("y"), lax.axis_index("xl"), lax.axis_index("c")

    shard = jnp.concatenate(
        [patch_basis.T, jnp.pad(output_basis.T, ((0, 0), (0, 1152 - 256)))]
    )
    a0, b0 = shard[:80], shard[80:]
    ap, am = ring(a0, "y", 4, 3), ring(a0, "y", 4, 1)
    bp, bm = ring(b0, "y", 4, 3), ring(b0, "y", 4, 1)
    a2, b2 = ring(ap, "y", 4, 3), ring(bm, "y", 4, 1)
    own = prepare(inputs, out_grads)
    other = swap_cores(own)
    far = swap_x(own)
    far_other = swap_cores(far)
    u_ring = jnp.concatenate([piece[64:, :256] for piece in (b0, bp, b2, bm)])
    u_near = jnp.concatenate([u_ring, ring(u_ring, "xl", 2, 1)])
    u_core = swap_cores(u_near)
    offsets = [
        (((y + dy) % 4 * 2 + (xl + dx) % 2) * 2 + (core + dc) % 2) * 16
        for dc in range(2)
        for dx in range(2)
        for dy in range(4)
    ]
    at = jnp.stack([y] + offsets).astype(jnp.int32)
    squares, linear = moments(
        at, own, other, far, far_other, a0, b0, ap, bp, am, bm, a2, b2, u_near, u_core
    )

    sums = jnp.stack([squares, linear]).astype(BF16).reshape(2, 4, 144, 256)
    sums = lax.all_to_all(sums.transpose(1, 0, 2, 3), "y", 0, 0, tiled=True)
    sums = jnp.sum(sums.astype(F32), axis=0).reshape(288, 256).T
    sums = lax.all_to_all(sums, ("z", "xh"), 0, 0, tiled=True)
    sums = jnp.sum(sums.reshape(16, 16, 288), axis=0)
    side = inputs.shape[1]
    return (
        sums[:, :144] * (1.0 / (side * side * examples)),
        sums[:, 144:] * (1.0 / (side * math.sqrt(examples))),
    )


def solution(mesh):
    fine = Mesh(mesh.devices.reshape(SIZES), AXES)
    every, columns = ("z", "xh", "y", "xl", "c"), ("y", "xl", "c")
    return jax.shard_map(
        on_device,
        mesh=fine,
        in_specs=(P(every), P(every), P(None, columns), P(None, columns)),
        out_specs=(P(("z", "xh"), columns), P(("z", "xh"), columns)),
        check_vma=False,
    )
```

time: 97 us -> 76.7 us (0.79)
  Pallas kernels: 20.5 us -> 10.2 us
  starting transfers between devices: 18 us -> 11 us
  waiting for transfers between devices: 14.5 us -> 12.7 us
  other arithmetic: 4.08 us -> 2.67 us
  local copies, waits for them, and re-layouts: 1.94 us -> 3.18 us
    pallas_call x1, Pallas kernels: 20.5 us -> 10.2 us  [moments(): pl.pallas_call(moments_kernel, out_shape=(shape, shape), in_specs=[pl.Blo...]
    ppermute x8 -> x7, starting transfers between devices: 15.2 us -> 8.65 us  [ring(): lax.ppermute(value, axis, [(i, (i + step) % size) for i in range(size)])]
    ppermute x1, waiting for transfers between devices: 7.63 us -> 4.36 us  [swap_x(): return lax.ppermute(value, ('xh', 'xl', 'c'), pairs)]
    ppermute x8 -> x7, waiting for transfers between devices: 6.9 us -> 8.38 us  [ring(): lax.ppermute(value, axis, [(i, (i + step) % size) for i in range(size)])]
    concatenate x2, other arithmetic: 1.44 us -> 0.03 us  [the longest x1 0.03 us: on_device(): jnp.concatenate([patch_basis.T, jnp.pad(output_basis.T, ((0, 0), (0, 1152...]
    unnamed x6 -> x12, local copies, waits for them, and re-layouts: 1.55 us -> 2.32 us
  transfers between devices with their start and end apart: 12 -> 11, of which waited for: 6 -> 4; matrix products, arithmetic and copies ran while one was open for 3% -> 1% of each run, Pallas kernels for 0% -> 0%
where the time goes in v2:
time: 76.7 us; the launch traced here: 76.4 us
  blocking collectives  35.7 us (47%)
  waiting for transfers between devices  12.7 us (17%)
  starting transfers between devices  11 us (14%)
  Pallas kernels  10.2 us (13%)
  local copies, waits for them, and re-layouts  3.18 us (4%)
  other arithmetic  2.67 us (3%)
  between operations  0.85 us (1%)
    all_to_all x1, blocking collectives, on_device(): sums = lax.all_to_all(sums, ('z', 'xh'), 0, 0, tiled=True)  22.8 us
    all_to_all x1, blocking collectives, on_device(): sums = lax.all_to_all(sums.transpose(1, 0, 2, 3), 'y', 0, 0, tiled=True)  12.9 us
    pallas_call x1, Pallas kernels, moments(): pl.pallas_call(moments_kernel, out_shape=(shape, shape), in_specs=[pl.Blo...  10.2 us
    ppermute x7, starting transfers between devices, ring(): lax.ppermute(value, axis, [(i, (i + step) % size) for i in range(size)])  8.65 us
    ppermute x7, waiting for transfers between devices, ring(): lax.ppermute(value, axis, [(i, (i + step) % size) for i in range(size)])  8.38 us
    ppermute x1, waiting for transfers between devices, swap_x(): return lax.ppermute(value, ('xh', 'xl', 'c'), pairs)  4.36 us
    ppermute x1, starting transfers between devices, swap_x(): return lax.ppermute(value, ('xh', 'xl', 'c'), pairs)  2.36 us
    unnamed x12, local copies, waits for them, and re-layouts  2.32 us
  transfers between devices with their start and end apart: 11, of which 4 were waited for; matrix products, arithmetic and copies ran while one was open for 1% of the time, Pallas kernels for 0%

profile of v2, /device:TPU:2, one launch (start us, length us, event | category | flops | bytes accessed | tf_op | source)
XLA Modules:
  0.0 76.4 jit_solution(6806823319940621070)
XLA Ops:
  0.6 1.7 %pad_maximum_fusion = bf16[2,4,14,14,256]{4,1,3,2,0:T(4,128)(2,1)S(1)} fusion(bf16[1,4,14,14,256]{4,1,3,2,0:T(4,128)(2,1)} %bitcast.43, bf16[1,4,14,14,256]{4,1,3,2,0:T(4,128)(2,1)} %bitcast.44), kind=kLoop, calls=%fused_computation.1 | loop fusion | flops 401408 | bytes 1605632 | tf_op jit(solution)/shard_map/stack | solution.py:35
  2.4 0.1 copy.14
  2.5 0.0 copy-start.3
  2.5 0.0 copy-start.4
  2.5 0.1 pad.8.clone
  2.6 2.4 %collective-permute-start.1 = (bf16[2,4,224,256]{3,2,1,0:T(8,128)(2,1)S(1)}, bf16[2,4,224,256]{3,2,1,0:T(8,128)(2,1)S(1)}, u32[]{:S(2)}, u32[]{:S(2)}) collective-permute-start(bf16[2,4,224,256]{3,2,1,0:T(8,128)(2,1)S(1)} %bitcast.35), channel_id=1, source_target_pairs={{0,2},{1,19},{2,0},{3,17},{16,18},{17,3},{18,16},{19,1},{4,6},{5,2... | collective-permute-start | bytes 2752520 | tf_op jit(solution)/shard_map/ppermute | solution.py:31
  5.0 0.0 copy-done.3
  5.0 0.0 copy-done.4
  5.0 0.1 collective-permute-start.6
  5.2 3.2 %collective-permute-start.4 = (bf16[80,1152]{1,0:T(8,128)(2,1)S(1)}, bf16[80,1152]{1,0:T(8,128)(2,1)S(1)}, u32[]{:S(2)}, u32[]{:S(2)}) collective-permute-start(bf16[80,1152]{1,0:T(8,128)(2,1)S(1)} %get-tuple-element.6.b0), channel_id=1, source_target_pairs={{0,12},{4,0},{8,4},{12,8},{1,13},{5,1},{9,5},{13,9},{2,14},{6,2},{... | collective-permute-start | bytes 552968 | tf_op jit(solution)/shard_map/ppermute | solution.py:19
  8.4 0.0 collective-permute-start
  8.4 0.3 collective-permute-start.3
  8.6 3.2 %collective-permute-done.6.bm = bf16[80,1152]{1,0:T(8,128)(2,1)S(1)} collective-permute-done((bf16[80,1152]{1,0:T(8,128)(2,1)S(1)}, bf16[80,1152]{1,0:T(8,128)(2,1)S(1)}, u32[]{:S(2)}, u32[]{:S(2)}) %collective-permute-start.6) | collective-permute-done | bytes 184352 | tf_op jit(solution)/shard_map/ppermute | solution.py:19
  11.9 0.1 collective-permute-start.8
  12.0 4.4 %collective-permute-done.1.far = bf16[2,4,224,256]{3,2,1,0:T(8,128)(2,1)S(1)} collective-permute-done((bf16[2,4,224,256]{3,2,1,0:T(8,128)(2,1)S(1)}, bf16[2,4,224,256]{3,2,1,0:T(8,128)(2,1)S(1)}, u32[]{:S(2)}, u32[]{:S(2)}) %collective-permute-start.1) | collective-permute-done | bytes 917536 | tf_op jit(solution)/shard_map/ppermute | solution.py:31
  16.4 0.0 collective-permute-start.2
  16.4 0.0 collective-permute-done.4.bp
  16.4 2.2 %collective-permute-done.8.b2 = bf16[80,1152]{1,0:T(8,128)(2,1)S(1)} collective-permute-done((bf16[80,1152]{1,0:T(8,128)(2,1)S(1)}, bf16[80,1152]{1,0:T(8,128)(2,1)S(1)}, u32[]{:S(2)}, u32[]{:S(2)}) %collective-permute-start.8) | collective-permute-done | bytes 184352 | tf_op jit(solution)/shard_map/ppermute | solution.py:19
  18.6 0.0 copy-start
  18.6 0.7 copy-done
  19.3 1.7 %collective-permute-start.9 = (bf16[64,256]{1,0:T(8,128)(2,1)S(1)}, bf16[64,256]{1,0:T(8,128)(2,1)S(1)}, u32[]{:S(2)}, u32[]{:S(2)}) collective-permute-start(bf16[64,256]{1,0:T(8,128)(2,1)S(1)} %pad_maximum_fusion.1), channel_id=1, source_target_pairs={{0,2},{2,0},{1,3},{3,1},{4,6},{6,4},{5,7},{7,5},{8,10},{10,8},{9,1... | collective-permute-start | bytes 98312 | tf_op jit(solution)/shard_map/ppermute | solution.py:19
  21.0 0.0 collective-permute-start.5
  21.0 0.0 collective-permute-done.3.ap
  21.0 3.2 %collective-permute-start.7 = (bf16[80,1152]{1,0:T(8,128)(2,1)}, bf16[80,1152]{1,0:T(8,128)(2,1)}, u32[]{:S(2)}, u32[]{:S(2)}) collective-permute-start(bf16[80,1152]{1,0:T(8,128)(2,1)} %collective-permute-done.3.ap), channel_id=1, source_target_pairs={{0,12},{4,0},{8,4},{12,8},{1,13},{5,1},{9,5},{13,9},{2,14},{6,2},{... | collective-permute-start | bytes 552968 | tf_op jit(solution)/shard_map/ppermute | solution.py:19
  24.2 0.0 collective-permute-done.9
  24.2 0.0 collective-permute-start.10
  24.3 0.6 stack.89.at_ref
  24.9 2.9 %collective-permute-done.5.am = bf16[80,1152]{1,0:T(8,128)(2,1)} collective-permute-done((bf16[80,1152]{1,0:T(8,128)(2,1)S(1)}, bf16[80,1152]{1,0:T(8,128)(2,1)}, u32[]{:S(2)}, u32[]{:S(2)}) %collective-permute-start.5) | collective-permute-done | bytes 184352 | tf_op jit(solution)/shard_map/ppermute | solution.py:19
  27.8 0.0 collective-permute-done.7.a2
  27.8 0.0 collective-permute-done.10.u_core
  27.8 0.0 collective-permute-done.other
  27.8 0.0 collective-permute-done.2.far_other
  27.8 0.0 copy-start.1
  27.9 0.9 %copy-done.1 = bf16[80,1152]{1,0:T(8,128)(2,1)S(1)} copy-done((bf16[80,1152]{1,0:T(8,128)(2,1)S(1)}, bf16[80,1152]{1,0:T(8,128)(2,1)}, u32[]{:S(2)}) %copy-start.1) | copy-done | bytes 184344
  28.8 0.0 copy-start.2
  28.8 0.6 copy-done.2
  29.3 10.2 %moments.1 = (f32[2,288,256]{2,1,0:T(8,128)S(1)}, f32[2,288,256]{2,1,0:T(8,128)S(1)}) custom-call(s32[17]{0:T(128)S(1)} %copy-done.2, bf16[2,4,224,256]{3,2,1,0:T(8,128)(2,1)S(1)} %bitcast.37, bf16[2,4,224,256]{3,2,1,0:T(8,128)(2,1)S(1)} %collective-permute-done.other, bf16[2,4,224,256]{3,2,1,0:T(8,128)(2,1)S(1)} %collective-permute-done.1.far, ...), custom_call_target="tpu_custom_call" | custom-call | tf_op jit(solution)/shard_map/moments/pallas_call | solution.py:98
  39.7 0.1 maximum_bitcast_fusion
  39.7 12.9 %all_to_all.14 = bf16[4,2,144,256]{3,2,1,0:T(8,128)(2,1)S(1)} all-to-all(bf16[4,2,144,256]{3,2,1,0:T(8,128)(2,1)S(1)} %maximum_bitcast_fusion), channel_id=1, replica_groups=mesh['z'=8,'xh'=2,'y'=4,'xl'=2,'c'=2] {'y'}, dimensions={0} | all-to-all | bytes 1179648 | tf_op jit(solution)/shard_map/all_to_all | solution.py:145
  52.7 0.1 convert_reduce_fusion
  52.7 0.2 copy.13
  52.9 22.8 %all_to_all.15 = f32[16,16,288]{2,1,0:T(8,128)S(1)} all-to-all(f32[16,16,288]{2,1,0:T(8,128)S(1)} %bitcast.38), channel_id=1, replica_groups=mesh['z'=8,'xh'=2,'y'=4,'xl'=2,'c'=2] {'z','xh'}, dimensions={0} | all-to-all | bytes 589824 | tf_op jit(solution)/shard_map/all_to_all | solution.py:147
  75.7 0.7 slice_multiply_fusion
  (10 shorter events, 0.1 us)
Async XLA Ops:
  2.5 2.5 %copy-start.3 = (bf16[1152,144]{0,1:T(8,128)(2,1)S(1)}, bf16[1152,144]{0,1:T(8,128)(2,1)}, u32[]{:S(2)}) copy-start(bf16[1152,144]{0,1:T(8,128)(2,1)} %param.6) | copy-start | bytes 995332
  2.5 2.5 %copy-start.4 = (bf16[256,16]{0,1:T(8,128)(2,1)S(1)}, bf16[256,16]{0,1:T(8,128)(2,1)}, u32[]{:S(2)}) copy-start(bf16[256,16]{0,1:T(8,128)(2,1)} %param.7) | copy-start | bytes 24580
  2.6 13.7 %collective-permute-start.1 = (bf16[2,4,224,256]{3,2,1,0:T(8,128)(2,1)S(1)}, bf16[2,4,224,256]{3,2,1,0:T(8,128)(2,1)S(1)}, u32[]{:S(2)}, u32[]{:S(2)}) collective-permute-start(bf16[2,4,224,256]{3,2,1,0:T(8,128)(2,1)S(1)} %bitcast.35), channel_id=1, source_target_pairs={{0,2},{1,19},{2,0},{3,17},{16,18},{17,3},{18,16},{19,1},{4,6},{5,2... | collective-permute-start | bytes 2752520 | tf_op jit(solution)/shard_map/ppermute | solution.py:31
  5.0 6.8 %collective-permute-start.6 = (bf16[80,1152]{1,0:T(8,128)(2,1)S(1)}, bf16[80,1152]{1,0:T(8,128)(2,1)S(1)}, u32[]{:S(2)}, u32[]{:S(2)}) collective-permute-start(bf16[80,1152]{1,0:T(8,128)(2,1)S(1)} %get-tuple-element.6.b0), channel_id=1, source_target_pairs={{0,4},{4,8},{8,12},{12,0},{1,5},{5,9},{9,13},{13,1},{2,6},{6,10},{... | collective-permute-start | bytes 552968 | tf_op jit(solution)/shard_map/ppermute | solution.py:19
  5.2 11.2 %collective-permute-start.4 = (bf16[80,1152]{1,0:T(8,128)(2,1)S(1)}, bf16[80,1152]{1,0:T(8,128)(2,1)S(1)}, u32[]{:S(2)}, u32[]{:S(2)}) collective-permute-start(bf16[80,1152]{1,0:T(8,128)(2,1)S(1)} %get-tuple-element.6.b0), channel_id=1, source_target_pairs={{0,12},{4,0},{8,4},{12,8},{1,13},{5,1},{9,5},{13,9},{2,14},{6,2},{... | collective-permute-start | bytes 552968 | tf_op jit(solution)/shard_map/ppermute | solution.py:19
  8.4 19.5 %collective-permute-start = (bf16[2,4,224,256]{3,2,1,0:T(8,128)(2,1)S(1)}, bf16[2,4,224,256]{3,2,1,0:T(8,128)(2,1)S(1)}, u32[]{:S(2)}, u32[]{:S(2)}) collective-permute-start(bf16[2,4,224,256]{3,2,1,0:T(8,128)(2,1)S(1)} %bitcast.36), channel_id=1, source_target_pairs={{0,1},{1,0},{2,3},{3,2},{4,5},{5,4},{6,7},{7,6},{8,9},{9,8},{10,11... | collective-permute-start | bytes 2752520 | tf_op jit(solution)/shard_map/ppermute | solution.py:23
  8.4 12.7 %collective-permute-start.3 = (bf16[80,1152]{1,0:T(8,128)(2,1)S(1)}, bf16[80,1152]{1,0:T(8,128)(2,1)}, u32[]{:S(2)}, u32[]{:S(2)}) collective-permute-start(bf16[80,1152]{1,0:T(8,128)(2,1)S(1)} %get-tuple-element.7.a0), channel_id=1, source_target_pairs={{0,12},{4,0},{8,4},{12,8},{1,13},{5,1},{9,5},{13,9},{2,14},{6,2},{... | collective-permute-start | bytes 552968 | tf_op jit(solution)/shard_map/ppermute | solution.py:19
  11.9 6.7 %collective-permute-start.8 = (bf16[80,1152]{1,0:T(8,128)(2,1)S(1)}, bf16[80,1152]{1,0:T(8,128)(2,1)S(1)}, u32[]{:S(2)}, u32[]{:S(2)}) collective-permute-start(bf16[80,1152]{1,0:T(8,128)(2,1)S(1)} %collective-permute-done.6.bm), channel_id=1, source_target_pairs={{0,4},{4,8},{8,12},{12,0},{1,5},{5,9},{9,13},{13,1},{2,6},{6,10},{... | collective-permute-start | bytes 552968 | tf_op jit(solution)/shard_map/ppermute | solution.py:19
  16.4 11.5 %collective-permute-start.2 = (bf16[2,4,224,256]{3,2,1,0:T(8,128)(2,1)S(1)}, bf16[2,4,224,256]{3,2,1,0:T(8,128)(2,1)}, u32[]{:S(2)}, u32[]{:S(2)}) collective-permute-start(bf16[2,4,224,256]{3,2,1,0:T(8,128)(2,1)S(1)} %collective-permute-done.1.far), channel_id=1, source_target_pairs={{0,1},{1,0},{2,3},{3,2},{4,5},{5,4},{6,7},{7,6},{8,9},{9,8},{10,11... | collective-permute-start | bytes 2752520 | tf_op jit(solution)/shard_map/ppermute | solution.py:23
  18.6 0.7 copy-start
  19.3 4.9 %collective-permute-start.9 = (bf16[64,256]{1,0:T(8,128)(2,1)S(1)}, bf16[64,256]{1,0:T(8,128)(2,1)S(1)}, u32[]{:S(2)}, u32[]{:S(2)}) collective-permute-start(bf16[64,256]{1,0:T(8,128)(2,1)S(1)} %pad_maximum_fusion.1), channel_id=1, source_target_pairs={{0,2},{2,0},{1,3},{3,1},{4,6},{6,4},{5,7},{7,5},{8,10},{10,8},{9,1... | collective-permute-start | bytes 98312 | tf_op jit(solution)/shard_map/ppermute | solution.py:19
  21.0 6.9 %collective-permute-start.5 = (bf16[80,1152]{1,0:T(8,128)(2,1)S(1)}, bf16[80,1152]{1,0:T(8,128)(2,1)}, u32[]{:S(2)}, u32[]{:S(2)}) collective-permute-start(bf16[80,1152]{1,0:T(8,128)(2,1)S(1)} %get-tuple-element.7.a0), channel_id=1, source_target_pairs={{0,4},{4,8},{8,12},{12,0},{1,5},{5,9},{9,13},{13,1},{2,6},{6,10},{... | collective-permute-start | bytes 552968 | tf_op jit(solution)/shard_map/ppermute | solution.py:19
  21.0 6.8 %collective-permute-start.7 = (bf16[80,1152]{1,0:T(8,128)(2,1)}, bf16[80,1152]{1,0:T(8,128)(2,1)}, u32[]{:S(2)}, u32[]{:S(2)}) collective-permute-start(bf16[80,1152]{1,0:T(8,128)(2,1)} %collective-permute-done.3.ap), channel_id=1, source_target_pairs={{0,12},{4,0},{8,4},{12,8},{1,13},{5,1},{9,5},{13,9},{2,14},{6,2},{... | collective-permute-start | bytes 552968 | tf_op jit(solution)/shard_map/ppermute | solution.py:19
  24.2 3.6 %collective-permute-start.10 = (bf16[128,256]{1,0:T(8,128)(2,1)S(1)}, bf16[128,256]{1,0:T(8,128)(2,1)}, u32[]{:S(2)}, u32[]{:S(2)}) collective-permute-start(bf16[128,256]{1,0:T(8,128)(2,1)S(1)} %constant_dynamic-update-slice_fusion.u_near), channel_id=1, source_target_pairs={{0,1},{1,0},{2,3},{3,2},{4,5},{5,4},{6,7},{7,6},{8,9},{9,8},{10,11... | collective-permute-start | bytes 196616 | tf_op jit(solution)/shard_map/ppermute | solution.py:23
  27.8 0.9 %copy-start.1 = (bf16[80,1152]{1,0:T(8,128)(2,1)S(1)}, bf16[80,1152]{1,0:T(8,128)(2,1)}, u32[]{:S(2)}) copy-start(bf16[80,1152]{1,0:T(8,128)(2,1)} %copy-done) | copy-start | bytes 552964
  28.8 0.6 copy-start.2

commit v3 on v1

v3 whole, which is shorter than its diff:
```python
import math

import jax
import jax.numpy as jnp
from jax import lax
from jax.experimental import pallas as pl
from jax.experimental.pallas import tpu as pltpu
from jax.sharding import Mesh, PartitionSpec as P

AXES = ("z", "xh", "y", "xl", "c")
SIZES = (8, 2, 4, 2, 2)
BF16 = jnp.bfloat16
F32 = jnp.float32
CONTRACT_LAST = (((1,), (1,)), ((), ()))
TOP = 80


def ring(value, axis, size, step):
    return lax.ppermute(value, axis, [(i, (i + step) % size) for i in range(size)])


def swap_cores(value):
    return lax.ppermute(value, "c", [(0, 1), (1, 0)])


def swap_x(value, turn):
    def partner(x, core):
        return (x + 1 if (x + core + turn) % 2 == 0 else x - 1) % 4

    pairs = [(x * 2 + core, partner(x, core) * 2 + core) for x in range(4) for core in range(2)]
    return lax.ppermute(value, ("xh", "xl", "c"), pairs)


def prepare(inputs, out_grads):
    both = jnp.stack([inputs, out_grads])
    padded = jnp.pad(both, ((0, 0), (0, 0), (0, 0), (0, 2), (0, 0)))
    return padded.reshape(2, inputs.shape[0], 224, 256)


def clear(rows, grads):
    rows[...] = jnp.zeros_like(rows)
    grads[...] = jnp.zeros_like(grads)


def add_group(group, basis, out_basis, squares_ref, linear_ref, rows, patches, grads):
    for n in range(4):
        feature = group[0, n].astype(F32)
        rows[n, 0, 16:240, :] = pltpu.roll(feature, 1, 0).astype(BF16)
        rows[n, 1, 16:240, :] = group[0, n]
        rows[n, 2, 16:240, :] = pltpu.roll(feature, 223, 0).astype(BF16)
        at = slice(256 * n, 256 * n + 256)
        for tap in range(9):
            ky, kx = tap // 3, tap % 3
            shifted = rows[n, kx, 16 * ky : 16 * ky + 256, :]
            if tap < 4:
                patches[0, at, 256 * tap : 256 * tap + 256] = shifted
            elif tap == 4:
                patches[0, at, 1024:1152] = shifted[:, :128]
                patches[1, at, 0:128] = shifted[:, 128:]
            else:
                patches[1, at, 256 * tap - 1152 : 256 * tap - 896] = shifted
        grads[n, 0:224, :] = lax.dot_general(
            group[1, n], out_basis[...], CONTRACT_LAST, preferred_element_type=F32
        ).astype(BF16)
    for block in range(2):
        rotated = lax.dot_general(
            basis[block], patches[block], CONTRACT_LAST, preferred_element_type=F32
        ).astype(BF16)
        squares, linear = squares_ref[block], linear_ref[block]
        for n in range(4):
            projected = jnp.dot(
                rotated[:, 256 * n : 256 * n + 256], grads[n], preferred_element_type=F32
            )
            squares = squares + projected * projected
            linear = linear + projected
        squares_ref[block] = squares
        linear_ref[block] = linear


def near_kernel(
    own, other, here, plus, minus, two_top, two_bottom,
    u_here, u_two,
    squares_ref, linear_ref, basis, out_basis, rows, patches, grads,
):
    y, xl, core = lax.axis_index("y"), lax.axis_index("xl"), lax.axis_index("c")

    def at(step, first, count):
        owner = lax.rem(y + step, 4)
        start = pl.multiple_of((owner % 2) * 144 + first, 16)
        return owner // 2, pl.ds(start, count), slice(None)

    basis[at(0, 0, 144)] = here[...]
    basis[at(1, 0, 144)] = plus[...]
    basis[at(3, 0, 144)] = minus[...]
    basis[at(2, 0, TOP)] = two_top[0:TOP, :]
    basis[at(2, TOP, 144 - TOP)] = two_bottom[0 : 144 - TOP, :]
    for dy, (source, row) in enumerate(
        ((u_here, 0), (two_top, TOP), (u_two, 0), (two_bottom, 144 - TOP))
    ):
        for piece in range(4):
            dx, dc = piece // 2, piece % 2
            owner = (lax.rem(y + dy, 4) * 2 + lax.rem(xl + dx, 2)) * 2 + lax.rem(core + dc, 2)
            place = owner % 2 * 128 + owner // 2 * 16
            out_basis[pl.ds(pl.multiple_of(place, 16), 16), :] = source[
                row : row + 16, 256 * piece : 256 * piece + 256
            ]
    clear(rows, grads)
    squares_ref[...] = jnp.zeros_like(squares_ref)
    linear_ref[...] = jnp.zeros_like(linear_ref)
    for group in (own, other):
        add_group(group, basis, out_basis, squares_ref, linear_ref, rows, patches, grads)


def far_kernel(
    far, far_other, squares_in, linear_in, basis, out_basis,
    sums, squares_ref, linear_ref, rows, patches, grads,
):
    clear(rows, grads)
    squares_ref[...] = squares_in[...]
    linear_ref[...] = linear_in[...]
    for group in (far, far_other):
        add_group(group, basis, out_basis, squares_ref, linear_ref, rows, patches, grads)
    for owner in range(4):
        at = slice(144 * (owner % 2), 144 * (owner % 2) + 144)
        for half in range(2):
            lanes = slice(128 * half, 128 * half + 128)
            sums[4 * half + owner, 0] = squares_ref[owner // 2, at, lanes].astype(BF16)
            sums[4 * half + owner, 1] = linear_ref[owner // 2, at, lanes].astype(BF16)


def call(kernel, name, out_shape, scratch, *operands):
    vmem = pl.BlockSpec(memory_space=pltpu.VMEM)
    work = [
        pltpu.VMEM((4, 3, 288, 256), BF16),
        pltpu.VMEM((2, 1024, 1152), BF16),
        pltpu.VMEM((4, 256, 256), BF16),
    ]
    return pl.pallas_call(
        kernel,
        out_shape=out_shape,
        in_specs=[vmem] * len(operands),
        out_specs=jax.tree.map(lambda _: vmem, out_shape),
        scratch_shapes=scratch + work,
        compiler_params=pltpu.CompilerParams(vmem_limit_bytes=20 * 2**20),
        cost_estimate=pl.CostEstimate(flops=4 * 10**9, bytes_accessed=10**6, transcendentals=0),
        name=name,
    )(*operands)


def on_device(inputs, out_grads, patch_basis, output_basis):
    examples = inputs.shape[0] * math.prod(SIZES)
    side = inputs.shape[1]

    shard = patch_basis.T
    plus, minus = ring(shard, "y", 4, 3), ring(shard, "y", 4, 1)
    u0 = output_basis.T
    u1 = jnp.concatenate([u0, swap_cores(u0)], axis=1)
    u2 = jnp.concatenate([u1, swap_x(u1, 1)], axis=1)
    plus, minus, u2 = lax.optimization_barrier((plus, minus, u2))
    tail = jnp.pad(u2, ((0, 0), (0, 128)))
    two_top = ring(jnp.concatenate([plus[:TOP], tail]), "y", 4, 3)
    two_bottom = ring(jnp.concatenate([minus[TOP:], tail]), "y", 4, 1)
    u_two = ring(u2, "y", 4, 2)
    own = prepare(inputs, out_grads)
    other = swap_cores(own)
    far = swap_x(own, 0)
    far, two_top, two_bottom, u_two = lax.optimization_barrier(
        (far, two_top, two_bottom, u_two)
    )
    far_other = swap_cores(far)

    moment = jax.ShapeDtypeStruct((2, 288, 256), F32)
    squares, linear, basis, out_basis = call(
        near_kernel,
        "near_examples",
        (
            moment,
            moment,
            jax.ShapeDtypeStruct((2, 288, 1152), BF16),
            jax.ShapeDtypeStruct((256, 256), BF16),
        ),
        [],
        own, other, shard, plus, minus, two_top, two_bottom,
        u2, u_two,
    )
    sums = call(
        far_kernel,
        "far_examples",
        jax.ShapeDtypeStruct((8, 2, 144, 128), BF16),
        [pltpu.VMEM((2, 288, 256), F32)] * 2,
        far, far_other, squares, linear, basis, out_basis,
    )

    sums = lax.all_to_all(sums, ("xh", "y"), 0, 0, tiled=True)
    sums = jnp.sum(sums.astype(F32), axis=0).reshape(288, 128).T
    sums = lax.all_to_all(sums, "z", 0, 0, tiled=True)
    sums = jnp.sum(sums.reshape(8, 16, 288), axis=0)
    return (
        sums[:, :144] * (1.0 / (side * side * examples)),
        sums[:, 144:] * (1.0 / (side * math.sqrt(examples))),
    )


def solution(mesh):
    fine = Mesh(mesh.devices.reshape(SIZES), AXES)
    every, columns = ("z", "xh", "y", "xl", "c"), ("y", "xl", "c")
    return jax.shard_map(
        on_device,
        mesh=fine,
        in_specs=(P(every), P(every), P(None, columns), P(None, columns)),
        out_specs=(P(("z", "xh"), columns), P(("z", "xh"), columns)),
        check_vma=False,
    )
```

time: 97 us -> 68.5 us (0.71)
  Pallas kernels: 20.5 us -> 9.35 us
  starting transfers between devices: 18 us -> 9.43 us
  waiting for transfers between devices: 14.5 us -> 9.94 us
  other arithmetic: 4.08 us -> 2.54 us
  local copies, waits for them, and re-layouts: 1.94 us -> 0.43 us
    pallas_call x1 -> x2, Pallas kernels: 20.5 us -> 9.35 us  [call(): pl.pallas_call(kernel, out_shape=out_shape, in_specs=[vmem] * len(operand...]
    ppermute x8 -> x5, starting transfers between devices: 15.2 us -> 6.65 us  [ring(): lax.ppermute(value, axis, [(i, (i + step) % size) for i in range(size)])]
    ppermute x1 -> x2, waiting for transfers between devices: 7.63 us -> 3.56 us  [swap_x(): return lax.ppermute(value, ('xh', 'xl', 'c'), pairs)]
    ppermute x8 -> x5, waiting for transfers between devices: 6.9 us -> 5.2 us  [ring(): lax.ppermute(value, axis, [(i, (i + step) % size) for i in range(size)])]
    concatenate x2 -> x4, other arithmetic: 1.44 us -> 0.04 us  [the longest x1 0.02 us: on_device(): two_top = ring(jnp.concatenate([plus[:TOP], tail]), 'y', 4, 3)]
    unnamed x6 -> x5, local copies, waits for them, and re-layouts: 1.55 us -> 0.16 us
    ppermute x3, waiting for transfers between devices: 0.01 us -> 1.17 us  [swap_cores(): return lax.ppermute(value, 'c', [(0, 1), (1, 0)])]
    ppermute x1 -> x2, starting transfers between devices: 2.36 us -> 2.78 us  [swap_x(): return lax.ppermute(value, ('xh', 'xl', 'c'), pairs)]
  transfers between devices with their start and end apart: 12 -> 10, of which waited for: 6 -> 4; matrix products, arithmetic and copies ran while one was open for 3% -> 3% of each run, Pallas kernels for 0% -> 7%
where the time goes in v3:
time: 68.5 us; the launch traced here: 68.3 us
  blocking collectives  35.9 us (52%)
  waiting for transfers between devices  9.94 us (15%)
  starting transfers between devices  9.43 us (14%)
  Pallas kernels  9.35 us (14%)
  other arithmetic  2.54 us (4%)
  between operations  0.76 us (1%)
    all_to_all x1, blocking collectives, on_device(): sums = lax.all_to_all(sums, 'z', 0, 0, tiled=True)  18 us
    all_to_all x1, blocking collectives, on_device(): sums = lax.all_to_all(sums, ('xh', 'y'), 0, 0, tiled=True)  17.8 us
    pallas_call x2, Pallas kernels, call(): pl.pallas_call(kernel, out_shape=out_shape, in_specs=[vmem] * len(operand...  9.35 us
    ppermute x5, starting transfers between devices, ring(): lax.ppermute(value, axis, [(i, (i + step) % size) for i in range(size)])  6.65 us
    ppermute x5, waiting for transfers between devices, ring(): lax.ppermute(value, axis, [(i, (i + step) % size) for i in range(size)])  5.2 us
    ppermute x2, waiting for transfers between devices, swap_x(): return lax.ppermute(value, ('xh', 'xl', 'c'), pairs)  3.56 us
    ppermute x2, starting transfers between devices, swap_x(): return lax.ppermute(value, ('xh', 'xl', 'c'), pairs)  2.78 us
    another operation x1, other arithmetic, prepare(): both = jnp.stack([inputs, out_grads])  1.72 us
  transfers between devices with their start and end apart: 10, of which 4 were waited for; matrix products, arithmetic and copies ran while one was open for 3% of the time, Pallas kernels for 7%

profile of v3, /device:TPU:2, one launch (start us, length us, event | category | flops | bytes accessed | tf_op | source)
XLA Modules:
  0.0 68.3 jit_solution(2511636612875090828)
XLA Ops:
  0.6 1.7 %collective-permute-start.2 = (bf16[144,1152]{1,0:T(8,128)(2,1)}, bf16[144,1152]{1,0:T(8,128)(2,1)S(1)}, u32[]{:S(2)}, u32[]{:S(2)}) collective-permute-start(bf16[144,1152]{1,0:T(8,128)(2,1)} %bitcast.12), channel_id=1, source_target_pairs={{0,4},{4,8},{8,12},{12,0},{1,5},{5,9},{9,13},{13,1},{2,6},{6,10},{... | collective-permute-start | bytes 995336 | tf_op jit(solution)/shard_map/ppermute | solution.py:19
  2.3 1.7 %collective-permute-start.1 = (bf16[144,1152]{1,0:T(8,128)(2,1)}, bf16[144,1152]{1,0:T(8,128)(2,1)S(1)}, u32[]{:S(2)}, u32[]{:S(2)}) collective-permute-start(bf16[144,1152]{1,0:T(8,128)(2,1)} %bitcast.13), channel_id=1, source_target_pairs={{0,12},{4,0},{8,4},{12,8},{1,13},{5,1},{9,5},{13,9},{2,14},{6,2},{... | collective-permute-start | bytes 995336 | tf_op jit(solution)/shard_map/ppermute | solution.py:19
  3.9 1.7 %pad_maximum_fusion = bf16[2,4,14,14,256]{4,1,3,2,0:T(4,128)(2,1)S(1)} fusion(bf16[1,4,14,14,256]{4,1,3,2,0:T(4,128)(2,1)} %bitcast.17, bf16[1,4,14,14,256]{4,1,3,2,0:T(4,128)(2,1)} %bitcast.18), kind=kLoop, calls=%fused_computation.1 | loop fusion | flops 401408 | bytes 1605632 | tf_op jit(solution)/shard_map/stack | solution.py:35
  5.7 0.1 copy.10
  5.8 0.0 copy-start.1
  5.8 0.0 copy-start
  5.8 0.1 pad.8.clone
  6.0 2.4 %collective-permute-start = (bf16[2,4,224,256]{3,2,1,0:T(8,128)(2,1)S(1)}, bf16[2,4,224,256]{3,2,1,0:T(8,128)(2,1)S(1)}, u32[]{:S(2)}, u32[]{:S(2)}) collective-permute-start(bf16[2,4,224,256]{3,2,1,0:T(8,128)(2,1)S(1)} %bitcast.9), channel_id=1, source_target_pairs={{0,2},{1,19},{2,0},{3,17},{16,18},{17,3},{18,16},{19,1},{4,6},{5,2... | collective-permute-start | bytes 2752520 | tf_op jit(solution)/shard_map/ppermute | solution.py:31
  8.3 0.0 copy-done.1
  8.3 0.0 collective-permute-start.3
  8.3 1.2 %collective-permute-done.3 = bf16[16,256]{1,0:T(8,128)(2,1)S(1)} collective-permute-done((bf16[16,256]{1,0:T(8,128)(2,1)S(1)}, bf16[16,256]{1,0:T(8,128)(2,1)S(1)}, u32[]{:S(2)}, u32[]{:S(2)}) %collective-permute-start.3) | collective-permute-done | bytes 8224 | tf_op jit(solution)/shard_map/ppermute | solution.py:23
  9.5 0.4 collective-permute-start.4
  9.9 0.0 collective-permute-start.9
  9.9 3.6 %collective-permute-done.4 = bf16[16,512]{1,0:T(8,128)(2,1)S(1)} collective-permute-done((bf16[16,512]{1,0:T(8,128)(2,1)S(1)}, bf16[16,512]{1,0:T(8,128)(2,1)S(1)}, u32[]{:S(2)}, u32[]{:S(2)}) %collective-permute-start.4) | collective-permute-done | bytes 16416 | tf_op jit(solution)/shard_map/ppermute | solution.py:31
  13.5 0.0 collective-permute-done.2.minus
  13.5 0.0 collective-permute-done.1.plus
  13.6 1.4 %collective-permute-start.5 = (bf16[96,1152]{1,0:T(8,128)(2,1)S(1)}, bf16[96,1152]{1,0:T(8,128)(2,1)S(1)}, u32[]{:S(2)}, u32[]{:S(2)}) collective-permute-start(bf16[96,1152]{1,0:T(8,128)(2,1)S(1)} %pad_maximum_fusion.1), channel_id=1, source_target_pairs={{0,12},{4,0},{8,4},{12,8},{1,13},{5,1},{9,5},{13,9},{2,14},{6,2},{... | collective-permute-start | bytes 663560 | tf_op jit(solution)/shard_map/ppermute | solution.py:19
  14.9 0.8 %collective-permute-start.6 = (bf16[80,1152]{1,0:T(8,128)(2,1)S(1)}, bf16[80,1152]{1,0:T(8,128)(2,1)S(1)}, u32[]{:S(2)}, u32[]{:S(2)}) collective-permute-start(bf16[80,1152]{1,0:T(8,128)(2,1)S(1)} %pad_maximum_fusion.2), channel_id=1, source_target_pairs={{0,4},{4,8},{8,12},{12,0},{1,5},{5,9},{9,13},{13,1},{2,6},{6,10},{... | collective-permute-start | bytes 552968 | tf_op jit(solution)/shard_map/ppermute | solution.py:19
  15.8 1.2 %collective-permute-start.7 = (bf16[16,1024]{1,0:T(8,128)(2,1)S(1)}, bf16[16,1024]{1,0:T(8,128)(2,1)S(1)}, u32[]{:S(2)}, u32[]{:S(2)}) collective-permute-start(bf16[16,1024]{1,0:T(8,128)(2,1)S(1)} %pad_maximum_fusion.3.u_here), channel_id=1, source_target_pairs={{0,8},{4,12},{8,0},{12,4},{1,9},{5,13},{9,1},{13,5},{2,10},{6,14},... | collective-permute-start | bytes 98312 | tf_op jit(solution)/shard_map/ppermute | solution.py:19
  16.9 4.4 %collective-permute-done.7.u_two = bf16[16,1024]{1,0:T(8,128)(2,1)S(1)} collective-permute-done((bf16[16,1024]{1,0:T(8,128)(2,1)S(1)}, bf16[16,1024]{1,0:T(8,128)(2,1)S(1)}, u32[]{:S(2)}, u32[]{:S(2)}) %collective-permute-start.7) | collective-permute-done | bytes 32800 | tf_op jit(solution)/shard_map/ppermute | solution.py:19
  21.3 0.8 %collective-permute-done.6.two_bottom = bf16[80,1152]{1,0:T(8,128)(2,1)S(1)} collective-permute-done((bf16[80,1152]{1,0:T(8,128)(2,1)S(1)}, bf16[80,1152]{1,0:T(8,128)(2,1)S(1)}, u32[]{:S(2)}, u32[]{:S(2)}) %collective-permute-start.6) | collective-permute-done | bytes 184352 | tf_op jit(solution)/shard_map/ppermute | solution.py:19
  22.1 0.0 collective-permute-done.5.two_top
  22.1 0.0 collective-permute-done.far
  22.1 0.0 collective-permute-start.8
  22.1 0.0 collective-permute-done.9.other
  22.1 0.0 copy-done
  22.2 4.8 %near_examples.1 = (f32[2,288,256]{2,1,0:T(8,128)S(1)}, f32[2,288,256]{2,1,0:T(8,128)S(1)}, bf16[2,288,1152]{2,1,0:T(8,128)(2,1)S(1)}, bf16[256,256]{1,0:T(8,128)(2,1)S(1)}) custom-call(bf16[2,4,224,256]{3,2,1,0:T(8,128)(2,1)S(1)} %bitcast.11, bf16[2,4,224,256]{3,2,1,0:T(8,128)(2,1)S(1)} %collective-permute-done.9.other, bf16[144,1152]{1,0:T(8,128)(2,1)S(1)} %bitcast.14, ...), custom_call_target="tpu_custom_call" | custom-call | flops 4000000000 | bytes 1000000 | tf_op jit(solution)/shard_map/near_examples/pallas_call | solution.py:138
  26.9 0.0 collective-permute-done.8.far_other
  27.0 4.6 %far_examples.1 = bf16[8,2,144,128]{3,2,1,0:T(8,128)(2,1)S(1)} custom-call(bf16[2,4,224,256]{3,2,1,0:T(8,128)(2,1)S(1)} %collective-permute-done.far, bf16[2,4,224,256]{3,2,1,0:T(8,128)(2,1)S(1)} %collective-permute-done.8.far_other, f32[2,288,256]{2,1,0:T(8,128)S(1)} %get-tuple-element.20.squares_in, f32[2,288,256]{2,1,0:T(8,128)S(1)} %get-tuple-element.21.linear_in, ...), custom_call_target="tpu_custom_call" | custom-call | flops 4000000000 | bytes 1000000 | tf_op jit(solution)/shard_map/far_examples/pallas_call | solution.py:138
  31.5 17.8 %all_to_all.14 = bf16[8,2,144,128]{3,2,1,0:T(8,128)(2,1)S(1)} all-to-all(bf16[8,2,144,128]{3,2,1,0:T(8,128)(2,1)S(1)} %far_examples.1), channel_id=1, replica_groups=mesh['z'=8,'xh'=2,'y'=4,'xl'=2,'c'=2] {'xh','y'}, dimensions={0} | all-to-all | bytes 1179648 | tf_op jit(solution)/shard_map/all_to_all | solution.py:194
  49.3 0.1 convert_reduce_fusion
  49.4 0.1 copy.9
  49.5 18.0 %all_to_all.15 = f32[8,16,288]{2,1,0:T(8,128)S(1)} all-to-all(f32[8,16,288]{2,1,0:T(8,128)S(1)} %bitcast.15), channel_id=1, replica_groups=mesh['z'=8,'xh'=2,'y'=4,'xl'=2,'c'=2] {'z'}, dimensions={0} | all-to-all | bytes 294912 | tf_op jit(solution)/shard_map/all_to_all | solution.py:196
  67.6 0.7 slice_multiply_fusion
  (8 shorter events, 0.1 us)
Async XLA Ops:
  0.6 12.9 %collective-permute-start.2 = (bf16[144,1152]{1,0:T(8,128)(2,1)}, bf16[144,1152]{1,0:T(8,128)(2,1)S(1)}, u32[]{:S(2)}, u32[]{:S(2)}) collective-permute-start(bf16[144,1152]{1,0:T(8,128)(2,1)} %bitcast.12), channel_id=1, source_target_pairs={{0,4},{4,8},{8,12},{12,0},{1,5},{5,9},{9,13},{13,1},{2,6},{6,10},{... | collective-permute-start | bytes 995336 | tf_op jit(solution)/shard_map/ppermute | solution.py:19
  2.3 11.2 %collective-permute-start.1 = (bf16[144,1152]{1,0:T(8,128)(2,1)}, bf16[144,1152]{1,0:T(8,128)(2,1)S(1)}, u32[]{:S(2)}, u32[]{:S(2)}) collective-permute-start(bf16[144,1152]{1,0:T(8,128)(2,1)} %bitcast.13), channel_id=1, source_target_pairs={{0,12},{4,0},{8,4},{12,8},{1,13},{5,1},{9,5},{13,9},{2,14},{6,2},{... | collective-permute-start | bytes 995336 | tf_op jit(solution)/shard_map/ppermute | solution.py:19
  5.8 2.5 %copy-start.1 = (bf16[256,16]{0,1:T(8,128)(2,1)S(1)}, bf16[256,16]{0,1:T(8,128)(2,1)}, u32[]{:S(2)}) copy-start(bf16[256,16]{0,1:T(8,128)(2,1)} %param.7) | copy-start | bytes 24580
  5.8 16.3 %copy-start = (bf16[1152,144]{0,1:T(8,128)(2,1)S(1)}, bf16[1152,144]{0,1:T(8,128)(2,1)}, u32[]{:S(2)}) copy-start(bf16[1152,144]{0,1:T(8,128)(2,1)} %param.6) | copy-start | bytes 995332
  6.0 16.2 %collective-permute-start = (bf16[2,4,224,256]{3,2,1,0:T(8,128)(2,1)S(1)}, bf16[2,4,224,256]{3,2,1,0:T(8,128)(2,1)S(1)}, u32[]{:S(2)}, u32[]{:S(2)}) collective-permute-start(bf16[2,4,224,256]{3,2,1,0:T(8,128)(2,1)S(1)} %bitcast.9), channel_id=1, source_target_pairs={{0,2},{1,19},{2,0},{3,17},{16,18},{17,3},{18,16},{19,1},{4,6},{5,2... | collective-permute-start | bytes 2752520 | tf_op jit(solution)/shard_map/ppermute | solution.py:31
  8.3 1.2 %collective-permute-start.3 = (bf16[16,256]{1,0:T(8,128)(2,1)S(1)}, bf16[16,256]{1,0:T(8,128)(2,1)S(1)}, u32[]{:S(2)}, u32[]{:S(2)}) collective-permute-start(bf16[16,256]{1,0:T(8,128)(2,1)S(1)} %bitcast.19), channel_id=1, source_target_pairs={{0,1},{1,0},{2,3},{3,2},{4,5},{5,4},{6,7},{7,6},{8,9},{9,8},{10,11... | collective-permute-start | bytes 24584 | tf_op jit(solution)/shard_map/ppermute | solution.py:23
  9.5 4.0 %collective-permute-start.4 = (bf16[16,512]{1,0:T(8,128)(2,1)S(1)}, bf16[16,512]{1,0:T(8,128)(2,1)S(1)}, u32[]{:S(2)}, u32[]{:S(2)}) collective-permute-start(bf16[16,512]{1,0:T(8,128)(2,1)S(1)} %pad_maximum_fusion.4), channel_id=1, source_target_pairs={{0,18},{1,3},{2,16},{3,1},{16,2},{17,19},{18,0},{19,17},{4,22},{5,... | collective-permute-start | bytes 49160 | tf_op jit(solution)/shard_map/ppermute | solution.py:31
  9.9 12.2 %collective-permute-start.9 = (bf16[2,4,224,256]{3,2,1,0:T(8,128)(2,1)S(1)}, bf16[2,4,224,256]{3,2,1,0:T(8,128)(2,1)S(1)}, u32[]{:S(2)}, u32[]{:S(2)}) collective-permute-start(bf16[2,4,224,256]{3,2,1,0:T(8,128)(2,1)S(1)} %bitcast.10), channel_id=1, source_target_pairs={{0,1},{1,0},{2,3},{3,2},{4,5},{5,4},{6,7},{7,6},{8,9},{9,8},{10,11... | collective-permute-start | bytes 2752520 | tf_op jit(solution)/shard_map/ppermute | solution.py:23
  13.6 8.5 %collective-permute-start.5 = (bf16[96,1152]{1,0:T(8,128)(2,1)S(1)}, bf16[96,1152]{1,0:T(8,128)(2,1)S(1)}, u32[]{:S(2)}, u32[]{:S(2)}) collective-permute-start(bf16[96,1152]{1,0:T(8,128)(2,1)S(1)} %pad_maximum_fusion.1), channel_id=1, source_target_pairs={{0,12},{4,0},{8,4},{12,8},{1,13},{5,1},{9,5},{13,9},{2,14},{6,2},{... | collective-permute-start | bytes 663560 | tf_op jit(solution)/shard_map/ppermute | solution.py:19
  14.9 7.2 %collective-permute-start.6 = (bf16[80,1152]{1,0:T(8,128)(2,1)S(1)}, bf16[80,1152]{1,0:T(8,128)(2,1)S(1)}, u32[]{:S(2)}, u32[]{:S(2)}) collective-permute-start(bf16[80,1152]{1,0:T(8,128)(2,1)S(1)} %pad_maximum_fusion.2), channel_id=1, source_target_pairs={{0,4},{4,8},{8,12},{12,0},{1,5},{5,9},{9,13},{13,1},{2,6},{6,10},{... | collective-permute-start | bytes 552968 | tf_op jit(solution)/shard_map/ppermute | solution.py:19
  15.8 5.5 %collective-permute-start.7 = (bf16[16,1024]{1,0:T(8,128)(2,1)S(1)}, bf16[16,1024]{1,0:T(8,128)(2,1)S(1)}, u32[]{:S(2)}, u32[]{:S(2)}) collective-permute-start(bf16[16,1024]{1,0:T(8,128)(2,1)S(1)} %pad_maximum_fusion.3.u_here), channel_id=1, source_target_pairs={{0,8},{4,12},{8,0},{12,4},{1,9},{5,13},{9,1},{13,5},{2,10},{6,14},... | collective-permute-start | bytes 98312 | tf_op jit(solution)/shard_map/ppermute | solution.py:19
  22.1 4.8 %collective-permute-start.8 = (bf16[2,4,224,256]{3,2,1,0:T(8,128)(2,1)S(1)}, bf16[2,4,224,256]{3,2,1,0:T(8,128)(2,1)S(1)}, u32[]{:S(2)}, u32[]{:S(2)}) collective-permute-start(bf16[2,4,224,256]{3,2,1,0:T(8,128)(2,1)S(1)} %collective-permute-done.far), channel_id=1, source_target_pairs={{0,1},{1,0},{2,3},{3,2},{4,5},{5,4},{6,7},{7,6},{8,9},{9,8},{10,11... | collective-permute-start | bytes 2752520 | tf_op jit(solution)/shard_map/ppermute | solution.py:23

commit v4 on v3

--- a/solution.py
+++ b/solution.py
@@ -7,8 +7,8 @@
 from jax.experimental.pallas import tpu as pltpu
 from jax.sharding import Mesh, PartitionSpec as P
 
-AXES = ("z", "xh", "y", "xl", "c")
-SIZES = (8, 2, 4, 2, 2)
+AXES = ("zh", "zl", "xh", "y", "xl", "c")
+SIZES = (4, 2, 2, 4, 2, 2)
 BF16 = jnp.bfloat16
 F32 = jnp.float32
 CONTRACT_LAST = (((1,), (1,)), ((), ()))
@@ -38,8 +38,9 @@
 
 
 def clear(rows, grads):
-    rows[...] = jnp.zeros_like(rows)
-    grads[...] = jnp.zeros_like(grads)
+    rows[:, :, 0:16, :] = jnp.zeros((4, 3, 16, 256), BF16)
+    rows[:, :, 240:288, :] = jnp.zeros((4, 3, 48, 256), BF16)
+    grads[:, 224:256, :] = jnp.zeros((4, 32, 256), BF16)
 
 
 def add_group(group, basis, out_basis, squares_ref, linear_ref, rows, patches, grads):
@@ -192,9 +193,9 @@
     )
 
     sums = lax.all_to_all(sums, ("xh", "y"), 0, 0, tiled=True)
-    sums = jnp.sum(sums.astype(F32), axis=0).reshape(288, 128).T
-    sums = lax.all_to_all(sums, "z", 0, 0, tiled=True)
-    sums = jnp.sum(sums.reshape(8, 16, 288), axis=0)
+    sums = jnp.sum(sums.astype(F32), axis=0).reshape(288, 128).T.astype(BF16)
+    sums = lax.all_to_all(sums, ("zh", "zl"), 0, 0, tiled=True)
+    sums = jnp.sum(sums.reshape(8, 16, 288).astype(F32), axis=0)
     return (
         sums[:, :144] * (1.0 / (side * side * examples)),
         sums[:, 144:] * (1.0 / (side * math.sqrt(examples))),
@@ -203,11 +204,11 @@
 
 def solution(mesh):
     fine = Mesh(mesh.devices.reshape(SIZES), AXES)
-    every, columns = ("z", "xh", "y", "xl", "c"), ("y", "xl", "c")
+    every, columns, rows = AXES, AXES[3:], AXES[:3]
     return jax.shard_map(
         on_device,
         mesh=fine,
         in_specs=(P(every), P(every), P(None, columns), P(None, columns)),
-        out_specs=(P(("z", "xh"), columns), P(("z", "xh"), columns)),
+        out_specs=(P(rows, columns), P(rows, columns)),
         check_vma=False,
     )

time: 68.5 us -> 67.5 us (0.985)
  blocking collectives: 35.9 us -> 34.8 us
    all_to_all x1, blocking collectives: 18 us -> 17 us  [on_device(): sums = lax.all_to_all(sums, ('zh', 'zl'), 0, 0, tiled=True)]
where the time goes in v4:
time: 67.5 us; the launch traced here: 67.2 us
  blocking collectives  34.8 us (52%)
  waiting for transfers between devices  9.94 us (15%)
  starting transfers between devices  9.43 us (14%)
  Pallas kernels  9.35 us (14%)
  other arithmetic  2.54 us (4%)
  between operations  0.77 us (1%)
    all_to_all x1, blocking collectives, on_device(): sums = lax.all_to_all(sums, ('xh', 'y'), 0, 0, tiled=True)  17.8 us
    all_to_all x1, blocking collectives, on_device(): sums = lax.all_to_all(sums, ('zh', 'zl'), 0, 0, tiled=True)  17 us
    pallas_call x2, Pallas kernels, call(): pl.pallas_call(kernel, out_shape=out_shape, in_specs=[vmem] * len(operand...  9.35 us
    ppermute x5, starting transfers between devices, ring(): lax.ppermute(value, axis, [(i, (i + step) % size) for i in range(size)])  6.65 us
    ppermute x5, waiting for transfers between devices, ring(): lax.ppermute(value, axis, [(i, (i + step) % size) for i in range(size)])  5.2 us
    ppermute x2, waiting for transfers between devices, swap_x(): return lax.ppermute(value, ('xh', 'xl', 'c'), pairs)  3.56 us
    ppermute x2, starting transfers between devices, swap_x(): return lax.ppermute(value, ('xh', 'xl', 'c'), pairs)  2.78 us
    another operation x1, other arithmetic, prepare(): both = jnp.stack([inputs, out_grads])  1.72 us
  transfers between devices with their start and end apart: 10, of which 4 were waited for; matrix products, arithmetic and copies ran while one was open for 3% of the time, Pallas kernels for 7%

profile of v4, /device:TPU:2, one launch (start us, length us, event | category | flops | bytes accessed | tf_op | source)
XLA Modules:
  0.0 67.2 jit_solution(5684192004023632257)
XLA Ops:
  0.6 1.7 %collective-permute-start.2 = (bf16[144,1152]{1,0:T(8,128)(2,1)}, bf16[144,1152]{1,0:T(8,128)(2,1)S(1)}, u32[]{:S(2)}, u32[]{:S(2)}) collective-permute-start(bf16[144,1152]{1,0:T(8,128)(2,1)} %bitcast.12), channel_id=1, source_target_pairs={{0,4},{4,8},{8,12},{12,0},{1,5},{5,9},{9,13},{13,1},{2,6},{6,10},{... | collective-permute-start | bytes 995336 | tf_op jit(solution)/shard_map/ppermute | solution.py:19
  2.3 1.7 %collective-permute-start.1 = (bf16[144,1152]{1,0:T(8,128)(2,1)}, bf16[144,1152]{1,0:T(8,128)(2,1)S(1)}, u32[]{:S(2)}, u32[]{:S(2)}) collective-permute-start(bf16[144,1152]{1,0:T(8,128)(2,1)} %bitcast.13), channel_id=1, source_target_pairs={{0,12},{4,0},{8,4},{12,8},{1,13},{5,1},{9,5},{13,9},{2,14},{6,2},{... | collective-permute-start | bytes 995336 | tf_op jit(solution)/shard_map/ppermute | solution.py:19
  3.9 1.7 %pad_maximum_fusion = bf16[2,4,14,14,256]{4,1,3,2,0:T(4,128)(2,1)S(1)} fusion(bf16[1,4,14,14,256]{4,1,3,2,0:T(4,128)(2,1)} %bitcast.15, bf16[1,4,14,14,256]{4,1,3,2,0:T(4,128)(2,1)} %bitcast.16), kind=kLoop, calls=%fused_computation | loop fusion | flops 401408 | bytes 1605632 | tf_op jit(solution)/shard_map/stack | solution.py:35
  5.7 0.1 copy.10
  5.8 0.0 copy-start.1
  5.8 0.0 copy-start
  5.8 0.1 pad.8.clone
  6.0 2.4 %collective-permute-start = (bf16[2,4,224,256]{3,2,1,0:T(8,128)(2,1)S(1)}, bf16[2,4,224,256]{3,2,1,0:T(8,128)(2,1)S(1)}, u32[]{:S(2)}, u32[]{:S(2)}) collective-permute-start(bf16[2,4,224,256]{3,2,1,0:T(8,128)(2,1)S(1)} %bitcast.9), channel_id=1, source_target_pairs={{0,2},{1,19},{2,0},{3,17},{16,18},{17,3},{18,16},{19,1},{4,6},{5,2... | collective-permute-start | bytes 2752520 | tf_op jit(solution)/shard_map/ppermute | solution.py:31
  8.3 0.0 copy-done.1
  8.3 0.0 collective-permute-start.3
  8.3 1.2 %collective-permute-done.3 = bf16[16,256]{1,0:T(8,128)(2,1)S(1)} collective-permute-done((bf16[16,256]{1,0:T(8,128)(2,1)S(1)}, bf16[16,256]{1,0:T(8,128)(2,1)S(1)}, u32[]{:S(2)}, u32[]{:S(2)}) %collective-permute-start.3) | collective-permute-done | bytes 8224 | tf_op jit(solution)/shard_map/ppermute | solution.py:23
  9.5 0.4 collective-permute-start.4
  9.9 0.0 collective-permute-start.9
  9.9 3.6 %collective-permute-done.4 = bf16[16,512]{1,0:T(8,128)(2,1)S(1)} collective-permute-done((bf16[16,512]{1,0:T(8,128)(2,1)S(1)}, bf16[16,512]{1,0:T(8,128)(2,1)S(1)}, u32[]{:S(2)}, u32[]{:S(2)}) %collective-permute-start.4) | collective-permute-done | bytes 16416 | tf_op jit(solution)/shard_map/ppermute | solution.py:31
  13.5 0.0 collective-permute-done.2.minus
  13.5 0.0 collective-permute-done.1.plus
  13.6 1.4 %collective-permute-start.5 = (bf16[96,1152]{1,0:T(8,128)(2,1)S(1)}, bf16[96,1152]{1,0:T(8,128)(2,1)S(1)}, u32[]{:S(2)}, u32[]{:S(2)}) collective-permute-start(bf16[96,1152]{1,0:T(8,128)(2,1)S(1)} %pad_maximum_fusion.1), channel_id=1, source_target_pairs={{0,12},{4,0},{8,4},{12,8},{1,13},{5,1},{9,5},{13,9},{2,14},{6,2},{... | collective-permute-start | bytes 663560 | tf_op jit(solution)/shard_map/ppermute | solution.py:19
  14.9 0.8 %collective-permute-start.6 = (bf16[80,1152]{1,0:T(8,128)(2,1)S(1)}, bf16[80,1152]{1,0:T(8,128)(2,1)S(1)}, u32[]{:S(2)}, u32[]{:S(2)}) collective-permute-start(bf16[80,1152]{1,0:T(8,128)(2,1)S(1)} %pad_maximum_fusion.2), channel_id=1, source_target_pairs={{0,4},{4,8},{8,12},{12,0},{1,5},{5,9},{9,13},{13,1},{2,6},{6,10},{... | collective-permute-start | bytes 552968 | tf_op jit(solution)/shard_map/ppermute | solution.py:19
  15.8 1.2 %collective-permute-start.7 = (bf16[16,1024]{1,0:T(8,128)(2,1)S(1)}, bf16[16,1024]{1,0:T(8,128)(2,1)S(1)}, u32[]{:S(2)}, u32[]{:S(2)}) collective-permute-start(bf16[16,1024]{1,0:T(8,128)(2,1)S(1)} %pad_maximum_fusion.3.u_here), channel_id=1, source_target_pairs={{0,8},{4,12},{8,0},{12,4},{1,9},{5,13},{9,1},{13,5},{2,10},{6,14},... | collective-permute-start | bytes 98312 | tf_op jit(solution)/shard_map/ppermute | solution.py:19
  16.9 4.4 %collective-permute-done.7.u_two = bf16[16,1024]{1,0:T(8,128)(2,1)S(1)} collective-permute-done((bf16[16,1024]{1,0:T(8,128)(2,1)S(1)}, bf16[16,1024]{1,0:T(8,128)(2,1)S(1)}, u32[]{:S(2)}, u32[]{:S(2)}) %collective-permute-start.7) | collective-permute-done | bytes 32800 | tf_op jit(solution)/shard_map/ppermute | solution.py:19
  21.3 0.8 %collective-permute-done.6.two_bottom = bf16[80,1152]{1,0:T(8,128)(2,1)S(1)} collective-permute-done((bf16[80,1152]{1,0:T(8,128)(2,1)S(1)}, bf16[80,1152]{1,0:T(8,128)(2,1)S(1)}, u32[]{:S(2)}, u32[]{:S(2)}) %collective-permute-start.6) | collective-permute-done | bytes 184352 | tf_op jit(solution)/shard_map/ppermute | solution.py:19
  22.1 0.0 collective-permute-done.5.two_top
  22.1 0.0 collective-permute-done.far
  22.1 0.0 collective-permute-start.8
  22.1 0.0 collective-permute-done.9.other
  22.1 0.0 copy-done
  22.2 4.8 %near_examples.1 = (f32[2,288,256]{2,1,0:T(8,128)S(1)}, f32[2,288,256]{2,1,0:T(8,128)S(1)}, bf16[2,288,1152]{2,1,0:T(8,128)(2,1)S(1)}, bf16[256,256]{1,0:T(8,128)(2,1)S(1)}) custom-call(bf16[2,4,224,256]{3,2,1,0:T(8,128)(2,1)S(1)} %bitcast.11, bf16[2,4,224,256]{3,2,1,0:T(8,128)(2,1)S(1)} %collective-permute-done.9.other, bf16[144,1152]{1,0:T(8,128)(2,1)S(1)} %bitcast.14, ...), custom_call_target="tpu_custom_call" | custom-call | flops 4000000000 | bytes 1000000 | tf_op jit(solution)/shard_map/near_examples/pallas_call | solution.py:139
  26.9 0.0 collective-permute-done.8.far_other
  27.0 4.6 %far_examples.1 = bf16[8,2,144,128]{3,2,1,0:T(8,128)(2,1)S(1)} custom-call(bf16[2,4,224,256]{3,2,1,0:T(8,128)(2,1)S(1)} %collective-permute-done.far, bf16[2,4,224,256]{3,2,1,0:T(8,128)(2,1)S(1)} %collective-permute-done.8.far_other, f32[2,288,256]{2,1,0:T(8,128)S(1)} %get-tuple-element.20.squares_in, f32[2,288,256]{2,1,0:T(8,128)S(1)} %get-tuple-element.21.linear_in, ...), custom_call_target="tpu_custom_call" | custom-call | flops 4000000000 | bytes 1000000 | tf_op jit(solution)/shard_map/far_examples/pallas_call | solution.py:139
  31.5 17.8 %all_to_all.14 = bf16[8,2,144,128]{3,2,1,0:T(8,128)(2,1)S(1)} all-to-all(bf16[8,2,144,128]{3,2,1,0:T(8,128)(2,1)S(1)} %far_examples.1), channel_id=1, replica_groups=mesh['zh'=4,'zl'=2,'xh'=2,'y'=4,'xl'=2,'c'=2] {'xh','y'}, dimensions={0} | all-to-all | bytes 1179648 | tf_op jit(solution)/shard_map/all_to_all | solution.py:195
  49.3 0.1 reduce_sum.21
  49.4 0.1 copy.9
  49.6 17.0 %all_to_all.15 = bf16[8,16,288]{2,1,0:T(8,128)(2,1)S(1)} all-to-all(bf16[8,16,288]{2,1,0:T(8,128)(2,1)S(1)} %bitcast.17), channel_id=1, replica_groups=mesh['zh'=4,'zl'=2,'xh'=2,'y'=4,'xl'=2,'c'=2] {'zh','zl'}, dimensions={0} | all-to-all | bytes 147456 | tf_op jit(solution)/shard_map/all_to_all | solution.py:197
  66.6 0.7 %slice_multiply_fusion = (f32[16,144]{1,0:T(8,128)}, f32[16,144]{1,0:T(8,128)}) fusion(f32[16,288]{1,0:T(8,128)S(1)} %convert_reduce_fusion), kind=kLoop, calls=%fused_computation.5 | loop fusion | flops 4608 | bytes 36864 | tf_op jit(solution)/shard_map/mul | solution.py:201
  (8 shorter events, 0.1 us)
Async XLA Ops:
  0.6 12.9 %collective-permute-start.2 = (bf16[144,1152]{1,0:T(8,128)(2,1)}, bf16[144,1152]{1,0:T(8,128)(2,1)S(1)}, u32[]{:S(2)}, u32[]{:S(2)}) collective-permute-start(bf16[144,1152]{1,0:T(8,128)(2,1)} %bitcast.12), channel_id=1, source_target_pairs={{0,4},{4,8},{8,12},{12,0},{1,5},{5,9},{9,13},{13,1},{2,6},{6,10},{... | collective-permute-start | bytes 995336 | tf_op jit(solution)/shard_map/ppermute | solution.py:19
  2.3 11.2 %collective-permute-start.1 = (bf16[144,1152]{1,0:T(8,128)(2,1)}, bf16[144,1152]{1,0:T(8,128)(2,1)S(1)}, u32[]{:S(2)}, u32[]{:S(2)}) collective-permute-start(bf16[144,1152]{1,0:T(8,128)(2,1)} %bitcast.13), channel_id=1, source_target_pairs={{0,12},{4,0},{8,4},{12,8},{1,13},{5,1},{9,5},{13,9},{2,14},{6,2},{... | collective-permute-start | bytes 995336 | tf_op jit(solution)/shard_map/ppermute | solution.py:19
  5.8 2.5 %copy-start.1 = (bf16[256,16]{0,1:T(8,128)(2,1)S(1)}, bf16[256,16]{0,1:T(8,128)(2,1)}, u32[]{:S(2)}) copy-start(bf16[256,16]{0,1:T(8,128)(2,1)} %param.7) | copy-start | bytes 24580
  5.8 16.3 %copy-start = (bf16[1152,144]{0,1:T(8,128)(2,1)S(1)}, bf16[1152,144]{0,1:T(8,128)(2,1)}, u32[]{:S(2)}) copy-start(bf16[1152,144]{0,1:T(8,128)(2,1)} %param.6) | copy-start | bytes 995332
  6.0 16.2 %collective-permute-start = (bf16[2,4,224,256]{3,2,1,0:T(8,128)(2,1)S(1)}, bf16[2,4,224,256]{3,2,1,0:T(8,128)(2,1)S(1)}, u32[]{:S(2)}, u32[]{:S(2)}) collective-permute-start(bf16[2,4,224,256]{3,2,1,0:T(8,128)(2,1)S(1)} %bitcast.9), channel_id=1, source_target_pairs={{0,2},{1,19},{2,0},{3,17},{16,18},{17,3},{18,16},{19,1},{4,6},{5,2... | collective-permute-start | bytes 2752520 | tf_op jit(solution)/shard_map/ppermute | solution.py:31
  8.3 1.2 %collective-permute-start.3 = (bf16[16,256]{1,0:T(8,128)(2,1)S(1)}, bf16[16,256]{1,0:T(8,128)(2,1)S(1)}, u32[]{:S(2)}, u32[]{:S(2)}) collective-permute-start(bf16[16,256]{1,0:T(8,128)(2,1)S(1)} %bitcast.19), channel_id=1, source_target_pairs={{0,1},{1,0},{2,3},{3,2},{4,5},{5,4},{6,7},{7,6},{8,9},{9,8},{10,11... | collective-permute-start | bytes 24584 | tf_op jit(solution)/shard_map/ppermute | solution.py:23
  9.5 4.0 %collective-permute-start.4 = (bf16[16,512]{1,0:T(8,128)(2,1)S(1)}, bf16[16,512]{1,0:T(8,128)(2,1)S(1)}, u32[]{:S(2)}, u32[]{:S(2)}) collective-permute-start(bf16[16,512]{1,0:T(8,128)(2,1)S(1)} %pad_maximum_fusion.4), channel_id=1, source_target_pairs={{0,18},{1,3},{2,16},{3,1},{16,2},{17,19},{18,0},{19,17},{4,22},{5,... | collective-permute-start | bytes 49160 | tf_op jit(solution)/shard_map/ppermute | solution.py:31
  9.9 12.2 %collective-permute-start.9 = (bf16[2,4,224,256]{3,2,1,0:T(8,128)(2,1)S(1)}, bf16[2,4,224,256]{3,2,1,0:T(8,128)(2,1)S(1)}, u32[]{:S(2)}, u32[]{:S(2)}) collective-permute-start(bf16[2,4,224,256]{3,2,1,0:T(8,128)(2,1)S(1)} %bitcast.10), channel_id=1, source_target_pairs={{0,1},{1,0},{2,3},{3,2},{4,5},{5,4},{6,7},{7,6},{8,9},{9,8},{10,11... | collective-permute-start | bytes 2752520 | tf_op jit(solution)/shard_map/ppermute | solution.py:23
  13.6 8.5 %collective-permute-start.5 = (bf16[96,1152]{1,0:T(8,128)(2,1)S(1)}, bf16[96,1152]{1,0:T(8,128)(2,1)S(1)}, u32[]{:S(2)}, u32[]{:S(2)}) collective-permute-start(bf16[96,1152]{1,0:T(8,128)(2,1)S(1)} %pad_maximum_fusion.1), channel_id=1, source_target_pairs={{0,12},{4,0},{8,4},{12,8},{1,13},{5,1},{9,5},{13,9},{2,14},{6,2},{... | collective-permute-start | bytes 663560 | tf_op jit(solution)/shard_map/ppermute | solution.py:19
  14.9 7.2 %collective-permute-start.6 = (bf16[80,1152]{1,0:T(8,128)(2,1)S(1)}, bf16[80,1152]{1,0:T(8,128)(2,1)S(1)}, u32[]{:S(2)}, u32[]{:S(2)}) collective-permute-start(bf16[80,1152]{1,0:T(8,128)(2,1)S(1)} %pad_maximum_fusion.2), channel_id=1, source_target_pairs={{0,4},{4,8},{8,12},{12,0},{1,5},{5,9},{9,13},{13,1},{2,6},{6,10},{... | collective-permute-start | bytes 552968 | tf_op jit(solution)/shard_map/ppermute | solution.py:19
  15.8 5.5 %collective-permute-start.7 = (bf16[16,1024]{1,0:T(8,128)(2,1)S(1)}, bf16[16,1024]{1,0:T(8,128)(2,1)S(1)}, u32[]{:S(2)}, u32[]{:S(2)}) collective-permute-start(bf16[16,1024]{1,0:T(8,128)(2,1)S(1)} %pad_maximum_fusion.3.u_here), channel_id=1, source_target_pairs={{0,8},{4,12},{8,0},{12,4},{1,9},{5,13},{9,1},{13,5},{2,10},{6,14},... | collective-permute-start | bytes 98312 | tf_op jit(solution)/shard_map/ppermute | solution.py:19
  22.1 4.8 %collective-permute-start.8 = (bf16[2,4,224,256]{3,2,1,0:T(8,128)(2,1)S(1)}, bf16[2,4,224,256]{3,2,1,0:T(8,128)(2,1)S(1)}, u32[]{:S(2)}, u32[]{:S(2)}) collective-permute-start(bf16[2,4,224,256]{3,2,1,0:T(8,128)(2,1)S(1)} %collective-permute-done.far), channel_id=1, source_target_pairs={{0,1},{1,0},{2,3},{3,2},{4,5},{5,4},{6,7},{7,6},{8,9},{9,8},{10,11... | collective-permute-start | bytes 2752520 | tf_op jit(solution)/shard_map/ppermute | solution.py:23

commit v5 on v4

v5 whole, which is shorter than its diff:
```python
import math

import jax
import jax.numpy as jnp
from jax import lax
from jax.experimental import pallas as pl
from jax.experimental.pallas import tpu as pltpu
from jax.sharding import Mesh, PartitionSpec as P

AXES = ("zh", "zl", "xh", "y", "xl", "c")
SIZES = (4, 2, 2, 4, 2, 2)
BF16 = jnp.bfloat16
F32 = jnp.float32
CONTRACT_LAST = (((1,), (1,)), ((), ()))
TOP = 80


def ring(value, axis, size, step):
    return lax.ppermute(value, axis, [(i, (i + step) % size) for i in range(size)])


def swap_cores(value):
    return lax.ppermute(value, "c", [(0, 1), (1, 0)])


def swap_x(value, turn):
    def partner(x, core):
        return (x + 1 if (x + core + turn) % 2 == 0 else x - 1) % 4

    pairs = [(x * 2 + core, partner(x, core) * 2 + core) for x in range(4) for core in range(2)]
    return lax.ppermute(value, ("xh", "xl", "c"), pairs)


def prepare(inputs, out_grads):
    both = jnp.stack([inputs, out_grads])
    padded = jnp.pad(both, ((0, 0), (0, 0), (0, 0), (0, 2), (0, 0)))
    return padded.reshape(2, inputs.shape[0], 224, 256)


def take_patches(group, rows, patches, blocks):
    for n in range(4):
        feature = group[0, n].astype(F32)
        rows[n, 0, 16:240, :] = pltpu.roll(feature, 1, 0).astype(BF16)
        rows[n, 1, 16:240, :] = group[0, n]
        rows[n, 2, 16:240, :] = pltpu.roll(feature, 223, 0).astype(BF16)
        at = slice(256 * n, 256 * n + 256)
        for tap in range(9):
            ky, kx = tap // 3, tap % 3
            shifted = rows[n, kx, 16 * ky : 16 * ky + 256, :]
            if tap <= 4 and 0 in blocks:
                last = min(256 * tap + 256, 1152)
                patches[0, at, 256 * tap : last] = shifted[:, : last - 256 * tap]
            if tap >= 4 and 1 in blocks:
                first = max(256 * tap - 1152, 0)
                patches[1, at, first : 256 * tap - 896] = shifted[:, first + 1152 - 256 * tap :]


def clear_edges(rows):
    rows[:, :, 0:16, :] = jnp.zeros((4, 3, 16, 256), BF16)
    rows[:, :, 240:288, :] = jnp.zeros((4, 3, 48, 256), BF16)


def rotate(basis, patches):
    return lax.dot_general(
        basis, patches, CONTRACT_LAST, preferred_element_type=F32
    ).astype(BF16)


def rotate_grads(group, out_basis, grads):
    for n in range(4):
        grads[n, 0:224, :] = lax.dot_general(
            group[1, n], out_basis[...], CONTRACT_LAST, preferred_element_type=F32
        ).astype(BF16)


def add_moments(rotated, grads, squares_ref, linear_ref, block):
    squares, linear = squares_ref[block], linear_ref[block]
    for n in range(4):
        projected = jnp.dot(
            rotated[:, 256 * n : 256 * n + 256], grads[n], preferred_element_type=F32
        )
        squares = squares + projected * projected
        linear = linear + projected
    squares_ref[block] = squares
    linear_ref[block] = linear


def first_kernel(own, other, here, plus, minus, rotated, basis, rows, patches):
    y = lax.axis_index("y")
    odd = lax.rem(y, 2)
    basis[pl.ds(pl.multiple_of(odd * 144, 16), 144), :] = here[...]
    basis[pl.ds(pl.multiple_of(144 - odd * 144, 16), 144), :] = jnp.where(
        odd == 0, plus[...], minus[...]
    )
    clear_edges(rows)
    for block in range(2):

        @pl.when(y // 2 == block)
        def _(block=block):
            for at, group in enumerate((own, other)):
                take_patches(group, rows, patches, (block,))
                rotated[at] = rotate(basis[...], patches[block])


def near_kernel(
    own, other, rotated, first, plus, minus, two_top, two_bottom, u_here, u_two,
    squares_ref, linear_ref, basis, out_basis, rows, patches, grads,
):
    y, xl, core = lax.axis_index("y"), lax.axis_index("xl"), lax.axis_index("c")
    odd, own_block = lax.rem(y, 2), y // 2
    at = odd * 144
    basis[own_block] = first[...]
    second = basis.at[1 - own_block]
    second[pl.ds(pl.multiple_of(at, 16), TOP), :] = two_top[0:TOP, :]
    second[pl.ds(pl.multiple_of(at + TOP, 16), 144 - TOP), :] = two_bottom[0 : 144 - TOP, :]
    second[pl.ds(pl.multiple_of(144 - at, 16), 144), :] = jnp.where(
        odd == 0, minus[...], plus[...]
    )
    for dy, (source, row) in enumerate(
        ((u_here, 0), (two_top, TOP), (u_two, 0), (two_bottom, 144 - TOP))
    ):
        for piece in range(4):
            dc, dx = piece // 2, piece % 2
            owner = (lax.rem(y + dy, 4) * 2 + lax.rem(xl + dx, 2)) * 2 + lax.rem(core + dc, 2)
            place = owner % 2 * 128 + owner // 2 * 16
            out_basis[pl.ds(pl.multiple_of(place, 16), 16), :] = source[
                row : row + 16, 256 * piece : 256 * piece + 256
            ]
    clear_edges(rows)
    grads[:, 224:256, :] = jnp.zeros((4, 32, 256), BF16)
    squares_ref[...] = jnp.zeros_like(squares_ref)
    linear_ref[...] = jnp.zeros_like(linear_ref)
    for block in range(2):

        @pl.when(own_block == block)
        def _(block=block):
            for n, group in enumerate((own, other)):
                take_patches(group, rows, patches, (1 - block,))
                rotate_grads(group, out_basis, grads)
                add_moments(rotated[n], grads, squares_ref, linear_ref, block)
                add_moments(
                    rotate(basis[1 - block], patches[1 - block]),
                    grads, squares_ref, linear_ref, 1 - block,
                )


def far_kernel(
    far, far_other, squares_in, linear_in, basis, out_basis,
    sums, squares_ref, linear_ref, rows, patches, grads,
):
    clear_edges(rows)
    grads[:, 224:256, :] = jnp.zeros((4, 32, 256), BF16)
    squares_ref[...] = squares_in[...]
    linear_ref[...] = linear_in[...]
    for group in (far, far_other):
        take_patches(group, rows, patches, (0, 1))
        rotate_grads(group, out_basis, grads)
        for block in range(2):
            add_moments(
                rotate(basis[block], patches[block]), grads, squares_ref, linear_ref, block
            )
    for owner in range(4):
        at = slice(144 * (owner % 2), 144 * (owner % 2) + 144)
        for half in range(2):
            lanes = slice(128 * half, 128 * half + 128)
            sums[4 * half + owner, 0] = squares_ref[owner // 2, at, lanes].astype(BF16)
            sums[4 * half + owner, 1] = linear_ref[owner // 2, at, lanes].astype(BF16)


def call(kernel, name, flops, out_shape, scratch, *operands):
    vmem = pl.BlockSpec(memory_space=pltpu.VMEM)
    return pl.pallas_call(
        kernel,
        out_shape=out_shape,
        in_specs=[vmem] * len(operands),
        out_specs=jax.tree.map(lambda _: vmem, out_shape),
        scratch_shapes=scratch,
        compiler_params=pltpu.CompilerParams(vmem_limit_bytes=20 * 2**20),
        cost_estimate=pl.CostEstimate(flops=flops, bytes_accessed=10**6, transcendentals=0),
        name=name,
    )(*operands)


def forward_kernel(plus, minus, eigenvectors, top, bottom):
    top[0:TOP, :] = plus[0:TOP, :]
    bottom[0 : 144 - TOP, :] = minus[TOP:144, :]
    for target, row in ((top, TOP), (bottom, 144 - TOP)):
        target[row : row + 16, 0:1024] = eigenvectors[...]
        target[row : row + 16, 1024:1152] = jnp.zeros((16, 128), BF16)


def on_device(inputs, out_grads, patch_basis, output_basis):
    examples = inputs.shape[0] * math.prod(SIZES)
    side = inputs.shape[1]

    shard = patch_basis.T
    plus, minus = ring(shard, "y", 4, 3), ring(shard, "y", 4, 1)
    u0 = output_basis.T
    u1 = jnp.concatenate([u0, swap_x(u0, 0)], axis=1)
    u2 = jnp.concatenate([u1, swap_cores(u1)], axis=1)
    top, bottom = call(
        forward_kernel,
        "forward",
        20*10**9,
        tuple(jax.ShapeDtypeStruct((n + 16, 1152), BF16) for n in (TOP, 144 - TOP)),
        [],
        plus, minus, u2,
    )
    two_top, two_bottom = ring(top, "y", 4, 3), ring(bottom, "y", 4, 1)
    u_two = ring(u2, "y", 4, 2)
    own = prepare(inputs, out_grads)
    other = swap_cores(own)
    far = swap_x(own, 0)

    moment = jax.ShapeDtypeStruct((2, 288, 256), F32)
    rows, patches = pltpu.VMEM((4, 3, 288, 256), BF16), pltpu.VMEM((2, 1024, 1152), BF16)
    grads = pltpu.VMEM((4, 256, 256), BF16)
    rotated, first = call(
        first_kernel,
        "first_block_near",
        4*10**9,
        (
            jax.ShapeDtypeStruct((2, 288, 1024), BF16),
            jax.ShapeDtypeStruct((288, 1152), BF16),
        ),
        [rows, patches],
        own, other, shard, plus, minus,
    )
    far, two_top, two_bottom, u_two, rotated = lax.optimization_barrier(
        (far, two_top, two_bottom, u_two, rotated)
    )
    far_other = swap_cores(far)
    squares, linear, basis, out_basis = call(
        near_kernel,
        "near_examples",
        4 * 10**9,
        (
            moment,
            moment,
            jax.ShapeDtypeStruct((2, 288, 1152), BF16),
            jax.ShapeDtypeStruct((256, 256), BF16),
        ),
        [rows, patches, grads],
        own, other, rotated, first, plus, minus, two_top, two_bottom, u2, u_two,
    )
    sums = call(
        far_kernel,
        "far_examples",
        4 * 10**9,
        jax.ShapeDtypeStruct((8, 2, 144, 128), BF16),
        [pltpu.VMEM((2, 288, 256), F32)] * 2 + [rows, patches, grads],
        far, far_other, squares, linear, basis, out_basis,
    )

    sums = lax.all_to_all(sums, ("xh", "y"), 0, 0, tiled=True)
    sums = jnp.sum(sums.astype(F32), axis=0).reshape(288, 128).T.astype(BF16)
    sums = lax.all_to_all(sums, ("zh", "zl"), 0, 0, tiled=True)
    sums = jnp.sum(sums.reshape(8, 16, 288).astype(F32), axis=0)
    return (
        sums[:, :144] * (1.0 / (side * side * examples)),
        sums[:, 144:] * (1.0 / (side * math.sqrt(examples))),
    )


def solution(mesh):
    fine = Mesh(mesh.devices.reshape(SIZES), AXES)
    every, columns, rows = AXES, AXES[3:], AXES[:3]
    return jax.shard_map(
        on_device,
        mesh=fine,
        in_specs=(P(every), P(every), P(None, columns), P(None, columns)),
        out_specs=(P(rows, columns), P(rows, columns)),
        check_vma=False,
    )
```

time: 67.5 us -> 66.5 us (0.985)
  waiting for transfers between devices: 9.94 us -> 5.87 us
  starting transfers between devices: 9.43 us -> 11.7 us
  Pallas kernels: 9.35 us -> 10.4 us
  blocking collectives: 34.8 us -> 34 us
    ppermute x2, waiting for transfers between devices: 3.56 us -> 1.79 us  [swap_x(): return lax.ppermute(value, ('xh', 'xl', 'c'), pairs)]
    ppermute x5, starting transfers between devices: 6.65 us -> 8.1 us  [ring(): lax.ppermute(value, axis, [(i, (i + step) % size) for i in range(size)])]
    ppermute x3, waiting for transfers between devices: 1.17 us -> 0.01 us  [swap_cores(): return lax.ppermute(value, 'c', [(0, 1), (1, 0)])]
    ppermute x5, waiting for transfers between devices: 5.2 us -> 4.08 us  [ring(): lax.ppermute(value, axis, [(i, (i + step) % size) for i in range(size)])]
    pallas_call x2 -> x4, Pallas kernels: 9.35 us -> 10.4 us  [call(): pl.pallas_call(kernel, out_shape=out_shape, in_specs=[vmem] * len(operand...]
    all_to_all x1, blocking collectives: 17.8 us -> 17 us  [on_device(): sums = lax.all_to_all(sums, ('xh', 'y'), 0, 0, tiled=True)]
  transfers between devices with their start and end apart: 10 -> 10, of which waited for: 4 -> 4; matrix products, arithmetic and copies ran while one was open for 3% -> 4% of each run, Pallas kernels for 7% -> 9%
where the time goes in v5:
time: 66.5 us; the launch traced here: 66.2 us
  blocking collectives  34 us (51%)
  starting transfers between devices  11.7 us (18%)
  Pallas kernels  10.4 us (16%)
  waiting for transfers between devices  5.87 us (9%)
  other arithmetic  3.2 us (5%)
  between operations  0.73 us (1%)
    all_to_all x1, blocking collectives, on_device(): sums = lax.all_to_all(sums, ('xh', 'y'), 0, 0, tiled=True)  17 us
    all_to_all x1, blocking collectives, on_device(): sums = lax.all_to_all(sums, ('zh', 'zl'), 0, 0, tiled=True)  17 us
    pallas_call x4, Pallas kernels, call(): pl.pallas_call(kernel, out_shape=out_shape, in_specs=[vmem] * len(operand...  10.4 us
    ppermute x5, starting transfers between devices, ring(): lax.ppermute(value, axis, [(i, (i + step) % size) for i in range(size)])  8.1 us
    ppermute x5, waiting for transfers between devices, ring(): lax.ppermute(value, axis, [(i, (i + step) % size) for i in range(size)])  4.08 us
    ppermute x2, starting transfers between devices, swap_x(): return lax.ppermute(value, ('xh', 'xl', 'c'), pairs)  2.98 us
    ppermute x2, waiting for transfers between devices, swap_x(): return lax.ppermute(value, ('xh', 'xl', 'c'), pairs)  1.79 us
    another operation x1, other arithmetic, prepare(): both = jnp.stack([inputs, out_grads])  1.72 us
  transfers between devices with their start and end apart: 10, of which 4 were waited for; matrix products, arithmetic and copies ran while one was open for 4% of the time, Pallas kernels for 9%

profile of v5, /device:TPU:2, one launch (start us, length us, event | category | flops | bytes accessed | tf_op | source)
XLA Modules:
  0.0 66.2 jit_solution(12760054418770071537)
XLA Ops:
  0.6 2.4 %collective-permute-start.3 = (bf16[16,256]{1,0:T(8,128)(2,1)}, bf16[16,256]{1,0:T(8,128)(2,1)S(1)}, u32[]{:S(2)}, u32[]{:S(2)}) collective-permute-start(bf16[16,256]{1,0:T(8,128)(2,1)} %bitcast.20), channel_id=1, source_target_pairs={{0,2},{1,19},{2,0},{3,17},{16,18},{17,3},{18,16},{19,1},{4,6},{5,2... | collective-permute-start | bytes 24584 | tf_op jit(solution)/shard_map/ppermute | solution.py:31
  3.0 0.0 collective-permute-start.2
  3.0 3.2 %collective-permute-start.1 = (bf16[144,1152]{1,0:T(8,128)(2,1)}, bf16[144,1152]{1,0:T(8,128)(2,1)S(1)}, u32[]{:S(2)}, u32[]{:S(2)}) collective-permute-start(bf16[144,1152]{1,0:T(8,128)(2,1)} %bitcast.14), channel_id=1, source_target_pairs={{0,12},{4,0},{8,4},{12,8},{1,13},{5,1},{9,5},{13,9},{2,14},{6,2},{... | collective-permute-start | bytes 995336 | tf_op jit(solution)/shard_map/ppermute | solution.py:19
  6.2 0.0 collective-permute-done.3
  6.2 0.7 %pad_maximum_fusion.2 = bf16[16,512]{1,0:T(8,128)(2,1)S(1)} fusion(bf16[16,256]{1,0:T(8,128)(2,1)S(1)} %collective-permute-done.3, bf16[16,256]{1,0:T(8,128)(2,1)} %bitcast.21), kind=kLoop, calls=%fused_computation.5 | loop fusion | flops 32768 | bytes 32768 | tf_op jit(solution)/shard_map/concatenate | solution.py:199
  6.9 0.0 collective-permute-start.4
  6.9 1.7 %pad_maximum_fusion = bf16[2,4,14,14,256]{4,1,3,2,0:T(4,128)(2,1)S(1)} fusion(bf16[1,4,14,14,256]{4,1,3,2,0:T(4,128)(2,1)} %bitcast.16, bf16[1,4,14,14,256]{4,1,3,2,0:T(4,128)(2,1)} %bitcast.17), kind=kLoop, calls=%fused_computation | loop fusion | flops 401408 | bytes 1605632 | tf_op jit(solution)/shard_map/stack | solution.py:35
  8.6 0.1 copy.10
  8.8 0.0 copy-start.1
  8.8 0.1 pad.4.clone
  8.9 0.6 collective-permute-start.8
  9.5 0.6 collective-permute-start
  10.1 0.0 collective-permute-done.4
  10.1 0.0 copy-done.1
  10.2 0.0 copy-start
  10.2 1.5 %collective-permute-start.7 = (bf16[16,1024]{1,0:T(8,128)(2,1)S(1)}, bf16[16,1024]{1,0:T(8,128)(2,1)S(1)}, u32[]{:S(2)}, u32[]{:S(2)}) collective-permute-start(bf16[16,1024]{1,0:T(8,128)(2,1)S(1)} %pad_maximum_fusion.1.eigenvectors.u_here), channel_id=1, source_target_pairs={{0,8},{4,12},{8,0},{12,4},{1,9},{5,13},{9,1},{13,5},{2,10},{6,14},... | collective-permute-start | bytes 98312 | tf_op jit(solution)/shard_map/ppermute | solution.py:19
  11.7 1.2 %collective-permute-done.2.minus = bf16[144,1152]{1,0:T(8,128)(2,1)S(1)} collective-permute-done((bf16[144,1152]{1,0:T(8,128)(2,1)}, bf16[144,1152]{1,0:T(8,128)(2,1)S(1)}, u32[]{:S(2)}, u32[]{:S(2)}) %collective-permute-start.2) | collective-permute-done | bytes 331808 | tf_op jit(solution)/shard_map/ppermute | solution.py:19
  12.9 0.0 collective-permute-done.1.plus
  13.0 1.7 %collective-permute-start.6 = (bf16[80,1152]{1,0:T(8,128)(2,1)S(1)}, bf16[80,1152]{1,0:T(8,128)(2,1)S(1)}, u32[]{:S(2)}, u32[]{:S(2)}) collective-permute-start(bf16[80,1152]{1,0:T(8,128)(2,1)S(1)} %get-tuple-element.16), channel_id=1, source_target_pairs={{0,4},{4,8},{8,12},{12,0},{1,5},{5,9},{9,13},{13,1},{2,6},{6,10},{... | collective-permute-start | bytes 552968 | tf_op jit(solution)/shard_map/ppermute | solution.py:19
  14.7 1.7 %collective-permute-start.5 = (bf16[96,1152]{1,0:T(8,128)(2,1)S(1)}, bf16[96,1152]{1,0:T(8,128)(2,1)S(1)}, u32[]{:S(2)}, u32[]{:S(2)}) collective-permute-start(bf16[96,1152]{1,0:T(8,128)(2,1)S(1)} %get-tuple-element.15), channel_id=1, source_target_pairs={{0,12},{4,0},{8,4},{12,8},{1,13},{5,1},{9,5},{13,9},{2,14},{6,2},{... | collective-permute-start | bytes 663560 | tf_op jit(solution)/shard_map/ppermute | solution.py:19
  16.3 0.0 collective-permute-done.8.other
  16.3 0.0 copy-done
  16.3 2.0 %first_block_near.1 = (bf16[2,288,1024]{2,1,0:T(8,128)(2,1)S(1)}, bf16[288,1152]{1,0:T(8,128)(2,1)S(1)}) custom-call(bf16[2,4,224,256]{3,2,1,0:T(8,128)(2,1)S(1)} %bitcast.11, bf16[2,4,224,256]{3,2,1,0:T(8,128)(2,1)S(1)} %collective-permute-done.8.other, bf16[144,1152]{1,0:T(8,128)(2,1)S(1)} %bitcast.15, bf16[144,1152]{1,0:T(8,128)(2,1)S(1)} %collective-permute-done.1.plus, ...), custom_call_target="tpu_custom_call" | custom-call | flops 4000000000 | bytes 1000000 | tf_op jit(solution)/shard_map/first_block_near/pallas_call | solution.py:172
  18.3 0.0 collective-permute-done.7.u_two
  18.3 1.8 %collective-permute-done.6.two_bottom = bf16[80,1152]{1,0:T(8,128)(2,1)S(1)} collective-permute-done((bf16[80,1152]{1,0:T(8,128)(2,1)S(1)}, bf16[80,1152]{1,0:T(8,128)(2,1)S(1)}, u32[]{:S(2)}, u32[]{:S(2)}) %collective-permute-start.6) | collective-permute-done | bytes 184352 | tf_op jit(solution)/shard_map/ppermute | solution.py:19
  20.1 1.0 %collective-permute-done.5.two_top = bf16[96,1152]{1,0:T(8,128)(2,1)S(1)} collective-permute-done((bf16[96,1152]{1,0:T(8,128)(2,1)S(1)}, bf16[96,1152]{1,0:T(8,128)(2,1)S(1)}, u32[]{:S(2)}, u32[]{:S(2)}) %collective-permute-start.5) | collective-permute-done | bytes 221216 | tf_op jit(solution)/shard_map/ppermute | solution.py:19
  21.1 1.8 %collective-permute-done.far = bf16[2,4,224,256]{3,2,1,0:T(8,128)(2,1)S(1)} collective-permute-done((bf16[2,4,224,256]{3,2,1,0:T(8,128)(2,1)S(1)}, bf16[2,4,224,256]{3,2,1,0:T(8,128)(2,1)S(1)}, u32[]{:S(2)}, u32[]{:S(2)}) %collective-permute-start) | collective-permute-done | bytes 917536 | tf_op jit(solution)/shard_map/ppermute | solution.py:31
  22.9 0.0 collective-permute-start.9
  22.9 3.8 %near_examples.1 = (f32[2,288,256]{2,1,0:T(8,128)S(1)}, f32[2,288,256]{2,1,0:T(8,128)S(1)}, bf16[2,288,1152]{2,1,0:T(8,128)(2,1)S(1)}, bf16[256,256]{1,0:T(8,128)(2,1)S(1)}) custom-call(bf16[2,4,224,256]{3,2,1,0:T(8,128)(2,1)S(1)} %bitcast.12, bf16[2,4,224,256]{3,2,1,0:T(8,128)(2,1)S(1)} %collective-permute-done.8.other, ...), custom_call_target="tpu_custom_call" | custom-call | flops 4000000000 | bytes 1000000 | tf_op jit(solution)/shard_map/near_examples/pallas_call | solution.py:172
  26.7 0.0 collective-permute-done.9.far_other
  26.7 4.6 %far_examples.1 = bf16[8,2,144,128]{3,2,1,0:T(8,128)(2,1)S(1)} custom-call(bf16[2,4,224,256]{3,2,1,0:T(8,128)(2,1)S(1)} %collective-permute-done.far, bf16[2,4,224,256]{3,2,1,0:T(8,128)(2,1)S(1)} %collective-permute-done.9.far_other, f32[2,288,256]{2,1,0:T(8,128)S(1)} %get-tuple-element.24.squares_in, f32[2,288,256]{2,1,0:T(8,128)S(1)} %get-tuple-element.25.linear_in, ...), custom_call_target="tpu_custom_call" | custom-call | flops 4000000000 | bytes 1000000 | tf_op jit(solution)/shard_map/far_examples/pallas_call | solution.py:172
  31.3 17.0 %all_to_all.14 = bf16[8,2,144,128]{3,2,1,0:T(8,128)(2,1)S(1)} all-to-all(bf16[8,2,144,128]{3,2,1,0:T(8,128)(2,1)S(1)} %far_examples.1), channel_id=1, replica_groups=mesh['zh'=4,'zl'=2,'xh'=2,'y'=4,'xl'=2,'c'=2] {'xh','y'}, dimensions={0} | all-to-all | bytes 1179648 | tf_op jit(solution)/shard_map/all_to_all | solution.py:255
  48.3 0.1 reduce_sum.21
  48.4 0.1 copy.9
  48.5 17.0 %all_to_all.15 = bf16[8,16,288]{2,1,0:T(8,128)(2,1)S(1)} all-to-all(bf16[8,16,288]{2,1,0:T(8,128)(2,1)S(1)} %bitcast.18), channel_id=1, replica_groups=mesh['zh'=4,'zl'=2,'xh'=2,'y'=4,'xl'=2,'c'=2] {'zh','zl'}, dimensions={0} | all-to-all | bytes 147456 | tf_op jit(solution)/shard_map/all_to_all | solution.py:257
  65.5 0.7 %slice_multiply_fusion = (f32[16,144]{1,0:T(8,128)}, f32[16,144]{1,0:T(8,128)}) fusion(f32[16,288]{1,0:T(8,128)S(1)} %convert_reduce_fusion), kind=kLoop, calls=%fused_computation.3 | loop fusion | flops 4608 | bytes 36864 | tf_op jit(solution)/shard_map/mul | solution.py:261
  (3 shorter events, 0.1 us)
Async XLA Ops:
  0.6 5.6 %collective-permute-start.3 = (bf16[16,256]{1,0:T(8,128)(2,1)}, bf16[16,256]{1,0:T(8,128)(2,1)S(1)}, u32[]{:S(2)}, u32[]{:S(2)}) collective-permute-start(bf16[16,256]{1,0:T(8,128)(2,1)} %bitcast.20), channel_id=1, source_target_pairs={{0,2},{1,19},{2,0},{3,17},{16,18},{17,3},{18,16},{19,1},{4,6},{5,2... | collective-permute-start | bytes 24584 | tf_op jit(solution)/shard_map/ppermute | solution.py:31
  3.0 10.0 %collective-permute-start.2 = (bf16[144,1152]{1,0:T(8,128)(2,1)}, bf16[144,1152]{1,0:T(8,128)(2,1)S(1)}, u32[]{:S(2)}, u32[]{:S(2)}) collective-permute-start(bf16[144,1152]{1,0:T(8,128)(2,1)} %bitcast.13), channel_id=1, source_target_pairs={{0,4},{4,8},{8,12},{12,0},{1,5},{5,9},{9,13},{13,1},{2,6},{6,10},{... | collective-permute-start | bytes 995336 | tf_op jit(solution)/shard_map/ppermute | solution.py:19
  3.0 10.0 %collective-permute-start.1 = (bf16[144,1152]{1,0:T(8,128)(2,1)}, bf16[144,1152]{1,0:T(8,128)(2,1)S(1)}, u32[]{:S(2)}, u32[]{:S(2)}) collective-permute-start(bf16[144,1152]{1,0:T(8,128)(2,1)} %bitcast.14), channel_id=1, source_target_pairs={{0,12},{4,0},{8,4},{12,8},{1,13},{5,1},{9,5},{13,9},{2,14},{6,2},{... | collective-permute-start | bytes 995336 | tf_op jit(solution)/shard_map/ppermute | solution.py:19
  6.9 3.2 %collective-permute-start.4 = (bf16[16,512]{1,0:T(8,128)(2,1)S(1)}, bf16[16,512]{1,0:T(8,128)(2,1)S(1)}, u32[]{:S(2)}, u32[]{:S(2)}) collective-permute-start(bf16[16,512]{1,0:T(8,128)(2,1)S(1)} %pad_maximum_fusion.2), channel_id=1, source_target_pairs={{0,1},{1,0},{2,3},{3,2},{4,5},{5,4},{6,7},{7,6},{8,9},{9,8},{10,11... | collective-permute-start | bytes 49160 | tf_op jit(solution)/shard_map/ppermute | solution.py:23
  8.8 1.3 %copy-start.1 = (bf16[256,16]{0,1:T(8,128)(2,1)S(1)}, bf16[256,16]{0,1:T(8,128)(2,1)}, u32[]{:S(2)}) copy-start(bf16[256,16]{0,1:T(8,128)(2,1)} %param.7) | copy-start | bytes 24580
  8.9 7.4 %collective-permute-start.8 = (bf16[2,4,224,256]{3,2,1,0:T(8,128)(2,1)S(1)}, bf16[2,4,224,256]{3,2,1,0:T(8,128)(2,1)S(1)}, u32[]{:S(2)}, u32[]{:S(2)}) collective-permute-start(bf16[2,4,224,256]{3,2,1,0:T(8,128)(2,1)S(1)} %bitcast.9), channel_id=1, source_target_pairs={{0,1},{1,0},{2,3},{3,2},{4,5},{5,4},{6,7},{7,6},{8,9},{9,8},{10,11... | collective-permute-start | bytes 2752520 | tf_op jit(solution)/shard_map/ppermute | solution.py:23
  9.5 13.4 %collective-permute-start = (bf16[2,4,224,256]{3,2,1,0:T(8,128)(2,1)S(1)}, bf16[2,4,224,256]{3,2,1,0:T(8,128)(2,1)S(1)}, u32[]{:S(2)}, u32[]{:S(2)}) collective-permute-start(bf16[2,4,224,256]{3,2,1,0:T(8,128)(2,1)S(1)} %bitcast.10), channel_id=1, source_target_pairs={{0,2},{1,19},{2,0},{3,17},{16,18},{17,3},{18,16},{19,1},{4,6},{5,2... | collective-permute-start | bytes 2752520 | tf_op jit(solution)/shard_map/ppermute | solution.py:31
  10.2 6.2 %copy-start = (bf16[1152,144]{0,1:T(8,128)(2,1)S(1)}, bf16[1152,144]{0,1:T(8,128)(2,1)}, u32[]{:S(2)}) copy-start(bf16[1152,144]{0,1:T(8,128)(2,1)} %param.6) | copy-start | bytes 995332
  10.2 8.1 %collective-permute-start.7 = (bf16[16,1024]{1,0:T(8,128)(2,1)S(1)}, bf16[16,1024]{1,0:T(8,128)(2,1)S(1)}, u32[]{:S(2)}, u32[]{:S(2)}) collective-permute-start(bf16[16,1024]{1,0:T(8,128)(2,1)S(1)} %pad_maximum_fusion.1.eigenvectors.u_here), channel_id=1, source_target_pairs={{0,8},{4,12},{8,0},{12,4},{1,9},{5,13},{9,1},{13,5},{2,10},{6,14},... | collective-permute-start | bytes 98312 | tf_op jit(solution)/shard_map/ppermute | solution.py:19
  13.0 7.1 %collective-permute-start.6 = (bf16[80,1152]{1,0:T(8,128)(2,1)S(1)}, bf16[80,1152]{1,0:T(8,128)(2,1)S(1)}, u32[]{:S(2)}, u32[]{:S(2)}) collective-permute-start(bf16[80,1152]{1,0:T(8,128)(2,1)S(1)} %get-tuple-element.16), channel_id=1, source_target_pairs={{0,4},{4,8},{8,12},{12,0},{1,5},{5,9},{9,13},{13,1},{2,6},{6,10},{... | collective-permute-start | bytes 552968 | tf_op jit(solution)/shard_map/ppermute | solution.py:19
  14.7 6.5 %collective-permute-start.5 = (bf16[96,1152]{1,0:T(8,128)(2,1)S(1)}, bf16[96,1152]{1,0:T(8,128)(2,1)S(1)}, u32[]{:S(2)}, u32[]{:S(2)}) collective-permute-start(bf16[96,1152]{1,0:T(8,128)(2,1)S(1)} %get-tuple-element.15), channel_id=1, source_target_pairs={{0,12},{4,0},{8,4},{12,8},{1,13},{5,1},{9,5},{13,9},{2,14},{6,2},{... | collective-permute-start | bytes 663560 | tf_op jit(solution)/shard_map/ppermute | solution.py:19
  22.9 3.8 %collective-permute-start.9 = (bf16[2,4,224,256]{3,2,1,0:T(8,128)(2,1)S(1)}, bf16[2,4,224,256]{3,2,1,0:T(8,128)(2,1)S(1)}, u32[]{:S(2)}, u32[]{:S(2)}) collective-permute-start(bf16[2,4,224,256]{3,2,1,0:T(8,128)(2,1)S(1)} %collective-permute-done.far), channel_id=1, source_target_pairs={{0,1},{1,0},{2,3},{3,2},{4,5},{5,4},{6,7},{7,6},{8,9},{9,8},{10,11... | collective-permute-start | bytes 2752520 | tf_op jit(solution)/shard_map/ppermute | solution.py:23

commit v6 on v5

--- a/solution.py
+++ b/solution.py
@@ -196,19 +196,21 @@
     shard = patch_basis.T
     plus, minus = ring(shard, "y", 4, 3), ring(shard, "y", 4, 1)
     u0 = output_basis.T
-    u1 = jnp.concatenate([u0, swap_x(u0, 0)], axis=1)
+    own = prepare(inputs, out_grads)
+    u_x = swap_x(u0, 0)
+    _, u_x = lax.optimization_barrier((own, u_x))
+    u1 = jnp.concatenate([u0, u_x], axis=1)
     u2 = jnp.concatenate([u1, swap_cores(u1)], axis=1)
     top, bottom = call(
         forward_kernel,
         "forward",
-        20*10**9,
+        13*10**9,
         tuple(jax.ShapeDtypeStruct((n + 16, 1152), BF16) for n in (TOP, 144 - TOP)),
         [],
         plus, minus, u2,
     )
     two_top, two_bottom = ring(top, "y", 4, 3), ring(bottom, "y", 4, 1)
     u_two = ring(u2, "y", 4, 2)
-    own = prepare(inputs, out_grads)
     other = swap_cores(own)
     far = swap_x(own, 0)
 

time: 66.5 us -> 65.7 us (0.988)
  other arithmetic: 3.2 us -> 2.51 us
    ppermute x2, waiting for transfers between devices: 1.79 us -> 3.05 us  [swap_x(): return lax.ppermute(value, ('xh', 'xl', 'c'), pairs)]
    ppermute x5, starting transfers between devices: 8.1 us -> 7.16 us  [ring(): lax.ppermute(value, axis, [(i, (i + step) % size) for i in range(size)])]
    ppermute x5, waiting for transfers between devices: 4.08 us -> 3.17 us  [ring(): lax.ppermute(value, axis, [(i, (i + step) % size) for i in range(size)])]
    concatenate x1, other arithmetic: 0.7 us -> 0.01 us  [on_device(): u1 = jnp.concatenate([u0, u_x], axis=1)]
  transfers between devices with their start and end apart: 10 -> 10, of which waited for: 4 -> 3; matrix products, arithmetic and copies ran while one was open for 4% -> 3% of each run, Pallas kernels for 9% -> 9%
where the time goes in v6:
time: 65.7 us; the launch traced here: 65.5 us
  blocking collectives  33.5 us (51%)
  starting transfers between devices  11.2 us (17%)
  Pallas kernels  10.3 us (16%)
  waiting for transfers between devices  6.23 us (9%)
  other arithmetic  2.51 us (4%)
  local copies, waits for them, and re-layouts  0.95 us (1%)
  between operations  0.73 us (1%)
    all_to_all x1, blocking collectives, on_device(): sums = lax.all_to_all(sums, ('zh', 'zl'), 0, 0, tiled=True)  17 us
    all_to_all x1, blocking collectives, on_device(): sums = lax.all_to_all(sums, ('xh', 'y'), 0, 0, tiled=True)  16.5 us
    pallas_call x4, Pallas kernels, call(): pl.pallas_call(kernel, out_shape=out_shape, in_specs=[vmem] * len(operand...  10.3 us
    ppermute x5, starting transfers between devices, ring(): lax.ppermute(value, axis, [(i, (i + step) % size) for i in range(size)])  7.16 us
    ppermute x2, starting transfers between devices, swap_x(): return lax.ppermute(value, ('xh', 'xl', 'c'), pairs)  3.56 us
    ppermute x5, waiting for transfers between devices, ring(): lax.ppermute(value, axis, [(i, (i + step) % size) for i in range(size)])  3.17 us
    ppermute x2, waiting for transfers between devices, swap_x(): return lax.ppermute(value, ('xh', 'xl', 'c'), pairs)  3.05 us
    another operation x1, other arithmetic, prepare(): both = jnp.stack([inputs, out_grads])  1.72 us
  transfers between devices with their start and end apart: 10, of which 3 were waited for; matrix products, arithmetic and copies ran while one was open for 3% of the time, Pallas kernels for 9%

profile of v6, /device:TPU:2, one launch (start us, length us, event | category | flops | bytes accessed | tf_op | source)
XLA Modules:
  0.0 65.5 jit_solution(8134253430367109399)
XLA Ops:
  0.6 1.7 %collective-permute-start.2 = (bf16[144,1152]{1,0:T(8,128)(2,1)}, bf16[144,1152]{1,0:T(8,128)(2,1)S(1)}, u32[]{:S(2)}, u32[]{:S(2)}) collective-permute-start(bf16[144,1152]{1,0:T(8,128)(2,1)} %bitcast.13), channel_id=1, source_target_pairs={{0,4},{4,8},{8,12},{12,0},{1,5},{5,9},{9,13},{13,1},{2,6},{6,10},{... | collective-permute-start | bytes 995336 | tf_op jit(solution)/shard_map/ppermute | solution.py:19
  2.3 1.7 %collective-permute-start.1 = (bf16[144,1152]{1,0:T(8,128)(2,1)}, bf16[144,1152]{1,0:T(8,128)(2,1)S(1)}, u32[]{:S(2)}, u32[]{:S(2)}) collective-permute-start(bf16[144,1152]{1,0:T(8,128)(2,1)} %bitcast.14), channel_id=1, source_target_pairs={{0,12},{4,0},{8,4},{12,8},{1,13},{5,1},{9,5},{13,9},{2,14},{6,2},{... | collective-permute-start | bytes 995336 | tf_op jit(solution)/shard_map/ppermute | solution.py:19
  3.9 2.3 %collective-permute-start.3 = (bf16[16,256]{1,0:T(8,128)(2,1)}, bf16[16,256]{1,0:T(8,128)(2,1)S(1)}, u32[]{:S(2)}, u32[]{:S(2)}) collective-permute-start(bf16[16,256]{1,0:T(8,128)(2,1)} %bitcast.20), channel_id=1, source_target_pairs={{0,2},{1,19},{2,0},{3,17},{16,18},{17,3},{18,16},{19,1},{4,6},{5,2... | collective-permute-start | bytes 24584 | tf_op jit(solution)/shard_map/ppermute | solution.py:31
  6.2 1.7 %pad_maximum_fusion = bf16[2,4,14,14,256]{4,1,3,2,0:T(4,128)(2,1)S(1)} fusion(bf16[1,4,14,14,256]{4,1,3,2,0:T(4,128)(2,1)} %bitcast.16, bf16[1,4,14,14,256]{4,1,3,2,0:T(4,128)(2,1)} %bitcast.17), kind=kLoop, calls=%fused_computation | loop fusion | flops 401408 | bytes 1605632 | tf_op jit(solution)/shard_map/stack | solution.py:35
  7.9 0.1 copy.10
  8.1 0.0 copy-start.1
  8.1 0.1 pad.4.clone
  8.2 0.0 collective-permute-done.3
  8.2 0.6 copy-done.1
  8.8 0.0 collective-permute-start.4
  8.8 0.5 collective-permute-start.8
  9.3 1.3 %collective-permute-start = (bf16[2,4,224,256]{3,2,1,0:T(8,128)(2,1)S(1)}, bf16[2,4,224,256]{3,2,1,0:T(8,128)(2,1)S(1)}, u32[]{:S(2)}, u32[]{:S(2)}) collective-permute-start(bf16[2,4,224,256]{3,2,1,0:T(8,128)(2,1)S(1)} %bitcast.10), channel_id=1, source_target_pairs={{0,2},{1,19},{2,0},{3,17},{16,18},{17,3},{18,16},{19,1},{4,6},{5,2... | collective-permute-start | bytes 2752520 | tf_op jit(solution)/shard_map/ppermute | solution.py:31
  10.6 0.0 collective-permute-done.4
  10.6 0.0 copy-start
  10.6 0.5 collective-permute-start.7
  11.1 0.6 collective-permute-done.2.minus
  11.7 0.0 collective-permute-done.1.plus
  11.8 1.7 %collective-permute-start.6 = (bf16[80,1152]{1,0:T(8,128)(2,1)S(1)}, bf16[80,1152]{1,0:T(8,128)(2,1)S(1)}, u32[]{:S(2)}, u32[]{:S(2)}) collective-permute-start(bf16[80,1152]{1,0:T(8,128)(2,1)S(1)} %get-tuple-element.18), channel_id=1, source_target_pairs={{0,4},{4,8},{8,12},{12,0},{1,5},{5,9},{9,13},{13,1},{2,6},{6,10},{... | collective-permute-start | bytes 552968 | tf_op jit(solution)/shard_map/ppermute | solution.py:19
  13.4 1.7 %collective-permute-start.5 = (bf16[96,1152]{1,0:T(8,128)(2,1)S(1)}, bf16[96,1152]{1,0:T(8,128)(2,1)S(1)}, u32[]{:S(2)}, u32[]{:S(2)}) collective-permute-start(bf16[96,1152]{1,0:T(8,128)(2,1)S(1)} %get-tuple-element.17), channel_id=1, source_target_pairs={{0,12},{4,0},{8,4},{12,8},{1,13},{5,1},{9,5},{13,9},{2,14},{6,2},{... | collective-permute-start | bytes 663560 | tf_op jit(solution)/shard_map/ppermute | solution.py:19
  15.1 0.0 collective-permute-done.8.other
  15.1 0.0 copy-done
  15.1 2.0 %first_block_near.1 = (bf16[2,288,1024]{2,1,0:T(8,128)(2,1)S(1)}, bf16[288,1152]{1,0:T(8,128)(2,1)S(1)}) custom-call(bf16[2,4,224,256]{3,2,1,0:T(8,128)(2,1)S(1)} %bitcast.11, bf16[2,4,224,256]{3,2,1,0:T(8,128)(2,1)S(1)} %collective-permute-done.8.other, bf16[144,1152]{1,0:T(8,128)(2,1)S(1)} %bitcast.15, bf16[144,1152]{1,0:T(8,128)(2,1)S(1)} %collective-permute-done.1.plus, ...), custom_call_target="tpu_custom_call" | custom-call | flops 4000000000 | bytes 1000000 | tf_op jit(solution)/shard_map/first_block_near/pallas_call | solution.py:172
  17.1 0.0 collective-permute-done.7.u_two
  17.1 2.6 %collective-permute-done.6.two_bottom = bf16[80,1152]{1,0:T(8,128)(2,1)S(1)} collective-permute-done((bf16[80,1152]{1,0:T(8,128)(2,1)S(1)}, bf16[80,1152]{1,0:T(8,128)(2,1)S(1)}, u32[]{:S(2)}, u32[]{:S(2)}) %collective-permute-start.6) | collective-permute-done | bytes 184352 | tf_op jit(solution)/shard_map/ppermute | solution.py:19
  19.7 0.0 collective-permute-done.5.two_top
  19.7 3.0 %collective-permute-done.far = bf16[2,4,224,256]{3,2,1,0:T(8,128)(2,1)S(1)} collective-permute-done((bf16[2,4,224,256]{3,2,1,0:T(8,128)(2,1)S(1)}, bf16[2,4,224,256]{3,2,1,0:T(8,128)(2,1)S(1)}, u32[]{:S(2)}, u32[]{:S(2)}) %collective-permute-start) | collective-permute-done | bytes 917536 | tf_op jit(solution)/shard_map/ppermute | solution.py:31
  22.7 0.0 collective-permute-start.9
  22.7 3.8 %near_examples.1 = (f32[2,288,256]{2,1,0:T(8,128)S(1)}, f32[2,288,256]{2,1,0:T(8,128)S(1)}, bf16[2,288,1152]{2,1,0:T(8,128)(2,1)S(1)}, bf16[256,256]{1,0:T(8,128)(2,1)S(1)}) custom-call(bf16[2,4,224,256]{3,2,1,0:T(8,128)(2,1)S(1)} %bitcast.12, bf16[2,4,224,256]{3,2,1,0:T(8,128)(2,1)S(1)} %collective-permute-done.8.other, ...), custom_call_target="tpu_custom_call" | custom-call | flops 4000000000 | bytes 1000000 | tf_op jit(solution)/shard_map/near_examples/pallas_call | solution.py:172
  26.5 0.0 collective-permute-done.9.far_other
  26.5 4.6 %far_examples.1 = bf16[8,2,144,128]{3,2,1,0:T(8,128)(2,1)S(1)} custom-call(bf16[2,4,224,256]{3,2,1,0:T(8,128)(2,1)S(1)} %collective-permute-done.far, bf16[2,4,224,256]{3,2,1,0:T(8,128)(2,1)S(1)} %collective-permute-done.9.far_other, f32[2,288,256]{2,1,0:T(8,128)S(1)} %get-tuple-element.26.squares_in, f32[2,288,256]{2,1,0:T(8,128)S(1)} %get-tuple-element.27.linear_in, ...), custom_call_target="tpu_custom_call" | custom-call | flops 4000000000 | bytes 1000000 | tf_op jit(solution)/shard_map/far_examples/pallas_call | solution.py:172
  31.1 16.5 %all_to_all.14 = bf16[8,2,144,128]{3,2,1,0:T(8,128)(2,1)S(1)} all-to-all(bf16[8,2,144,128]{3,2,1,0:T(8,128)(2,1)S(1)} %far_examples.1), channel_id=1, replica_groups=mesh['zh'=4,'zl'=2,'xh'=2,'y'=4,'xl'=2,'c'=2] {'xh','y'}, dimensions={0} | all-to-all | bytes 1179648 | tf_op jit(solution)/shard_map/all_to_all | solution.py:257
  47.5 0.1 reduce_sum.21
  47.6 0.1 copy.9
  47.8 17.0 %all_to_all.15 = bf16[8,16,288]{2,1,0:T(8,128)(2,1)S(1)} all-to-all(bf16[8,16,288]{2,1,0:T(8,128)(2,1)S(1)} %bitcast.18), channel_id=1, replica_groups=mesh['zh'=4,'zl'=2,'xh'=2,'y'=4,'xl'=2,'c'=2] {'zh','zl'}, dimensions={0} | all-to-all | bytes 147456 | tf_op jit(solution)/shard_map/all_to_all | solution.py:259
  64.8 0.7 %slice_multiply_fusion = (f32[16,144]{1,0:T(8,128)}, f32[16,144]{1,0:T(8,128)}) fusion(f32[16,288]{1,0:T(8,128)S(1)} %convert_reduce_fusion), kind=kLoop, calls=%fused_computation.3 | loop fusion | flops 4608 | bytes 36864 | tf_op jit(solution)/shard_map/mul | solution.py:263
  (4 shorter events, 0.1 us)
Async XLA Ops:
  0.6 11.1 %collective-permute-start.2 = (bf16[144,1152]{1,0:T(8,128)(2,1)}, bf16[144,1152]{1,0:T(8,128)(2,1)S(1)}, u32[]{:S(2)}, u32[]{:S(2)}) collective-permute-start(bf16[144,1152]{1,0:T(8,128)(2,1)} %bitcast.13), channel_id=1, source_target_pairs={{0,4},{4,8},{8,12},{12,0},{1,5},{5,9},{9,13},{13,1},{2,6},{6,10},{... | collective-permute-start | bytes 995336 | tf_op jit(solution)/shard_map/ppermute | solution.py:19
  2.3 9.5 %collective-permute-start.1 = (bf16[144,1152]{1,0:T(8,128)(2,1)}, bf16[144,1152]{1,0:T(8,128)(2,1)S(1)}, u32[]{:S(2)}, u32[]{:S(2)}) collective-permute-start(bf16[144,1152]{1,0:T(8,128)(2,1)} %bitcast.14), channel_id=1, source_target_pairs={{0,12},{4,0},{8,4},{12,8},{1,13},{5,1},{9,5},{13,9},{2,14},{6,2},{... | collective-permute-start | bytes 995336 | tf_op jit(solution)/shard_map/ppermute | solution.py:19
  3.9 4.3 %collective-permute-start.3 = (bf16[16,256]{1,0:T(8,128)(2,1)}, bf16[16,256]{1,0:T(8,128)(2,1)S(1)}, u32[]{:S(2)}, u32[]{:S(2)}) collective-permute-start(bf16[16,256]{1,0:T(8,128)(2,1)} %bitcast.20), channel_id=1, source_target_pairs={{0,2},{1,19},{2,0},{3,17},{16,18},{17,3},{18,16},{19,1},{4,6},{5,2... | collective-permute-start | bytes 24584 | tf_op jit(solution)/shard_map/ppermute | solution.py:31
  8.1 0.7 %copy-start.1 = (bf16[256,16]{0,1:T(8,128)(2,1)S(1)}, bf16[256,16]{0,1:T(8,128)(2,1)}, u32[]{:S(2)}) copy-start(bf16[256,16]{0,1:T(8,128)(2,1)} %param.7) | copy-start | bytes 24580
  8.8 1.8 %collective-permute-start.4 = (bf16[16,512]{1,0:T(8,128)(2,1)S(1)}, bf16[16,512]{1,0:T(8,128)(2,1)S(1)}, u32[]{:S(2)}, u32[]{:S(2)}) collective-permute-start(bf16[16,512]{1,0:T(8,128)(2,1)S(1)} %pad_maximum_fusion.2), channel_id=1, source_target_pairs={{0,1},{1,0},{2,3},{3,2},{4,5},{5,4},{6,7},{7,6},{8,9},{9,8},{10,11... | collective-permute-start | bytes 49160 | tf_op jit(solution)/shard_map/ppermute | solution.py:23
  8.8 6.3 %collective-permute-start.8 = (bf16[2,4,224,256]{3,2,1,0:T(8,128)(2,1)S(1)}, bf16[2,4,224,256]{3,2,1,0:T(8,128)(2,1)S(1)}, u32[]{:S(2)}, u32[]{:S(2)}) collective-permute-start(bf16[2,4,224,256]{3,2,1,0:T(8,128)(2,1)S(1)} %bitcast.9), channel_id=1, source_target_pairs={{0,1},{1,0},{2,3},{3,2},{4,5},{5,4},{6,7},{7,6},{8,9},{9,8},{10,11... | collective-permute-start | bytes 2752520 | tf_op jit(solution)/shard_map/ppermute | solution.py:23
  9.3 13.4 %collective-permute-start = (bf16[2,4,224,256]{3,2,1,0:T(8,128)(2,1)S(1)}, bf16[2,4,224,256]{3,2,1,0:T(8,128)(2,1)S(1)}, u32[]{:S(2)}, u32[]{:S(2)}) collective-permute-start(bf16[2,4,224,256]{3,2,1,0:T(8,128)(2,1)S(1)} %bitcast.10), channel_id=1, source_target_pairs={{0,2},{1,19},{2,0},{3,17},{16,18},{17,3},{18,16},{19,1},{4,6},{5,2... | collective-permute-start | bytes 2752520 | tf_op jit(solution)/shard_map/ppermute | solution.py:31
  10.6 4.5 %copy-start = (bf16[1152,144]{0,1:T(8,128)(2,1)S(1)}, bf16[1152,144]{0,1:T(8,128)(2,1)}, u32[]{:S(2)}) copy-start(bf16[1152,144]{0,1:T(8,128)(2,1)} %param.6) | copy-start | bytes 995332
  10.6 6.5 %collective-permute-start.7 = (bf16[16,1024]{1,0:T(8,128)(2,1)S(1)}, bf16[16,1024]{1,0:T(8,128)(2,1)S(1)}, u32[]{:S(2)}, u32[]{:S(2)}) collective-permute-start(bf16[16,1024]{1,0:T(8,128)(2,1)S(1)} %pad_maximum_fusion.1.eigenvectors.u_here), channel_id=1, source_target_pairs={{0,8},{4,12},{8,0},{12,4},{1,9},{5,13},{9,1},{13,5},{2,10},{6,14},... | collective-permute-start | bytes 98312 | tf_op jit(solution)/shard_map/ppermute | solution.py:19
  11.8 7.9 %collective-permute-start.6 = (bf16[80,1152]{1,0:T(8,128)(2,1)S(1)}, bf16[80,1152]{1,0:T(8,128)(2,1)S(1)}, u32[]{:S(2)}, u32[]{:S(2)}) collective-permute-start(bf16[80,1152]{1,0:T(8,128)(2,1)S(1)} %get-tuple-element.18), channel_id=1, source_target_pairs={{0,4},{4,8},{8,12},{12,0},{1,5},{5,9},{9,13},{13,1},{2,6},{6,10},{... | collective-permute-start | bytes 552968 | tf_op jit(solution)/shard_map/ppermute | solution.py:19
  13.4 6.2 %collective-permute-start.5 = (bf16[96,1152]{1,0:T(8,128)(2,1)S(1)}, bf16[96,1152]{1,0:T(8,128)(2,1)S(1)}, u32[]{:S(2)}, u32[]{:S(2)}) collective-permute-start(bf16[96,1152]{1,0:T(8,128)(2,1)S(1)} %get-tuple-element.17), channel_id=1, source_target_pairs={{0,12},{4,0},{8,4},{12,8},{1,13},{5,1},{9,5},{13,9},{2,14},{6,2},{... | collective-permute-start | bytes 663560 | tf_op jit(solution)/shard_map/ppermute | solution.py:19
  22.7 3.8 %collective-permute-start.9 = (bf16[2,4,224,256]{3,2,1,0:T(8,128)(2,1)S(1)}, bf16[2,4,224,256]{3,2,1,0:T(8,128)(2,1)S(1)}, u32[]{:S(2)}, u32[]{:S(2)}) collective-permute-start(bf16[2,4,224,256]{3,2,1,0:T(8,128)(2,1)S(1)} %collective-permute-done.far), channel_id=1, source_target_pairs={{0,1},{1,0},{2,3},{3,2},{4,5},{5,4},{6,7},{7,6},{8,9},{9,8},{10,11... | collective-permute-start | bytes 2752520 | tf_op jit(solution)/shard_map/ppermute | solution.py:23

commit v7 on v6

--- a/solution.py
+++ b/solution.py
@@ -163,8 +163,8 @@
         at = slice(144 * (owner % 2), 144 * (owner % 2) + 144)
         for half in range(2):
             lanes = slice(128 * half, 128 * half + 128)
-            sums[4 * half + owner, 0] = squares_ref[owner // 2, at, lanes].astype(BF16)
-            sums[4 * half + owner, 1] = linear_ref[owner // 2, at, lanes].astype(BF16)
+            sums[2 * owner + half, 0] = squares_ref[owner // 2, at, lanes].astype(BF16)
+            sums[2 * owner + half, 1] = linear_ref[owner // 2, at, lanes].astype(BF16)
 
 
 def call(kernel, name, flops, out_shape, scratch, *operands):
@@ -211,7 +211,8 @@
     )
     two_top, two_bottom = ring(top, "y", 4, 3), ring(bottom, "y", 4, 1)
     u_two = ring(u2, "y", 4, 2)
-    other = swap_cores(own)
+    late, _ = lax.optimization_barrier((own, u2))
+    other = swap_cores(late)
     far = swap_x(own, 0)
 
     moment = jax.ShapeDtypeStruct((2, 288, 256), F32)
@@ -254,7 +255,7 @@
         far, far_other, squares, linear, basis, out_basis,
     )
 
-    sums = lax.all_to_all(sums, ("xh", "y"), 0, 0, tiled=True)
+    sums = lax.all_to_all(sums, ("y", "xh"), 0, 0, tiled=True)
     sums = jnp.sum(sums.astype(F32), axis=0).reshape(288, 128).T.astype(BF16)
     sums = lax.all_to_all(sums, ("zh", "zl"), 0, 0, tiled=True)
     sums = jnp.sum(sums.reshape(8, 16, 288).astype(F32), axis=0)

time: 65.7 us -> 65.3 us (level)
  waiting for transfers between devices: 6.23 us -> 5.52 us
  transfers between devices with their start and end apart: 10 -> 10, of which waited for: 3 -> 4; matrix products, arithmetic and copies ran while one was open for 3% -> 3% of each run, Pallas kernels for 9% -> 9%
where the time goes in v7:
time: 65.3 us; the launch traced here: 65 us
  blocking collectives  33.5 us (51%)
  starting transfers between devices  11.4 us (17%)
  Pallas kernels  10.3 us (16%)
  waiting for transfers between devices  5.52 us (8%)
  other arithmetic  2.51 us (4%)
  local copies, waits for them, and re-layouts  0.95 us (1%)
  between operations  0.73 us (1%)
    all_to_all x1, blocking collectives, on_device(): sums = lax.all_to_all(sums, ('zh', 'zl'), 0, 0, tiled=True)  17 us
    all_to_all x1, blocking collectives, on_device(): sums = lax.all_to_all(sums, ('y', 'xh'), 0, 0, tiled=True)  16.5 us
    pallas_call x4, Pallas kernels, call(): pl.pallas_call(kernel, out_shape=out_shape, in_specs=[vmem] * len(operand...  10.3 us
    ppermute x5, starting transfers between devices, ring(): lax.ppermute(value, axis, [(i, (i + step) % size) for i in range(size)])  7.43 us
    ppermute x2, starting transfers between devices, swap_x(): return lax.ppermute(value, ('xh', 'xl', 'c'), pairs)  3.65 us
    ppermute x5, waiting for transfers between devices, ring(): lax.ppermute(value, axis, [(i, (i + step) % size) for i in range(size)])  3.03 us
    ppermute x2, waiting for transfers between devices, swap_x(): return lax.ppermute(value, ('xh', 'xl', 'c'), pairs)  2.49 us
    another operation x1, other arithmetic, prepare(): both = jnp.stack([inputs, out_grads])  1.72 us
  transfers between devices with their start and end apart: 10, of which 4 were waited for; matrix products, arithmetic and copies ran while one was open for 3% of the time, Pallas kernels for 9%

profile of v7, /device:TPU:2, one launch (start us, length us, event | category | flops | bytes accessed | tf_op | source)
XLA Modules:
  0.0 65.0 jit_solution(15945833619585624889)
XLA Ops:
  0.6 1.7 %collective-permute-start.2 = (bf16[144,1152]{1,0:T(8,128)(2,1)}, bf16[144,1152]{1,0:T(8,128)(2,1)S(1)}, u32[]{:S(2)}, u32[]{:S(2)}) collective-permute-start(bf16[144,1152]{1,0:T(8,128)(2,1)} %bitcast.13), channel_id=1, source_target_pairs={{0,4},{4,8},{8,12},{12,0},{1,5},{5,9},{9,13},{13,1},{2,6},{6,10},{... | collective-permute-start | bytes 995336 | tf_op jit(solution)/shard_map/ppermute | solution.py:19
  2.3 1.7 %collective-permute-start.1 = (bf16[144,1152]{1,0:T(8,128)(2,1)}, bf16[144,1152]{1,0:T(8,128)(2,1)S(1)}, u32[]{:S(2)}, u32[]{:S(2)}) collective-permute-start(bf16[144,1152]{1,0:T(8,128)(2,1)} %bitcast.14), channel_id=1, source_target_pairs={{0,12},{4,0},{8,4},{12,8},{1,13},{5,1},{9,5},{13,9},{2,14},{6,2},{... | collective-permute-start | bytes 995336 | tf_op jit(solution)/shard_map/ppermute | solution.py:19
  3.9 2.3 %collective-permute-start.3 = (bf16[16,256]{1,0:T(8,128)(2,1)}, bf16[16,256]{1,0:T(8,128)(2,1)S(1)}, u32[]{:S(2)}, u32[]{:S(2)}) collective-permute-start(bf16[16,256]{1,0:T(8,128)(2,1)} %bitcast.20), channel_id=1, source_target_pairs={{0,2},{1,19},{2,0},{3,17},{16,18},{17,3},{18,16},{19,1},{4,6},{5,2... | collective-permute-start | bytes 24584 | tf_op jit(solution)/shard_map/ppermute | solution.py:31
  6.2 1.7 %pad_maximum_fusion = bf16[2,4,14,14,256]{4,1,3,2,0:T(4,128)(2,1)S(1)} fusion(bf16[1,4,14,14,256]{4,1,3,2,0:T(4,128)(2,1)} %bitcast.16, bf16[1,4,14,14,256]{4,1,3,2,0:T(4,128)(2,1)} %bitcast.17), kind=kLoop, calls=%fused_computation | loop fusion | flops 401408 | bytes 1605632 | tf_op jit(solution)/shard_map/stack | solution.py:35
  7.9 0.1 copy.10
  8.1 0.0 copy-start.1
  8.1 0.1 pad.4.clone
  8.2 0.0 collective-permute-done.3
  8.2 0.6 copy-done.1
  8.8 0.0 collective-permute-start.4
  8.8 1.4 %collective-permute-start = (bf16[2,4,224,256]{3,2,1,0:T(8,128)(2,1)S(1)}, bf16[2,4,224,256]{3,2,1,0:T(8,128)(2,1)S(1)}, u32[]{:S(2)}, u32[]{:S(2)}) collective-permute-start(bf16[2,4,224,256]{3,2,1,0:T(8,128)(2,1)S(1)} %bitcast.9), channel_id=1, source_target_pairs={{0,2},{1,19},{2,0},{3,17},{16,18},{17,3},{18,16},{19,1},{4,6},{5,2... | collective-permute-start | bytes 2752520 | tf_op jit(solution)/shard_map/ppermute | solution.py:31
  10.2 0.0 collective-permute-done.4
  10.2 0.0 copy-start
  10.2 0.8 %collective-permute-start.7 = (bf16[16,1024]{1,0:T(8,128)(2,1)S(1)}, bf16[16,1024]{1,0:T(8,128)(2,1)S(1)}, u32[]{:S(2)}, u32[]{:S(2)}) collective-permute-start(bf16[16,1024]{1,0:T(8,128)(2,1)S(1)} %pad_maximum_fusion.1.eigenvectors.u_here), channel_id=1, source_target_pairs={{0,8},{4,12},{8,0},{12,4},{1,9},{5,13},{9,1},{13,5},{2,10},{6,14},... | collective-permute-start | bytes 98312 | tf_op jit(solution)/shard_map/ppermute | solution.py:19
  11.0 0.3 collective-permute-start.8
  11.3 0.4 collective-permute-done.2.minus
  11.7 0.0 collective-permute-done.1.plus
  11.8 1.7 %collective-permute-start.6 = (bf16[80,1152]{1,0:T(8,128)(2,1)S(1)}, bf16[80,1152]{1,0:T(8,128)(2,1)S(1)}, u32[]{:S(2)}, u32[]{:S(2)}) collective-permute-start(bf16[80,1152]{1,0:T(8,128)(2,1)S(1)} %get-tuple-element.19), channel_id=1, source_target_pairs={{0,4},{4,8},{8,12},{12,0},{1,5},{5,9},{9,13},{13,1},{2,6},{6,10},{... | collective-permute-start | bytes 552968 | tf_op jit(solution)/shard_map/ppermute | solution.py:19
  13.4 1.7 %collective-permute-start.5 = (bf16[96,1152]{1,0:T(8,128)(2,1)S(1)}, bf16[96,1152]{1,0:T(8,128)(2,1)S(1)}, u32[]{:S(2)}, u32[]{:S(2)}) collective-permute-start(bf16[96,1152]{1,0:T(8,128)(2,1)S(1)} %get-tuple-element.18), channel_id=1, source_target_pairs={{0,12},{4,0},{8,4},{12,8},{1,13},{5,1},{9,5},{13,9},{2,14},{6,2},{... | collective-permute-start | bytes 663560 | tf_op jit(solution)/shard_map/ppermute | solution.py:19
  15.1 0.0 collective-permute-done.8.other
  15.1 0.0 copy-done
  15.1 2.0 %first_block_near.1 = (bf16[2,288,1024]{2,1,0:T(8,128)(2,1)S(1)}, bf16[288,1152]{1,0:T(8,128)(2,1)S(1)}) custom-call(bf16[2,4,224,256]{3,2,1,0:T(8,128)(2,1)S(1)} %bitcast.11, bf16[2,4,224,256]{3,2,1,0:T(8,128)(2,1)S(1)} %collective-permute-done.8.other, bf16[144,1152]{1,0:T(8,128)(2,1)S(1)} %bitcast.15, bf16[144,1152]{1,0:T(8,128)(2,1)S(1)} %collective-permute-done.1.plus, ...), custom_call_target="tpu_custom_call" | custom-call | flops 4000000000 | bytes 1000000 | tf_op jit(solution)/shard_map/first_block_near/pallas_call | solution.py:172
  17.1 0.0 collective-permute-done.7.u_two
  17.1 2.5 %collective-permute-done.6.two_bottom = bf16[80,1152]{1,0:T(8,128)(2,1)S(1)} collective-permute-done((bf16[80,1152]{1,0:T(8,128)(2,1)S(1)}, bf16[80,1152]{1,0:T(8,128)(2,1)S(1)}, u32[]{:S(2)}, u32[]{:S(2)}) %collective-permute-start.6) | collective-permute-done | bytes 184352 | tf_op jit(solution)/shard_map/ppermute | solution.py:19
  19.6 0.1 collective-permute-done.5.two_top
  19.7 2.5 %collective-permute-done.far = bf16[2,4,224,256]{3,2,1,0:T(8,128)(2,1)S(1)} collective-permute-done((bf16[2,4,224,256]{3,2,1,0:T(8,128)(2,1)S(1)}, bf16[2,4,224,256]{3,2,1,0:T(8,128)(2,1)S(1)}, u32[]{:S(2)}, u32[]{:S(2)}) %collective-permute-start) | collective-permute-done | bytes 917536 | tf_op jit(solution)/shard_map/ppermute | solution.py:31
  22.2 0.0 collective-permute-start.9
  22.2 3.8 %near_examples.1 = (f32[2,288,256]{2,1,0:T(8,128)S(1)}, f32[2,288,256]{2,1,0:T(8,128)S(1)}, bf16[2,288,1152]{2,1,0:T(8,128)(2,1)S(1)}, bf16[256,256]{1,0:T(8,128)(2,1)S(1)}) custom-call(bf16[2,4,224,256]{3,2,1,0:T(8,128)(2,1)S(1)} %bitcast.12, bf16[2,4,224,256]{3,2,1,0:T(8,128)(2,1)S(1)} %collective-permute-done.8.other, ...), custom_call_target="tpu_custom_call" | custom-call | flops 4000000000 | bytes 1000000 | tf_op jit(solution)/shard_map/near_examples/pallas_call | solution.py:172
  26.0 0.0 collective-permute-done.9.far_other
  26.0 4.6 %far_examples.1 = bf16[8,2,144,128]{3,2,1,0:T(8,128)(2,1)S(1)} custom-call(bf16[2,4,224,256]{3,2,1,0:T(8,128)(2,1)S(1)} %collective-permute-done.far, bf16[2,4,224,256]{3,2,1,0:T(8,128)(2,1)S(1)} %collective-permute-done.9.far_other, f32[2,288,256]{2,1,0:T(8,128)S(1)} %get-tuple-element.28.squares_in, f32[2,288,256]{2,1,0:T(8,128)S(1)} %get-tuple-element.29.linear_in, ...), custom_call_target="tpu_custom_call" | custom-call | flops 4000000000 | bytes 1000000 | tf_op jit(solution)/shard_map/far_examples/pallas_call | solution.py:172
  30.6 16.5 %all_to_all.14 = bf16[8,2,144,128]{3,2,1,0:T(8,128)(2,1)S(1)} all-to-all(bf16[8,2,144,128]{3,2,1,0:T(8,128)(2,1)S(1)} %far_examples.1), channel_id=1, replica_groups=mesh['zh'=4,'zl'=2,'xh'=2,'y'=4,'xl'=2,'c'=2] {'y','xh'}, dimensions={0} | all-to-all | bytes 1179648 | tf_op jit(solution)/shard_map/all_to_all | solution.py:258
  47.1 0.1 reduce_sum.21
  47.2 0.1 copy.9
  47.3 17.0 %all_to_all.15 = bf16[8,16,288]{2,1,0:T(8,128)(2,1)S(1)} all-to-all(bf16[8,16,288]{2,1,0:T(8,128)(2,1)S(1)} %bitcast.18), channel_id=1, replica_groups=mesh['zh'=4,'zl'=2,'xh'=2,'y'=4,'xl'=2,'c'=2] {'zh','zl'}, dimensions={0} | all-to-all | bytes 147456 | tf_op jit(solution)/shard_map/all_to_all | solution.py:260
  64.4 0.7 %slice_multiply_fusion = (f32[16,144]{1,0:T(8,128)}, f32[16,144]{1,0:T(8,128)}) fusion(f32[16,288]{1,0:T(8,128)S(1)} %convert_reduce_fusion), kind=kLoop, calls=%fused_computation.3 | loop fusion | flops 4608 | bytes 36864 | tf_op jit(solution)/shard_map/mul | solution.py:264
  (4 shorter events, 0.1 us)
Async XLA Ops:
  0.6 11.1 %collective-permute-start.2 = (bf16[144,1152]{1,0:T(8,128)(2,1)}, bf16[144,1152]{1,0:T(8,128)(2,1)S(1)}, u32[]{:S(2)}, u32[]{:S(2)}) collective-permute-start(bf16[144,1152]{1,0:T(8,128)(2,1)} %bitcast.13), channel_id=1, source_target_pairs={{0,4},{4,8},{8,12},{12,0},{1,5},{5,9},{9,13},{13,1},{2,6},{6,10},{... | collective-permute-start | bytes 995336 | tf_op jit(solution)/shard_map/ppermute | solution.py:19
  2.3 9.5 %collective-permute-start.1 = (bf16[144,1152]{1,0:T(8,128)(2,1)}, bf16[144,1152]{1,0:T(8,128)(2,1)S(1)}, u32[]{:S(2)}, u32[]{:S(2)}) collective-permute-start(bf16[144,1152]{1,0:T(8,128)(2,1)} %bitcast.14), channel_id=1, source_target_pairs={{0,12},{4,0},{8,4},{12,8},{1,13},{5,1},{9,5},{13,9},{2,14},{6,2},{... | collective-permute-start | bytes 995336 | tf_op jit(solution)/shard_map/ppermute | solution.py:19
  3.9 4.3 %collective-permute-start.3 = (bf16[16,256]{1,0:T(8,128)(2,1)}, bf16[16,256]{1,0:T(8,128)(2,1)S(1)}, u32[]{:S(2)}, u32[]{:S(2)}) collective-permute-start(bf16[16,256]{1,0:T(8,128)(2,1)} %bitcast.20), channel_id=1, source_target_pairs={{0,2},{1,19},{2,0},{3,17},{16,18},{17,3},{18,16},{19,1},{4,6},{5,2... | collective-permute-start | bytes 24584 | tf_op jit(solution)/shard_map/ppermute | solution.py:31
  8.1 0.7 %copy-start.1 = (bf16[256,16]{0,1:T(8,128)(2,1)S(1)}, bf16[256,16]{0,1:T(8,128)(2,1)}, u32[]{:S(2)}) copy-start(bf16[256,16]{0,1:T(8,128)(2,1)} %param.7) | copy-start | bytes 24580
  8.8 1.4 %collective-permute-start.4 = (bf16[16,512]{1,0:T(8,128)(2,1)S(1)}, bf16[16,512]{1,0:T(8,128)(2,1)S(1)}, u32[]{:S(2)}, u32[]{:S(2)}) collective-permute-start(bf16[16,512]{1,0:T(8,128)(2,1)S(1)} %pad_maximum_fusion.2), channel_id=1, source_target_pairs={{0,1},{1,0},{2,3},{3,2},{4,5},{5,4},{6,7},{7,6},{8,9},{9,8},{10,11... | collective-permute-start | bytes 49160 | tf_op jit(solution)/shard_map/ppermute | solution.py:23
  8.8 13.4 %collective-permute-start = (bf16[2,4,224,256]{3,2,1,0:T(8,128)(2,1)S(1)}, bf16[2,4,224,256]{3,2,1,0:T(8,128)(2,1)S(1)}, u32[]{:S(2)}, u32[]{:S(2)}) collective-permute-start(bf16[2,4,224,256]{3,2,1,0:T(8,128)(2,1)S(1)} %bitcast.9), channel_id=1, source_target_pairs={{0,2},{1,19},{2,0},{3,17},{16,18},{17,3},{18,16},{19,1},{4,6},{5,2... | collective-permute-start | bytes 2752520 | tf_op jit(solution)/shard_map/ppermute | solution.py:31
  10.2 4.9 %copy-start = (bf16[1152,144]{0,1:T(8,128)(2,1)S(1)}, bf16[1152,144]{0,1:T(8,128)(2,1)}, u32[]{:S(2)}) copy-start(bf16[1152,144]{0,1:T(8,128)(2,1)} %param.6) | copy-start | bytes 995332
  10.2 6.9 %collective-permute-start.7 = (bf16[16,1024]{1,0:T(8,128)(2,1)S(1)}, bf16[16,1024]{1,0:T(8,128)(2,1)S(1)}, u32[]{:S(2)}, u32[]{:S(2)}) collective-permute-start(bf16[16,1024]{1,0:T(8,128)(2,1)S(1)} %pad_maximum_fusion.1.eigenvectors.u_here), channel_id=1, source_target_pairs={{0,8},{4,12},{8,0},{12,4},{1,9},{5,13},{9,1},{13,5},{2,10},{6,14},... | collective-permute-start | bytes 98312 | tf_op jit(solution)/shard_map/ppermute | solution.py:19
  11.0 4.1 %collective-permute-start.8 = (bf16[2,4,224,256]{3,2,1,0:T(8,128)(2,1)S(1)}, bf16[2,4,224,256]{3,2,1,0:T(8,128)(2,1)S(1)}, u32[]{:S(2)}, u32[]{:S(2)}) collective-permute-start(bf16[2,4,224,256]{3,2,1,0:T(8,128)(2,1)S(1)} %bitcast.10), channel_id=1, source_target_pairs={{0,1},{1,0},{2,3},{3,2},{4,5},{5,4},{6,7},{7,6},{8,9},{9,8},{10,11... | collective-permute-start | bytes 2752520 | tf_op jit(solution)/shard_map/ppermute | solution.py:23
  11.8 7.9 %collective-permute-start.6 = (bf16[80,1152]{1,0:T(8,128)(2,1)S(1)}, bf16[80,1152]{1,0:T(8,128)(2,1)S(1)}, u32[]{:S(2)}, u32[]{:S(2)}) collective-permute-start(bf16[80,1152]{1,0:T(8,128)(2,1)S(1)} %get-tuple-element.19), channel_id=1, source_target_pairs={{0,4},{4,8},{8,12},{12,0},{1,5},{5,9},{9,13},{13,1},{2,6},{6,10},{... | collective-permute-start | bytes 552968 | tf_op jit(solution)/shard_map/ppermute | solution.py:19
  13.4 6.3 %collective-permute-start.5 = (bf16[96,1152]{1,0:T(8,128)(2,1)S(1)}, bf16[96,1152]{1,0:T(8,128)(2,1)S(1)}, u32[]{:S(2)}, u32[]{:S(2)}) collective-permute-start(bf16[96,1152]{1,0:T(8,128)(2,1)S(1)} %get-tuple-element.18), channel_id=1, source_target_pairs={{0,12},{4,0},{8,4},{12,8},{1,13},{5,1},{9,5},{13,9},{2,14},{6,2},{... | collective-permute-start | bytes 663560 | tf_op jit(solution)/shard_map/ppermute | solution.py:19
  22.2 3.8 %collective-permute-start.9 = (bf16[2,4,224,256]{3,2,1,0:T(8,128)(2,1)S(1)}, bf16[2,4,224,256]{3,2,1,0:T(8,128)(2,1)S(1)}, u32[]{:S(2)}, u32[]{:S(2)}) collective-permute-start(bf16[2,4,224,256]{3,2,1,0:T(8,128)(2,1)S(1)} %collective-permute-done.far), channel_id=1, source_target_pairs={{0,1},{1,0},{2,3},{3,2},{4,5},{5,4},{6,7},{7,6},{8,9},{9,8},{10,11... | collective-permute-start | bytes 2752520 | tf_op jit(solution)/shard_map/ppermute | solution.py:23

commit v8 on v7

--- a/solution.py
+++ b/solution.py
@@ -145,20 +145,24 @@
 
 
 def far_kernel(
-    far, far_other, squares_in, linear_in, basis, out_basis,
-    sums, squares_ref, linear_ref, rows, patches, grads,
+    far, squares_in, linear_in, basis, out_basis, squares_ref, linear_ref, rows, patches, grads
 ):
     clear_edges(rows)
     grads[:, 224:256, :] = jnp.zeros((4, 32, 256), BF16)
     squares_ref[...] = squares_in[...]
     linear_ref[...] = linear_in[...]
-    for group in (far, far_other):
-        take_patches(group, rows, patches, (0, 1))
-        rotate_grads(group, out_basis, grads)
-        for block in range(2):
-            add_moments(
-                rotate(basis[block], patches[block]), grads, squares_ref, linear_ref, block
-            )
+    take_patches(far, rows, patches, (0, 1))
+    rotate_grads(far, out_basis, grads)
+    for block in range(2):
+        add_moments(rotate(basis[block], patches[block]), grads, squares_ref, linear_ref, block)
+
+
+def last_kernel(
+    far, squares_in, linear_in, basis, out_basis, sums, squares_ref, linear_ref, *scratch
+):
+    far_kernel(
+        far, squares_in, linear_in, basis, out_basis, squares_ref, linear_ref, *scratch
+    )
     for owner in range(4):
         at = slice(144 * (owner % 2), 144 * (owner % 2) + 144)
         for half in range(2):
@@ -229,10 +233,6 @@
         [rows, patches],
         own, other, shard, plus, minus,
     )
-    far, two_top, two_bottom, u_two, rotated = lax.optimization_barrier(
-        (far, two_top, two_bottom, u_two, rotated)
-    )
-    far_other = swap_cores(far)
     squares, linear, basis, out_basis = call(
         near_kernel,
         "near_examples",
@@ -246,13 +246,23 @@
         [rows, patches, grads],
         own, other, rotated, first, plus, minus, two_top, two_bottom, u2, u_two,
     )
-    sums = call(
+    far, squares = lax.optimization_barrier((far, squares))
+    far_other = swap_cores(far)
+    squares, linear = call(
         far_kernel,
         "far_examples",
         4 * 10**9,
+        (moment, moment),
+        [rows, patches, grads],
+        far, squares, linear, basis, out_basis,
+    )
+    sums = call(
+        last_kernel,
+        "last_examples",
+        2 * 10**9,
         jax.ShapeDtypeStruct((8, 2, 144, 128), BF16),
         [pltpu.VMEM((2, 288, 256), F32)] * 2 + [rows, patches, grads],
-        far, far_other, squares, linear, basis, out_basis,
+        far_other, squares, linear, basis, out_basis,
     )
 
     sums = lax.all_to_all(sums, ("y", "xh"), 0, 0, tiled=True)

time: 65.3 us -> 65.2 us (level)
  waiting for transfers between devices: 5.52 us -> 7.29 us
  starting transfers between devices: 11.4 us -> 10.3 us
    ppermute x5, waiting for transfers between devices: 3.03 us -> 6.56 us  [ring(): lax.ppermute(value, axis, [(i, (i + step) % size) for i in range(size)])]
    ppermute x2, waiting for transfers between devices: 2.49 us -> 0.58 us  [swap_x(): return lax.ppermute(value, ('xh', 'xl', 'c'), pairs)]
    ppermute x2, starting transfers between devices: 3.65 us -> 2.65 us  [swap_x(): return lax.ppermute(value, ('xh', 'xl', 'c'), pairs)]
    pallas_call x4 -> x5, Pallas kernels: 10.3 us -> 10.5 us  [call(): pl.pallas_call(kernel, out_shape=out_shape, in_specs=[vmem] * len(operand...]
  transfers between devices with their start and end apart: 10 -> 10, of which waited for: 4 -> 4; matrix products, arithmetic and copies ran while one was open for 3% -> 3% of each run, Pallas kernels for 9% -> 13%
where the time goes in v8:
time: 65.2 us; the launch traced here: 65 us
  blocking collectives  33.3 us (51%)
  Pallas kernels  10.5 us (16%)
  starting transfers between devices  10.3 us (16%)
  waiting for transfers between devices  7.29 us (11%)
  other arithmetic  2.51 us (4%)
  between operations  0.75 us (1%)
    all_to_all x1, blocking collectives, on_device(): sums = lax.all_to_all(sums, ('zh', 'zl'), 0, 0, tiled=True)  17 us
    all_to_all x1, blocking collectives, on_device(): sums = lax.all_to_all(sums, ('y', 'xh'), 0, 0, tiled=True)  16.3 us
    pallas_call x5, Pallas kernels, call(): pl.pallas_call(kernel, out_shape=out_shape, in_specs=[vmem] * len(operand...  10.5 us
    ppermute x5, starting transfers between devices, ring(): lax.ppermute(value, axis, [(i, (i + step) % size) for i in range(size)])  7.2 us
    ppermute x5, waiting for transfers between devices, ring(): lax.ppermute(value, axis, [(i, (i + step) % size) for i in range(size)])  6.56 us
    ppermute x2, starting transfers between devices, swap_x(): return lax.ppermute(value, ('xh', 'xl', 'c'), pairs)  2.65 us
    another operation x1, other arithmetic, prepare(): both = jnp.stack([inputs, out_grads])  1.72 us
  transfers between devices with their start and end apart: 10, of which 4 were waited for; matrix products, arithmetic and copies ran while one was open for 3% of the time, Pallas kernels for 13%

profile of v8, /device:TPU:2, one launch (start us, length us, event | category | flops | bytes accessed | tf_op | source)
XLA Modules:
  0.0 65.0 jit_solution(12815979308749818618)
XLA Ops:
  0.6 3.1 %collective-permute-start.4 = (bf16[144,1152]{1,0:T(8,128)(2,1)}, bf16[144,1152]{1,0:T(8,128)(2,1)S(1)}, u32[]{:S(2)}, u32[]{:S(2)}) collective-permute-start(bf16[144,1152]{1,0:T(8,128)(2,1)} %bitcast.13), channel_id=1, source_target_pairs={{0,12},{4,0},{8,4},{12,8},{1,13},{5,1},{9,5},{13,9},{2,14},{6,2},{... | collective-permute-start | bytes 995336 | tf_op jit(solution)/shard_map/ppermute | solution.py:19
  3.7 0.0 collective-permute-start.5
  3.7 1.3 %collective-permute-start.1 = (bf16[16,256]{1,0:T(8,128)(2,1)}, bf16[16,256]{1,0:T(8,128)(2,1)S(1)}, u32[]{:S(2)}, u32[]{:S(2)}) collective-permute-start(bf16[16,256]{1,0:T(8,128)(2,1)} %bitcast.20), channel_id=1, source_target_pairs={{0,2},{1,19},{2,0},{3,17},{16,18},{17,3},{18,16},{19,1},{4,6},{5,2... | collective-permute-start | bytes 24584 | tf_op jit(solution)/shard_map/ppermute | solution.py:31
  5.0 1.7 %pad_maximum_fusion = bf16[2,4,14,14,256]{4,1,3,2,0:T(4,128)(2,1)S(1)} fusion(bf16[1,4,14,14,256]{4,1,3,2,0:T(4,128)(2,1)} %bitcast.16, bf16[1,4,14,14,256]{4,1,3,2,0:T(4,128)(2,1)} %bitcast.17), kind=kLoop, calls=%fused_computation | loop fusion | flops 401408 | bytes 1605632 | tf_op jit(solution)/shard_map/stack | solution.py:35
  6.7 0.1 copy.10
  6.9 0.0 copy-start.1
  6.9 0.1 pad.4.clone
  7.0 0.6 collective-permute-done.1
  7.6 0.0 copy-done.1
  7.6 0.0 collective-permute-start.2
  7.6 1.4 %collective-permute-start = (bf16[2,4,224,256]{3,2,1,0:T(8,128)(2,1)S(1)}, bf16[2,4,224,256]{3,2,1,0:T(8,128)(2,1)S(1)}, u32[]{:S(2)}, u32[]{:S(2)}) collective-permute-start(bf16[2,4,224,256]{3,2,1,0:T(8,128)(2,1)S(1)} %bitcast.9), channel_id=1, source_target_pairs={{0,2},{1,19},{2,0},{3,17},{16,18},{17,3},{18,16},{19,1},{4,6},{5,2... | collective-permute-start | bytes 2752520 | tf_op jit(solution)/shard_map/ppermute | solution.py:31
  9.0 0.0 collective-permute-done.2
  9.0 0.0 copy-start
  9.0 2.0 %collective-permute-start.8 = (bf16[16,1024]{1,0:T(8,128)(2,1)S(1)}, bf16[16,1024]{1,0:T(8,128)(2,1)S(1)}, u32[]{:S(2)}, u32[]{:S(2)}) collective-permute-start(bf16[16,1024]{1,0:T(8,128)(2,1)S(1)} %pad_maximum_fusion.1.eigenvectors.u_here), channel_id=1, source_target_pairs={{0,8},{4,12},{8,0},{12,4},{1,9},{5,13},{9,1},{13,5},{2,10},{6,14},... | collective-permute-start | bytes 98312 | tf_op jit(solution)/shard_map/ppermute | solution.py:19
  11.0 0.3 collective-permute-start.3
  11.3 0.0 collective-permute-done.4.plus
  11.3 3.8 %collective-permute-done.5.minus = bf16[144,1152]{1,0:T(8,128)(2,1)S(1)} collective-permute-done((bf16[144,1152]{1,0:T(8,128)(2,1)}, bf16[144,1152]{1,0:T(8,128)(2,1)S(1)}, u32[]{:S(2)}, u32[]{:S(2)}) %collective-permute-start.5) | collective-permute-done | bytes 331808 | tf_op jit(solution)/shard_map/ppermute | solution.py:19
  15.1 0.1 collective-permute-start.6
  15.2 2.0 %collective-permute-start.7 = (bf16[80,1152]{1,0:T(8,128)(2,1)S(1)}, bf16[80,1152]{1,0:T(8,128)(2,1)S(1)}, u32[]{:S(2)}, u32[]{:S(2)}) collective-permute-start(bf16[80,1152]{1,0:T(8,128)(2,1)S(1)} %get-tuple-element.21), channel_id=1, source_target_pairs={{0,4},{4,8},{8,12},{12,0},{1,5},{5,9},{9,13},{13,1},{2,6},{6,10},{... | collective-permute-start | bytes 552968 | tf_op jit(solution)/shard_map/ppermute | solution.py:19
  17.2 0.0 collective-permute-done.3.other
  17.2 0.0 copy-done
  17.2 2.0 %first_block_near.1 = (bf16[2,288,1024]{2,1,0:T(8,128)(2,1)S(1)}, bf16[288,1152]{1,0:T(8,128)(2,1)S(1)}) custom-call(bf16[2,4,224,256]{3,2,1,0:T(8,128)(2,1)S(1)} %bitcast.11, bf16[2,4,224,256]{3,2,1,0:T(8,128)(2,1)S(1)} %collective-permute-done.3.other, bf16[144,1152]{1,0:T(8,128)(2,1)S(1)} %bitcast.15, bf16[144,1152]{1,0:T(8,128)(2,1)S(1)} %collective-permute-done.4.plus, ...), custom_call_target="tpu_custom_call" | custom-call | flops 4000000000 | bytes 1000000 | tf_op jit(solution)/shard_map/first_block_near/pallas_call | solution.py:176
  19.3 0.0 collective-permute-done.8.u_two
  19.3 2.8 %collective-permute-done.7.two_bottom = bf16[80,1152]{1,0:T(8,128)(2,1)S(1)} collective-permute-done((bf16[80,1152]{1,0:T(8,128)(2,1)S(1)}, bf16[80,1152]{1,0:T(8,128)(2,1)S(1)}, u32[]{:S(2)}, u32[]{:S(2)}) %collective-permute-start.7) | collective-permute-done | bytes 184352 | tf_op jit(solution)/shard_map/ppermute | solution.py:19
  22.1 0.0 collective-permute-done.6.two_top
  22.1 3.8 %near_examples.1 = (f32[2,288,256]{2,1,0:T(8,128)S(1)}, f32[2,288,256]{2,1,0:T(8,128)S(1)}, bf16[2,288,1152]{2,1,0:T(8,128)(2,1)S(1)}, bf16[256,256]{1,0:T(8,128)(2,1)S(1)}) custom-call(bf16[2,4,224,256]{3,2,1,0:T(8,128)(2,1)S(1)} %bitcast.12, bf16[2,4,224,256]{3,2,1,0:T(8,128)(2,1)S(1)} %collective-permute-done.3.other, ...), custom_call_target="tpu_custom_call" | custom-call | flops 4000000000 | bytes 1000000 | tf_op jit(solution)/shard_map/near_examples/pallas_call | solution.py:176
  25.9 0.0 collective-permute-done.far
  25.9 0.1 collective-permute-start.9
  26.0 2.3 %far_examples.1 = (f32[2,288,256]{2,1,0:T(8,128)S(1)}, f32[2,288,256]{2,1,0:T(8,128)S(1)}) custom-call(bf16[2,4,224,256]{3,2,1,0:T(8,128)(2,1)S(1)} %collective-permute-done.far, f32[2,288,256]{2,1,0:T(8,128)S(1)} %get-tuple-element.24.squares_in, f32[2,288,256]{2,1,0:T(8,128)S(1)} %get-tuple-element.25.linear_in, ...), custom_call_target="tpu_custom_call" | custom-call | flops 4000000000 | bytes 1000000 | tf_op jit(solution)/shard_map/far_examples/pallas_call | solution.py:176
  28.3 0.1 collective-permute-done.9.far
  28.5 2.3 %last_examples.1 = bf16[8,2,144,128]{3,2,1,0:T(8,128)(2,1)S(1)} custom-call(bf16[2,4,224,256]{3,2,1,0:T(8,128)(2,1)S(1)} %collective-permute-done.9.far, f32[2,288,256]{2,1,0:T(8,128)S(1)} %get-tuple-element.28.squares_in, f32[2,288,256]{2,1,0:T(8,128)S(1)} %get-tuple-element.29.linear_in, bf16[2,288,1152]{2,1,0:T(8,128)(2,1)S(1)} %get-tuple-element.26.basis, ...), custom_call_target="tpu_custom_call" | custom-call | flops 2000000000 | bytes 1000000 | tf_op jit(solution)/shard_map/last_examples/pallas_call | solution.py:176
  30.8 16.3 %all_to_all.14 = bf16[8,2,144,128]{3,2,1,0:T(8,128)(2,1)S(1)} all-to-all(bf16[8,2,144,128]{3,2,1,0:T(8,128)(2,1)S(1)} %last_examples.1), channel_id=1, replica_groups=mesh['zh'=4,'zl'=2,'xh'=2,'y'=4,'xl'=2,'c'=2] {'y','xh'}, dimensions={0} | all-to-all | bytes 1179648 | tf_op jit(solution)/shard_map/all_to_all | solution.py:268
  47.0 0.1 reduce_sum.21
  47.1 0.1 copy.9
  47.3 17.0 %all_to_all.15 = bf16[8,16,288]{2,1,0:T(8,128)(2,1)S(1)} all-to-all(bf16[8,16,288]{2,1,0:T(8,128)(2,1)S(1)} %bitcast.18), channel_id=1, replica_groups=mesh['zh'=4,'zl'=2,'xh'=2,'y'=4,'xl'=2,'c'=2] {'zh','zl'}, dimensions={0} | all-to-all | bytes 147456 | tf_op jit(solution)/shard_map/all_to_all | solution.py:270
  64.3 0.7 %slice_multiply_fusion = (f32[16,144]{1,0:T(8,128)}, f32[16,144]{1,0:T(8,128)}) fusion(f32[16,288]{1,0:T(8,128)S(1)} %convert_reduce_fusion), kind=kLoop, calls=%fused_computation.3 | loop fusion | flops 4608 | bytes 36864 | tf_op jit(solution)/shard_map/mul | solution.py:274
  (4 shorter events, 0.1 us)
Async XLA Ops:
  0.6 10.7 %collective-permute-start.4 = (bf16[144,1152]{1,0:T(8,128)(2,1)}, bf16[144,1152]{1,0:T(8,128)(2,1)S(1)}, u32[]{:S(2)}, u32[]{:S(2)}) collective-permute-start(bf16[144,1152]{1,0:T(8,128)(2,1)} %bitcast.13), channel_id=1, source_target_pairs={{0,12},{4,0},{8,4},{12,8},{1,13},{5,1},{9,5},{13,9},{2,14},{6,2},{... | collective-permute-start | bytes 995336 | tf_op jit(solution)/shard_map/ppermute | solution.py:19
  3.7 11.4 %collective-permute-start.5 = (bf16[144,1152]{1,0:T(8,128)(2,1)}, bf16[144,1152]{1,0:T(8,128)(2,1)S(1)}, u32[]{:S(2)}, u32[]{:S(2)}) collective-permute-start(bf16[144,1152]{1,0:T(8,128)(2,1)} %bitcast.14), channel_id=1, source_target_pairs={{0,4},{4,8},{8,12},{12,0},{1,5},{5,9},{9,13},{13,1},{2,6},{6,10},{... | collective-permute-start | bytes 995336 | tf_op jit(solution)/shard_map/ppermute | solution.py:19
  3.7 3.9 %collective-permute-start.1 = (bf16[16,256]{1,0:T(8,128)(2,1)}, bf16[16,256]{1,0:T(8,128)(2,1)S(1)}, u32[]{:S(2)}, u32[]{:S(2)}) collective-permute-start(bf16[16,256]{1,0:T(8,128)(2,1)} %bitcast.20), channel_id=1, source_target_pairs={{0,2},{1,19},{2,0},{3,17},{16,18},{17,3},{18,16},{19,1},{4,6},{5,2... | collective-permute-start | bytes 24584 | tf_op jit(solution)/shard_map/ppermute | solution.py:31
  6.9 0.7 %copy-start.1 = (bf16[256,16]{0,1:T(8,128)(2,1)S(1)}, bf16[256,16]{0,1:T(8,128)(2,1)}, u32[]{:S(2)}) copy-start(bf16[256,16]{0,1:T(8,128)(2,1)} %param.7) | copy-start | bytes 24580
  7.6 1.4 %collective-permute-start.2 = (bf16[16,512]{1,0:T(8,128)(2,1)S(1)}, bf16[16,512]{1,0:T(8,128)(2,1)S(1)}, u32[]{:S(2)}, u32[]{:S(2)}) collective-permute-start(bf16[16,512]{1,0:T(8,128)(2,1)S(1)} %pad_maximum_fusion.2), channel_id=1, source_target_pairs={{0,1},{1,0},{2,3},{3,2},{4,5},{5,4},{6,7},{7,6},{8,9},{9,8},{10,11... | collective-permute-start | bytes 49160 | tf_op jit(solution)/shard_map/ppermute | solution.py:23
  7.6 18.3 %collective-permute-start = (bf16[2,4,224,256]{3,2,1,0:T(8,128)(2,1)S(1)}, bf16[2,4,224,256]{3,2,1,0:T(8,128)(2,1)S(1)}, u32[]{:S(2)}, u32[]{:S(2)}) collective-permute-start(bf16[2,4,224,256]{3,2,1,0:T(8,128)(2,1)S(1)} %bitcast.9), channel_id=1, source_target_pairs={{0,2},{1,19},{2,0},{3,17},{16,18},{17,3},{18,16},{19,1},{4,6},{5,2... | collective-permute-start | bytes 2752520 | tf_op jit(solution)/shard_map/ppermute | solution.py:31
  9.0 8.3 %copy-start = (bf16[1152,144]{0,1:T(8,128)(2,1)S(1)}, bf16[1152,144]{0,1:T(8,128)(2,1)}, u32[]{:S(2)}) copy-start(bf16[1152,144]{0,1:T(8,128)(2,1)} %param.6) | copy-start | bytes 995332
  9.0 10.3 %collective-permute-start.8 = (bf16[16,1024]{1,0:T(8,128)(2,1)S(1)}, bf16[16,1024]{1,0:T(8,128)(2,1)S(1)}, u32[]{:S(2)}, u32[]{:S(2)}) collective-permute-start(bf16[16,1024]{1,0:T(8,128)(2,1)S(1)} %pad_maximum_fusion.1.eigenvectors.u_here), channel_id=1, source_target_pairs={{0,8},{4,12},{8,0},{12,4},{1,9},{5,13},{9,1},{13,5},{2,10},{6,14},... | collective-permute-start | bytes 98312 | tf_op jit(solution)/shard_map/ppermute | solution.py:19
  11.0 6.3 %collective-permute-start.3 = (bf16[2,4,224,256]{3,2,1,0:T(8,128)(2,1)S(1)}, bf16[2,4,224,256]{3,2,1,0:T(8,128)(2,1)S(1)}, u32[]{:S(2)}, u32[]{:S(2)}) collective-permute-start(bf16[2,4,224,256]{3,2,1,0:T(8,128)(2,1)S(1)} %bitcast.10), channel_id=1, source_target_pairs={{0,1},{1,0},{2,3},{3,2},{4,5},{5,4},{6,7},{7,6},{8,9},{9,8},{10,11... | collective-permute-start | bytes 2752520 | tf_op jit(solution)/shard_map/ppermute | solution.py:23
  15.1 6.9 %collective-permute-start.6 = (bf16[96,1152]{1,0:T(8,128)(2,1)S(1)}, bf16[96,1152]{1,0:T(8,128)(2,1)S(1)}, u32[]{:S(2)}, u32[]{:S(2)}) collective-permute-start(bf16[96,1152]{1,0:T(8,128)(2,1)S(1)} %get-tuple-element.20), channel_id=1, source_target_pairs={{0,12},{4,0},{8,4},{12,8},{1,13},{5,1},{9,5},{13,9},{2,14},{6,2},{... | collective-permute-start | bytes 663560 | tf_op jit(solution)/shard_map/ppermute | solution.py:19
  15.2 6.8 %collective-permute-start.7 = (bf16[80,1152]{1,0:T(8,128)(2,1)S(1)}, bf16[80,1152]{1,0:T(8,128)(2,1)S(1)}, u32[]{:S(2)}, u32[]{:S(2)}) collective-permute-start(bf16[80,1152]{1,0:T(8,128)(2,1)S(1)} %get-tuple-element.21), channel_id=1, source_target_pairs={{0,4},{4,8},{8,12},{12,0},{1,5},{5,9},{9,13},{13,1},{2,6},{6,10},{... | collective-permute-start | bytes 552968 | tf_op jit(solution)/shard_map/ppermute | solution.py:19
  25.9 2.6 %collective-permute-start.9 = (bf16[2,4,224,256]{3,2,1,0:T(8,128)(2,1)S(1)}, bf16[2,4,224,256]{3,2,1,0:T(8,128)(2,1)S(1)}, u32[]{:S(2)}, u32[]{:S(2)}) collective-permute-start(bf16[2,4,224,256]{3,2,1,0:T(8,128)(2,1)S(1)} %collective-permute-done.far), channel_id=1, source_target_pairs={{0,1},{1,0},{2,3},{3,2},{4,5},{5,4},{6,7},{7,6},{8,9},{9,8},{10,11... | collective-permute-start | bytes 2752520 | tf_op jit(solution)/shard_map/ppermute | solution.py:23

commit v9 on v8

--- a/solution.py
+++ b/solution.py
@@ -122,7 +122,7 @@
         for piece in range(4):
             dc, dx = piece // 2, piece % 2
             owner = (lax.rem(y + dy, 4) * 2 + lax.rem(xl + dx, 2)) * 2 + lax.rem(core + dc, 2)
-            place = owner % 2 * 128 + owner // 2 * 16
+            place = owner % 2 * 128 + owner // 2 % 2 * 64 + owner // 4 * 16
             out_basis[pl.ds(pl.multiple_of(place, 16), 16), :] = source[
                 row : row + 16, 256 * piece : 256 * piece + 256
             ]
@@ -267,7 +267,7 @@
 
     sums = lax.all_to_all(sums, ("y", "xh"), 0, 0, tiled=True)
     sums = jnp.sum(sums.astype(F32), axis=0).reshape(288, 128).T.astype(BF16)
-    sums = lax.all_to_all(sums, ("zh", "zl"), 0, 0, tiled=True)
+    sums = lax.all_to_all(sums, ("zl", "zh"), 0, 0, tiled=True)
     sums = jnp.sum(sums.reshape(8, 16, 288).astype(F32), axis=0)
     return (
         sums[:, :144] * (1.0 / (side * side * examples)),

time: 65.2 us -> 64.7 us (level)
  blocking collectives: 33.3 us -> 32.6 us
    all_to_all x1, blocking collectives: 17 us -> 16.3 us  [on_device(): sums = lax.all_to_all(sums, ('zl', 'zh'), 0, 0, tiled=True)]
where the time goes in v9:
time: 64.7 us; the launch traced here: 64.2 us
  blocking collectives  32.6 us (50%)
  Pallas kernels  10.4 us (16%)
  starting transfers between devices  10.3 us (16%)
  waiting for transfers between devices  7.29 us (11%)
  other arithmetic  2.51 us (4%)
  between operations  0.75 us (1%)
    all_to_all x1, blocking collectives, on_device(): sums = lax.all_to_all(sums, ('zl', 'zh'), 0, 0, tiled=True)  16.3 us
    all_to_all x1, blocking collectives, on_device(): sums = lax.all_to_all(sums, ('y', 'xh'), 0, 0, tiled=True)  16.3 us
    pallas_call x5, Pallas kernels, call(): pl.pallas_call(kernel, out_shape=out_shape, in_specs=[vmem] * len(operand...  10.4 us
    ppermute x5, starting transfers between devices, ring(): lax.ppermute(value, axis, [(i, (i + step) % size) for i in range(size)])  7.2 us
    ppermute x5, waiting for transfers between devices, ring(): lax.ppermute(value, axis, [(i, (i + step) % size) for i in range(size)])  6.56 us
    ppermute x2, starting transfers between devices, swap_x(): return lax.ppermute(value, ('xh', 'xl', 'c'), pairs)  2.65 us
    another operation x1, other arithmetic, prepare(): both = jnp.stack([inputs, out_grads])  1.72 us
  transfers between devices with their start and end apart: 10, of which 4 were waited for; matrix products, arithmetic and copies ran while one was open for 3% of the time, Pallas kernels for 13%

profile of v9, /device:TPU:2, one launch (start us, length us, event | category | flops | bytes accessed | tf_op | source)
XLA Modules:
  0.0 64.2 jit_solution(16056016206660292928)
XLA Ops:
  0.6 3.1 %collective-permute-start.4 = (bf16[144,1152]{1,0:T(8,128)(2,1)}, bf16[144,1152]{1,0:T(8,128)(2,1)S(1)}, u32[]{:S(2)}, u32[]{:S(2)}) collective-permute-start(bf16[144,1152]{1,0:T(8,128)(2,1)} %bitcast.13), channel_id=1, source_target_pairs={{0,12},{4,0},{8,4},{12,8},{1,13},{5,1},{9,5},{13,9},{2,14},{6,2},{... | collective-permute-start | bytes 995336 | tf_op jit(solution)/shard_map/ppermute | solution.py:19
  3.7 0.0 collective-permute-start.5
  3.7 1.3 %collective-permute-start.1 = (bf16[16,256]{1,0:T(8,128)(2,1)}, bf16[16,256]{1,0:T(8,128)(2,1)S(1)}, u32[]{:S(2)}, u32[]{:S(2)}) collective-permute-start(bf16[16,256]{1,0:T(8,128)(2,1)} %bitcast.20), channel_id=1, source_target_pairs={{0,2},{1,19},{2,0},{3,17},{16,18},{17,3},{18,16},{19,1},{4,6},{5,2... | collective-permute-start | bytes 24584 | tf_op jit(solution)/shard_map/ppermute | solution.py:31
  5.0 1.7 %pad_maximum_fusion = bf16[2,4,14,14,256]{4,1,3,2,0:T(4,128)(2,1)S(1)} fusion(bf16[1,4,14,14,256]{4,1,3,2,0:T(4,128)(2,1)} %bitcast.16, bf16[1,4,14,14,256]{4,1,3,2,0:T(4,128)(2,1)} %bitcast.17), kind=kLoop, calls=%fused_computation | loop fusion | flops 401408 | bytes 1605632 | tf_op jit(solution)/shard_map/stack | solution.py:35
  6.7 0.1 copy.10
  6.9 0.0 copy-start.1
  6.9 0.1 pad.4.clone
  7.0 0.6 collective-permute-done.1
  7.6 0.0 copy-done.1
  7.6 0.0 collective-permute-start.2
  7.6 1.4 %collective-permute-start = (bf16[2,4,224,256]{3,2,1,0:T(8,128)(2,1)S(1)}, bf16[2,4,224,256]{3,2,1,0:T(8,128)(2,1)S(1)}, u32[]{:S(2)}, u32[]{:S(2)}) collective-permute-start(bf16[2,4,224,256]{3,2,1,0:T(8,128)(2,1)S(1)} %bitcast.9), channel_id=1, source_target_pairs={{0,2},{1,19},{2,0},{3,17},{16,18},{17,3},{18,16},{19,1},{4,6},{5,2... | collective-permute-start | bytes 2752520 | tf_op jit(solution)/shard_map/ppermute | solution.py:31
  9.0 0.0 collective-permute-done.2
  9.0 0.0 copy-start
  9.0 2.0 %collective-permute-start.8 = (bf16[16,1024]{1,0:T(8,128)(2,1)S(1)}, bf16[16,1024]{1,0:T(8,128)(2,1)S(1)}, u32[]{:S(2)}, u32[]{:S(2)}) collective-permute-start(bf16[16,1024]{1,0:T(8,128)(2,1)S(1)} %pad_maximum_fusion.1.eigenvectors.u_here), channel_id=1, source_target_pairs={{0,8},{4,12},{8,0},{12,4},{1,9},{5,13},{9,1},{13,5},{2,10},{6,14},... | collective-permute-start | bytes 98312 | tf_op jit(solution)/shard_map/ppermute | solution.py:19
  11.0 0.3 collective-permute-start.3
  11.3 0.0 collective-permute-done.4.plus
  11.3 3.8 %collective-permute-done.5.minus = bf16[144,1152]{1,0:T(8,128)(2,1)S(1)} collective-permute-done((bf16[144,1152]{1,0:T(8,128)(2,1)}, bf16[144,1152]{1,0:T(8,128)(2,1)S(1)}, u32[]{:S(2)}, u32[]{:S(2)}) %collective-permute-start.5) | collective-permute-done | bytes 331808 | tf_op jit(solution)/shard_map/ppermute | solution.py:19
  15.1 0.1 collective-permute-start.6
  15.2 2.0 %collective-permute-start.7 = (bf16[80,1152]{1,0:T(8,128)(2,1)S(1)}, bf16[80,1152]{1,0:T(8,128)(2,1)S(1)}, u32[]{:S(2)}, u32[]{:S(2)}) collective-permute-start(bf16[80,1152]{1,0:T(8,128)(2,1)S(1)} %get-tuple-element.21), channel_id=1, source_target_pairs={{0,4},{4,8},{8,12},{12,0},{1,5},{5,9},{9,13},{13,1},{2,6},{6,10},{... | collective-permute-start | bytes 552968 | tf_op jit(solution)/shard_map/ppermute | solution.py:19
  17.2 0.0 collective-permute-done.3.other
  17.2 0.0 copy-done
  17.2 2.0 %first_block_near.1 = (bf16[2,288,1024]{2,1,0:T(8,128)(2,1)S(1)}, bf16[288,1152]{1,0:T(8,128)(2,1)S(1)}) custom-call(bf16[2,4,224,256]{3,2,1,0:T(8,128)(2,1)S(1)} %bitcast.11, bf16[2,4,224,256]{3,2,1,0:T(8,128)(2,1)S(1)} %collective-permute-done.3.other, bf16[144,1152]{1,0:T(8,128)(2,1)S(1)} %bitcast.15, bf16[144,1152]{1,0:T(8,128)(2,1)S(1)} %collective-permute-done.4.plus, ...), custom_call_target="tpu_custom_call" | custom-call | flops 4000000000 | bytes 1000000 | tf_op jit(solution)/shard_map/first_block_near/pallas_call | solution.py:176
  19.3 0.0 collective-permute-done.8.u_two
  19.3 2.8 %collective-permute-done.7.two_bottom = bf16[80,1152]{1,0:T(8,128)(2,1)S(1)} collective-permute-done((bf16[80,1152]{1,0:T(8,128)(2,1)S(1)}, bf16[80,1152]{1,0:T(8,128)(2,1)S(1)}, u32[]{:S(2)}, u32[]{:S(2)}) %collective-permute-start.7) | collective-permute-done | bytes 184352 | tf_op jit(solution)/shard_map/ppermute | solution.py:19
  22.1 0.0 collective-permute-done.6.two_top
  22.1 3.8 %near_examples.1 = (f32[2,288,256]{2,1,0:T(8,128)S(1)}, f32[2,288,256]{2,1,0:T(8,128)S(1)}, bf16[2,288,1152]{2,1,0:T(8,128)(2,1)S(1)}, bf16[256,256]{1,0:T(8,128)(2,1)S(1)}) custom-call(bf16[2,4,224,256]{3,2,1,0:T(8,128)(2,1)S(1)} %bitcast.12, bf16[2,4,224,256]{3,2,1,0:T(8,128)(2,1)S(1)} %collective-permute-done.3.other, ...), custom_call_target="tpu_custom_call" | custom-call | flops 4000000000 | bytes 1000000 | tf_op jit(solution)/shard_map/near_examples/pallas_call | solution.py:176
  25.9 0.0 collective-permute-done.far
  25.9 0.1 collective-permute-start.9
  26.0 2.3 %far_examples.1 = (f32[2,288,256]{2,1,0:T(8,128)S(1)}, f32[2,288,256]{2,1,0:T(8,128)S(1)}) custom-call(bf16[2,4,224,256]{3,2,1,0:T(8,128)(2,1)S(1)} %collective-permute-done.far, f32[2,288,256]{2,1,0:T(8,128)S(1)} %get-tuple-element.24.squares_in, f32[2,288,256]{2,1,0:T(8,128)S(1)} %get-tuple-element.25.linear_in, ...), custom_call_target="tpu_custom_call" | custom-call | flops 4000000000 | bytes 1000000 | tf_op jit(solution)/shard_map/far_examples/pallas_call | solution.py:176
  28.3 0.1 collective-permute-done.9.far
  28.4 2.3 %last_examples.1 = bf16[8,2,144,128]{3,2,1,0:T(8,128)(2,1)S(1)} custom-call(bf16[2,4,224,256]{3,2,1,0:T(8,128)(2,1)S(1)} %collective-permute-done.9.far, f32[2,288,256]{2,1,0:T(8,128)S(1)} %get-tuple-element.28.squares_in, f32[2,288,256]{2,1,0:T(8,128)S(1)} %get-tuple-element.29.linear_in, bf16[2,288,1152]{2,1,0:T(8,128)(2,1)S(1)} %get-tuple-element.26.basis, ...), custom_call_target="tpu_custom_call" | custom-call | flops 2000000000 | bytes 1000000 | tf_op jit(solution)/shard_map/last_examples/pallas_call | solution.py:176
  30.7 16.3 %all_to_all.14 = bf16[8,2,144,128]{3,2,1,0:T(8,128)(2,1)S(1)} all-to-all(bf16[8,2,144,128]{3,2,1,0:T(8,128)(2,1)S(1)} %last_examples.1), channel_id=1, replica_groups=mesh['zh'=4,'zl'=2,'xh'=2,'y'=4,'xl'=2,'c'=2] {'y','xh'}, dimensions={0} | all-to-all | bytes 1179648 | tf_op jit(solution)/shard_map/all_to_all | solution.py:268
  47.0 0.1 reduce_sum.21
  47.1 0.1 copy.9
  47.2 16.3 %all_to_all.15 = bf16[8,16,288]{2,1,0:T(8,128)(2,1)S(1)} all-to-all(bf16[8,16,288]{2,1,0:T(8,128)(2,1)S(1)} %bitcast.18), channel_id=1, replica_groups=mesh['zh'=4,'zl'=2,'xh'=2,'y'=4,'xl'=2,'c'=2] {'zl','zh'}, dimensions={0} | all-to-all | bytes 147456 | tf_op jit(solution)/shard_map/all_to_all | solution.py:270
  63.5 0.7 %slice_multiply_fusion = (f32[16,144]{1,0:T(8,128)}, f32[16,144]{1,0:T(8,128)}) fusion(f32[16,288]{1,0:T(8,128)S(1)} %convert_reduce_fusion), kind=kLoop, calls=%fused_computation.3 | loop fusion | flops 4608 | bytes 36864 | tf_op jit(solution)/shard_map/mul | solution.py:274
  (4 shorter events, 0.1 us)
Async XLA Ops:
  0.6 10.7 %collective-permute-start.4 = (bf16[144,1152]{1,0:T(8,128)(2,1)}, bf16[144,1152]{1,0:T(8,128)(2,1)S(1)}, u32[]{:S(2)}, u32[]{:S(2)}) collective-permute-start(bf16[144,1152]{1,0:T(8,128)(2,1)} %bitcast.13), channel_id=1, source_target_pairs={{0,12},{4,0},{8,4},{12,8},{1,13},{5,1},{9,5},{13,9},{2,14},{6,2},{... | collective-permute-start | bytes 995336 | tf_op jit(solution)/shard_map/ppermute | solution.py:19
  3.7 11.4 %collective-permute-start.5 = (bf16[144,1152]{1,0:T(8,128)(2,1)}, bf16[144,1152]{1,0:T(8,128)(2,1)S(1)}, u32[]{:S(2)}, u32[]{:S(2)}) collective-permute-start(bf16[144,1152]{1,0:T(8,128)(2,1)} %bitcast.14), channel_id=1, source_target_pairs={{0,4},{4,8},{8,12},{12,0},{1,5},{5,9},{9,13},{13,1},{2,6},{6,10},{... | collective-permute-start | bytes 995336 | tf_op jit(solution)/shard_map/ppermute | solution.py:19
  3.7 3.9 %collective-permute-start.1 = (bf16[16,256]{1,0:T(8,128)(2,1)}, bf16[16,256]{1,0:T(8,128)(2,1)S(1)}, u32[]{:S(2)}, u32[]{:S(2)}) collective-permute-start(bf16[16,256]{1,0:T(8,128)(2,1)} %bitcast.20), channel_id=1, source_target_pairs={{0,2},{1,19},{2,0},{3,17},{16,18},{17,3},{18,16},{19,1},{4,6},{5,2... | collective-permute-start | bytes 24584 | tf_op jit(solution)/shard_map/ppermute | solution.py:31
  6.9 0.7 %copy-start.1 = (bf16[256,16]{0,1:T(8,128)(2,1)S(1)}, bf16[256,16]{0,1:T(8,128)(2,1)}, u32[]{:S(2)}) copy-start(bf16[256,16]{0,1:T(8,128)(2,1)} %param.7) | copy-start | bytes 24580
  7.6 1.4 %collective-permute-start.2 = (bf16[16,512]{1,0:T(8,128)(2,1)S(1)}, bf16[16,512]{1,0:T(8,128)(2,1)S(1)}, u32[]{:S(2)}, u32[]{:S(2)}) collective-permute-start(bf16[16,512]{1,0:T(8,128)(2,1)S(1)} %pad_maximum_fusion.2), channel_id=1, source_target_pairs={{0,1},{1,0},{2,3},{3,2},{4,5},{5,4},{6,7},{7,6},{8,9},{9,8},{10,11... | collective-permute-start | bytes 49160 | tf_op jit(solution)/shard_map/ppermute | solution.py:23
  7.6 18.3 %collective-permute-start = (bf16[2,4,224,256]{3,2,1,0:T(8,128)(2,1)S(1)}, bf16[2,4,224,256]{3,2,1,0:T(8,128)(2,1)S(1)}, u32[]{:S(2)}, u32[]{:S(2)}) collective-permute-start(bf16[2,4,224,256]{3,2,1,0:T(8,128)(2,1)S(1)} %bitcast.9), channel_id=1, source_target_pairs={{0,2},{1,19},{2,0},{3,17},{16,18},{17,3},{18,16},{19,1},{4,6},{5,2... | collective-permute-start | bytes 2752520 | tf_op jit(solution)/shard_map/ppermute | solution.py:31
  9.0 8.3 %copy-start = (bf16[1152,144]{0,1:T(8,128)(2,1)S(1)}, bf16[1152,144]{0,1:T(8,128)(2,1)}, u32[]{:S(2)}) copy-start(bf16[1152,144]{0,1:T(8,128)(2,1)} %param.6) | copy-start | bytes 995332
  9.0 10.3 %collective-permute-start.8 = (bf16[16,1024]{1,0:T(8,128)(2,1)S(1)}, bf16[16,1024]{1,0:T(8,128)(2,1)S(1)}, u32[]{:S(2)}, u32[]{:S(2)}) collective-permute-start(bf16[16,1024]{1,0:T(8,128)(2,1)S(1)} %pad_maximum_fusion.1.eigenvectors.u_here), channel_id=1, source_target_pairs={{0,8},{4,12},{8,0},{12,4},{1,9},{5,13},{9,1},{13,5},{2,10},{6,14},... | collective-permute-start | bytes 98312 | tf_op jit(solution)/shard_map/ppermute | solution.py:19
  11.0 6.3 %collective-permute-start.3 = (bf16[2,4,224,256]{3,2,1,0:T(8,128)(2,1)S(1)}, bf16[2,4,224,256]{3,2,1,0:T(8,128)(2,1)S(1)}, u32[]{:S(2)}, u32[]{:S(2)}) collective-permute-start(bf16[2,4,224,256]{3,2,1,0:T(8,128)(2,1)S(1)} %bitcast.10), channel_id=1, source_target_pairs={{0,1},{1,0},{2,3},{3,2},{4,5},{5,4},{6,7},{7,6},{8,9},{9,8},{10,11... | collective-permute-start | bytes 2752520 | tf_op jit(solution)/shard_map/ppermute | solution.py:23
  15.1 6.9 %collective-permute-start.6 = (bf16[96,1152]{1,0:T(8,128)(2,1)S(1)}, bf16[96,1152]{1,0:T(8,128)(2,1)S(1)}, u32[]{:S(2)}, u32[]{:S(2)}) collective-permute-start(bf16[96,1152]{1,0:T(8,128)(2,1)S(1)} %get-tuple-element.20), channel_id=1, source_target_pairs={{0,12},{4,0},{8,4},{12,8},{1,13},{5,1},{9,5},{13,9},{2,14},{6,2},{... | collective-permute-start | bytes 663560 | tf_op jit(solution)/shard_map/ppermute | solution.py:19
  15.2 6.8 %collective-permute-start.7 = (bf16[80,1152]{1,0:T(8,128)(2,1)S(1)}, bf16[80,1152]{1,0:T(8,128)(2,1)S(1)}, u32[]{:S(2)}, u32[]{:S(2)}) collective-permute-start(bf16[80,1152]{1,0:T(8,128)(2,1)S(1)} %get-tuple-element.21), channel_id=1, source_target_pairs={{0,4},{4,8},{8,12},{12,0},{1,5},{5,9},{9,13},{13,1},{2,6},{6,10},{... | collective-permute-start | bytes 552968 | tf_op jit(solution)/shard_map/ppermute | solution.py:19
  25.9 2.6 %collective-permute-start.9 = (bf16[2,4,224,256]{3,2,1,0:T(8,128)(2,1)S(1)}, bf16[2,4,224,256]{3,2,1,0:T(8,128)(2,1)S(1)}, u32[]{:S(2)}, u32[]{:S(2)}) collective-permute-start(bf16[2,4,224,256]{3,2,1,0:T(8,128)(2,1)S(1)} %collective-permute-done.far), channel_id=1, source_target_pairs={{0,1},{1,0},{2,3},{3,2},{4,5},{5,4},{6,7},{7,6},{8,9},{9,8},{10,11... | collective-permute-start | bytes 2752520 | tf_op jit(solution)/shard_map/ppermute | solution.py:23
